TPU v7x, 32 devices: a whole 2x2x4 slice. The times are simulated.
32 devices in a mesh: drift: 4 (over x, core), beam: 8 (over z, y).
Axes of the slice: x: 2, y: 2, z: 4, core: 2. Of those that a mesh axis runs over, the one named last changes fastest.
Arguments:
- features: bfloat16 [32, 32, 128, 128], P('drift', None, 'beam'), may hold values from -6 to 6
- occupied: int32 [4, 16, 16], P('drift', 'beam'), may hold values 0 or 1
- voxel_fragment: int32 [32, 128, 128], P('drift', 'beam'), may hold values from 0 to 2047, as said below
- conv_weight: bfloat16 [32, 864], replicated, may hold values from -0.21875 to 0.21875
- embed_weight: bfloat16 [32, 256], replicated, may hold values from -6 to 6
- message_weight: bfloat16 [256, 256], replicated, may hold values from -0.375 to 0.375
- update_weight: bfloat16 [256, 256], replicated, may hold values from -0.375 to 0.375
- edge_source: int32 [32768], P(('drift', 'beam')), may hold values from 0 to 2047
- edge_target: int32 [32768], P(('drift', 'beam')), may hold values from 0 to 255
- out_cotangent: bfloat16 [8192, 256], P(('drift', 'beam')), may hold values from -6 to 6
Outputs:
- fragment_out: bfloat16 [8192, 256], P(('drift', 'beam'))
- grad_features: float32 [32, 32, 128, 128], P('drift', None, 'beam')
- grad_conv: float32 [32, 864], replicated
Inputs may be any that keep to these rules, and one draw needn't show every extreme that they name: `voxel_fragment`: index among the 2048 fragments of the voxel's drift row.
All inputs are finite; a program needn't handle non-finite values. No bound on the sum of `occupied` on one device may be relied on, other than what follows from the above.
Results may differ from a plain program's by a relative error of at most 0.01.
Values may be sent and summed in bfloat16 or wider, within the bound.
No kernel may reach another device: no remote copies, remote signals or barrier semaphores. Data moves between devices by JAX's collectives and lax.ppermute only.
A program may use at most 64 MiB of HBM per device.

v0:
```python
import jax
import jax.numpy as jnp
from jax import lax
from jax.sharding import PartitionSpec as P

BLOCK = 8


def padded_2(cells, sides, width):
    for axis, dim in sides:
        count = lax.axis_size(axis)
        ends = count - 1
        head = lax.slice_in_dim(cells, 0, width, axis=dim)
        tail = lax.slice_in_dim(cells, cells.shape[dim] - width, cells.shape[dim], axis=dim)
        cells = jnp.concatenate(
            [
                lax.ppermute(tail, axis, [(i, (i + 1) % count) for i in range(ends)]),
                cells,
                lax.ppermute(head, axis, [((i + 1) % count, i) for i in range(ends)]),
            ],
            axis=dim,
        )
    return cells


def slope(value):
    sig = jax.nn.sigmoid(value)
    return sig * (1.0 + value * (1.0 - sig))


def columns(padded, row):
    channels = padded.shape[1]
    height = padded.shape[2] - 2
    depth = padded.shape[3] - 2
    anchor = jnp.zeros((), jnp.int32)
    pieces = []
    for off_a in range(3):
        for off_b in range(3):
            for off_c in range(3):
                index = (row + off_a, anchor, anchor + off_b, anchor + off_c)
                piece = lax.dynamic_slice(padded, index, (1, channels, height, depth))
                pieces.append(piece.reshape(channels, height * depth))
    return jnp.concatenate(pieces, 0)


def convolve(padded, weight):
    rows = padded.shape[0] - 2
    height = padded.shape[2] - 2
    depth = padded.shape[3] - 2

    def one_row(row):
        return jnp.dot(weight, columns(padded, row), preferred_element_type=jnp.float32)

    result = lax.map(one_row, jnp.arange(rows, dtype=jnp.int32))
    return result.reshape(rows, weight.shape[0], height, depth)


def project_back(embed_full, grad, pre):
    return lax.dot_general(
        embed_full, grad * slope(pre), (((1,), (1,)), ((), ())), precision=lax.Precision.HIGHEST
    )


def embed_rows(pooled, embed_weight):
    return lax.dot_general(
        pooled, embed_weight, (((0,), (0,)), ((), ())), preferred_element_type=jnp.float32
    )


def body(
    features,
    occupied,
    voxel_fragment,
    conv_weight,
    embed_weight,
    message_weight,
    update_weight,
    edge_source,
    edge_target,
    out_cotangent,
):
    f32 = jnp.float32
    rows, channels, height, depth = features.shape
    frag_dev = out_cotangent.shape[0]
    frag_row = frag_dev * lax.axis_size("beam")
    mask = jnp.repeat(jnp.repeat(jnp.repeat(occupied, BLOCK, 0), BLOCK, 1), BLOCK, 2).astype(f32)
    mask_four = mask[:, None]
    active = features * mask_four.astype(jnp.bfloat16)
    rimmed = padded_2(active, (("drift", 0), ("beam", 2)), 1)
    rimmed = jnp.pad(rimmed, ((0, 0), (0, 0), (0, 0), (1, 1)))
    conv_out = convolve(rimmed, conv_weight)
    hidden = mask_four * (active.astype(f32) + jax.nn.silu(conv_out))
    frag_ids = voxel_fragment.reshape(-1)
    by_voxel = hidden.transpose(0, 2, 3, 1).reshape(-1, channels)
    sums = jax.ops.segment_sum(by_voxel, frag_ids, num_segments=frag_row).T
    counts = jax.ops.segment_sum(mask.reshape(-1), frag_ids, num_segments=frag_row)
    sums, counts = (
        lax.psum_scatter(sums, "beam", scatter_dimension=1, tiled=True),
        lax.psum_scatter(counts, "beam", scatter_dimension=0, tiled=True),
    )
    divisor = jnp.maximum(counts, 1.0)[None, :]
    pooled = (sums / divisor).astype(jnp.bfloat16)
    pre_own = embed_rows(pooled, embed_weight)
    own = jax.nn.silu(pre_own).astype(jnp.bfloat16)
    table = lax.all_gather(own, "beam", axis=0, tiled=True)
    sources = jnp.take(table, edge_source, axis=0)
    pre_msg = jnp.dot(sources, message_weight, preferred_element_type=f32)
    messages = jax.nn.silu(pre_msg).astype(jnp.bfloat16)
    gathered = jax.ops.segment_sum(messages.astype(f32), edge_target, num_segments=frag_dev).astype(
        jnp.bfloat16
    )
    fragment_out = (
        own.astype(f32) + jnp.dot(gathered, update_weight, preferred_element_type=f32)
    ).astype(jnp.bfloat16)
    back_agg = jnp.dot(out_cotangent, update_weight.T, preferred_element_type=f32).astype(
        jnp.bfloat16
    )
    back_pre = (jnp.take(back_agg, edge_target, axis=0).astype(f32) * slope(pre_msg)).astype(
        jnp.bfloat16
    )
    back_src = jnp.dot(back_pre, message_weight.T, preferred_element_type=f32)
    back_rows = jax.ops.segment_sum(back_src, edge_source, num_segments=frag_row)
    embed_full = embed_weight.astype(f32)
    remote = lax.psum_scatter(
        back_rows.astype(jnp.bfloat16), "beam", scatter_dimension=0, tiled=True
    ).astype(jnp.float32)
    back_pooled = project_back(embed_full, out_cotangent.astype(f32) + remote, pre_own)
    back_mean = back_pooled / divisor
    mean_all = lax.all_gather(back_mean, "beam", axis=1, tiled=True)
    back_hidden = (
        jnp.take(mean_all, frag_ids, axis=1)
        .reshape(channels, rows, height, depth)
        .transpose(1, 0, 2, 3)
    )
    back_conv = (mask_four * back_hidden * slope(conv_out)).astype(jnp.bfloat16)
    rim_grad = padded_2(back_conv, (("drift", 0), ("beam", 2)), 1)
    rim_grad = jnp.pad(rim_grad, ((0, 0), (0, 0), (0, 0), (1, 1)))
    flipped = (
        conv_weight.reshape(channels, 27, channels)[:, ::-1, :]
        .transpose(2, 1, 0)
        .reshape(channels, 27 * channels)
    )
    back_active = mask_four * back_hidden + convolve(rim_grad, flipped)
    grad_features = mask_four * back_active

    def accumulate(total, row):
        cols = columns(rimmed, row)
        slab = lax.dynamic_index_in_dim(back_conv, row, 0, keepdims=False).reshape(channels, -1)
        term = lax.dot_general(slab, cols, (((1,), (1,)), ((), ())), preferred_element_type=f32)
        return (total + term, None)

    local_grad, _ = lax.scan(
        accumulate, jnp.zeros((channels, 27 * channels), f32), jnp.arange(rows, dtype=jnp.int32)
    )
    grad_conv = lax.psum(local_grad, ("drift", "beam"))
    return (fragment_out, grad_features, grad_conv)


def solution(mesh):
    return jax.shard_map(
        body,
        mesh=mesh,
        in_specs=(
            P("drift", None, "beam", None),
            P("drift", "beam", None),
            P("drift", "beam", None),
            P(),
            P(),
            P(),
            P(),
            P(("drift", "beam")),
            P(("drift", "beam")),
            P(("drift", "beam"), None),
        ),
        out_specs=(P(("drift", "beam"), None), P("drift", None, "beam", None), P()),
        check_vma=False,
    )
```

profile of v0, /device:TPU:1, one launch (start us, length us, event | category | flops | bytes accessed | tf_op | source)
XLA Modules:
  0.0 840.3 jit_solution(670104779173036249)
XLA Ops:
  9.4 4.5 collective-permute-start
  14.0 1.9 collective-permute-start.1
  15.9 4.3 collective-permute-done.1
  21.9 4.0 collective-permute-start.2
  27.6 6.2 select_maximum_fusion.4
  33.8 1.6 broadcast.75.clone
  35.4 109.4 %while.37 = (s32[]{:T(128)}, f32[8,32,2048]{2,1,0:T(8,128)}, s32[8]{0:T(128)S(1)}, bf16[10,32,18,130]{3,2,1,0:T(8,128)(2,1)}, bf16[32,864]{1,0:T(8,128)(2,1)S(1)...) while((s32[]{:T(128)}, f32[8,32,2048]{2,1,0:T(8,128)}, ...), condition=%wide.region_1.2_spmd, body=%wide.region_0.1_spmd.sunk | while | flops 113246224 | bytes 18012432 | solution.py:54
  40.5 6.4 constant_dynamic-slice_fusion.85
  47.8 1.4 fusion.80
  54.4 6.1 constant_dynamic-slice_fusion.85
  61.4 1.4 fusion.80
  67.9 6.1 constant_dynamic-slice_fusion.85
  81.5 6.2 constant_dynamic-slice_fusion.85
  88.7 1.4 fusion.80
  95.3 5.9 constant_dynamic-slice_fusion.85
  108.7 5.9 constant_dynamic-slice_fusion.85
  122.1 6.5 constant_dynamic-slice_fusion.85
  136.1 6.4 constant_dynamic-slice_fusion.85
  144.8 2.1 copy.149
  146.9 2.0 fusion.16
  148.9 6.4 copy.65
  155.3 88.6 %scatter_custom_fusion = f32[2048,32]{1,0:T(8,128)} fusion(s32[16384]{0:T(1024)S(1)} %bitcast.862, f32[16384,32]{1,0:T(8,128)} %bitcast.856, f32[]{:T(128)} %constant.161.clone.1), kind=kCustom, calls=%fused_computation.222 | custom fusion | flops 524288 | bytes 262656 | tf_op jit(solution)/shard_map/scatter-add | solution.py:95
  246.2 87.3 %scatter_custom_fusion.1 = f32[2048]{0:T(1024)S(1)} fusion(s32[16384]{0:T(1024)S(1)} %bitcast.863, f32[16384]{0:T(1024)S(1)} %reshape.632, f32[]{:T(128)} %constant.161.clone.1), kind=kCustom, calls=%fused_computation.258 | custom fusion | flops 16384 | bytes 8196 | tf_op jit(solution)/shard_map/scatter-add | solution.py:96
  333.5 28.1 %all-reduce.2 = f32[2048]{0:T(1024)S(1)} all-reduce(f32[2048]{0:T(1024)S(1)} %scatter_custom_fusion.1), channel_id=3, replica_groups=mesh['drift'=4,'beam'=8] {'beam'}, use_global_device_ids=true, to_apply=%region_5.6.clone | all-reduce | flops 2048 | bytes 16384
  361.7 1.9 multiply_convert_fusion.4
  364.9 3.9 gather_fusion.1
  368.9 36.0 %all-gather.2.cloned.1.call-done = bf16[2048,256]{1,0:T(8,128)(2,1)} async-done(((bf16[256,256]{1,0:T(8,128)(2,1)}), bf16[2048,256]{1,0:T(8,128)(2,1)}) %all-gather.2.cloned.1.call-update) | async-done | bytes 1048592 | tf_op jit(solution)/shard_map/all_gather | solution.py:105
  404.9 4.8 gather_fusion
  410.1 1.6 fusion.32
  411.7 7.0 scatter_custom_fusion.3
  421.3 7.0 scatter_custom_fusion.2
  428.3 53.2 %reduce-scatter.5.cloned.1.call-done = bf16[256,256]{1,0:T(8,128)(2,1)} async-done(((bf16[2048,256]{1,0:T(8,128)(2,1)}), bf16[256,256]{1,0:T(8,128)(2,1)}) %reduce-scatter.5.cloned.1.call-update) | async-done | bytes 131088 | tf_op jit(solution)/shard_map/reduce_scatter | solution.py:124
  482.8 24.7 %all_gather.7 = f32[32,2048]{1,0:T(8,128)S(1)} all-gather(f32[32,256]{1,0:T(8,128)S(1)} %fusion.22), channel_id=1, replica_groups=mesh['drift'=4,'beam'=8] {'beam'}, dimensions={1}, use_global_device_ids=true | all-gather | bytes 294912 | tf_op jit(solution)/shard_map/all_gather | solution.py:129
  507.9 54.8 %gather_fusion.2 = f32[16384,32]{1,0:T(8,128)} fusion(f32[32,2048]{0,1:T(8,128)S(1)} %copy.58, s32[16384]{0:T(1024)S(1)} %broadcast_clamp_fusion), kind=kCustom, calls=%fused_computation.2 | custom fusion | bytes 4259840 | tf_op jit(solution)/shard_map/jit(_take)/gather | solution.py:131
  562.6 5.2 copy.59
  567.9 2.5 fusion.20
  570.4 11.4 %collective-permute-start.4 = (bf16[1,32,16,128]{3,2,1,0:T(8,128)(2,1)S(1)}, bf16[1,32,16,128]{3,2,1,0:T(8,128)(2,1)S(1)}, u32[]{:S(2)}, u32[]{:S(2)}) collective-permute-start(bf16[1,32,16,128]{3,2,1,0:T(8,128)(2,1)S(1)} %get-tuple-element.356), channel_id=1, source_target_pairs={{0,8},{8,16},{16,24},{1,9},{9,17},{17,25},{2,10},{10,18},{18,26},{... | collective-permute-start | bytes 393224 | tf_op jit(solution)/shard_map/ppermute | solution.py:17
  581.8 1.9 collective-permute-start.5
  584.6 3.5 collective-permute-done.5
  591.0 4.8 collective-permute-start.6
  595.8 110.8 %while.39 = (s32[]{:T(128)}, f32[32,864]{1,0:T(8,128)S(1)}, s32[8]{0:T(128)S(1)}, bf16[8,32,16,128]{3,2,1,0:T(8,128)(2,1)S(1)}, bf16[10,32,18,130]{3,2,1,0:T(8,1...) while((s32[]{:T(128)}, f32[32,864]{1,0:T(8,128)S(1)}, ...), condition=%wide.region_12.13_spmd.clone, body=%wide.region_11.12_spmd.clone.sunk | while | flops 113301520 | bytes 18309432 | solution.py:152
  601.4 6.4 constant_dynamic-slice_fusion.87
  615.4 6.1 constant_dynamic-slice_fusion.87
  629.2 6.1 constant_dynamic-slice_fusion.87
  642.9 6.2 constant_dynamic-slice_fusion.87
  656.8 5.9 constant_dynamic-slice_fusion.87
  670.4 5.9 constant_dynamic-slice_fusion.87
  684.0 6.5 constant_dynamic-slice_fusion.87
  698.2 6.4 constant_dynamic-slice_fusion.87
  709.5 7.0 select_maximum_fusion
  716.5 1.6 broadcast.75
  718.0 110.4 %while.38 = (s32[]{:T(128)}, f32[8,32,2048]{2,1,0:T(8,128)}, s32[8]{0:T(128)S(1)}, bf16[10,32,18,130]{3,2,1,0:T(8,128)(2,1)}, bf16[32,864]{1,0:T(8,128)(2,1)S(1)...) while((s32[]{:T(128)}, f32[8,32,2048]{2,1,0:T(8,128)}, ...), condition=%wide.region_10.11_spmd, body=%wide.region_9.10_spmd.sunk | while | flops 113246224 | bytes 18012432 | solution.py:54
  723.4 6.1 constant_dynamic-slice_fusion.86
  737.3 6.1 constant_dynamic-slice_fusion.86
  751.1 6.3 constant_dynamic-slice_fusion.86
  765.2 5.9 constant_dynamic-slice_fusion.86
  772.1 1.4 fusion.83
  778.9 6.0 constant_dynamic-slice_fusion.86
  792.6 5.9 constant_dynamic-slice_fusion.86
  806.3 5.9 constant_dynamic-slice_fusion.86
  820.0 6.1 constant_dynamic-slice_fusion.86
  828.4 2.0 copy.150
  830.5 1.6 fusion.10
  832.1 1.6 copy.503
  (793 shorter events, 78.4 us)
Async XLA Ops:
  7.2 402.6 %copy-start = (bf16[256,256]{1,0:T(8,128)(2,1)S(1)}, bf16[256,256]{1,0:T(8,128)(2,1)}, u32[]{:S(2)}) copy-start(bf16[256,256]{1,0:T(8,128)(2,1)} %param.21) | copy-start | bytes 393220
  7.2 354.5 %reduce-scatter.3.cloned.1.call-start = ((), (), s32[]{:S(2)}) async-start(), calls=%async_computation.2 | async-start | bytes 1179648 | tf_op jit(solution)/shard_map/reduce_scatter | solution.py:98
  9.4 6.4 collective-permute-start
  14.0 6.3 collective-permute-start.1
  20.6 5.4 collective-permute-start.3
  21.9 5.5 collective-permute-start.2
  27.6 7.8 copy-start.5
  144.8 2.1 copy-start.3
  146.9 216.7 %copy-start.2 = (f32[32,8,16,128]{3,2,1,0:T(8,128)}, f32[32,8,16,128]{3,2,1,0:T(8,128)S(1)}, u32[]{:S(2)}) copy-start(f32[32,8,16,128]{3,2,1,0:T(8,128)S(1)} %copy.149) | copy-start | bytes 6291460
  148.9 6.4 copy-start.11
  155.2 89.7 %copy-start.17 = (u32[32]{0:T(128)S(1)}, u32[32]{0:T(128)}, u32[]{:S(2)}) copy-start(u32[32]{0:T(128)} %constant.178) | copy-start | bytes 388
  155.3 206.4 %copy-start.15 = (bf16[32,256]{1,0:T(8,128)(2,1)S(1)}, bf16[32,256]{1,0:T(8,128)(2,1)}, u32[]{:S(2)}) copy-start(bf16[32,256]{1,0:T(8,128)(2,1)} %param.20) | copy-start | bytes 49156
  155.3 208.4 %copy-start.14 = (s32[1024]{0:T(1024)S(1)}, s32[1024]{0:T(1024)}, u32[]{:S(2)}) copy-start(s32[1024]{0:T(1024)} %param.24) | copy-start | bytes 12292
  243.9 161.0 %all-gather.2.cloned.1.call-start = ((), (), s32[]{:S(2)}) async-start(), calls=%async_computation.3 | async-start | bytes 1179648 | tf_op jit(solution)/shard_map/all_gather | solution.py:105
  245.0 123.9 %copy-start.13 = (s32[1024]{0:T(1024)S(1)}, s32[1024]{0:T(1024)}, u32[]{:S(2)}) copy-start(s32[1024]{0:T(1024)} %param.23) | copy-start | bytes 12292
  363.6 117.9 %reduce-scatter.5.cloned.1.call-start = ((), (), s32[]{:S(2)}) async-start(), calls=%async_computation.4 | async-start | bytes 1179648 | tf_op jit(solution)/shard_map/reduce_scatter | solution.py:124
  418.7 62.8 %copy-start.12 = (bf16[256,256]{1,0:T(8,128)(2,1)S(1)}, bf16[256,256]{1,0:T(8,128)(2,1)}, u32[]{:S(2)}) copy-start(bf16[256,256]{1,0:T(8,128)(2,1)} %param.25) | copy-start | bytes 393220
  419.8 61.7 %copy-start.16 = (bf16[32,256]{1,0:T(8,128)(2,1)S(1)}, bf16[32,256]{1,0:T(8,128)(2,1)}, u32[]{:S(2)}) copy-start(bf16[32,256]{1,0:T(8,128)(2,1)} %param.20) | copy-start | bytes 49156
  419.8 61.7 %copy-start.18 = (f32[256,256]{1,0:T(8,128)S(1)}, f32[256,256]{1,0:T(8,128)}, u32[]{:S(2)}) copy-start(f32[256,256]{1,0:T(8,128)} %get-tuple-element.361) | copy-start | bytes 786436
  419.8 412.2 %all-reduce.5.cloned.1.call-start = ((), (), s32[]{:S(2)}) async-start(), calls=%async_computation.5 | async-start | bytes 229376 | tf_op jit(solution)/shard_map/psum | solution.py:155
  567.9 15.9 %copy-start.6 = (f32[256,256]{1,0:T(8,128)S(1)}, f32[256,256]{1,0:T(8,128)}, u32[]{:S(2)}) copy-start(f32[256,256]{1,0:T(8,128)} %scatter_custom_fusion.2) | copy-start | bytes 786436
  567.9 15.9 %copy-start.7 = (bf16[256,256]{1,0:T(8,128)(2,1)S(1)}, bf16[256,256]{1,0:T(8,128)(2,1)}, u32[]{:S(2)}) copy-start(bf16[256,256]{1,0:T(8,128)(2,1)} %param.22) | copy-start | bytes 393220
  567.9 15.9 %copy-start.10 = (bf16[256,256]{1,0:T(8,128)(2,1)S(1)}, bf16[256,256]{1,0:T(8,128)(2,1)}, u32[]{:S(2)}) copy-start(bf16[256,256]{1,0:T(8,128)(2,1)} %get-tuple-element.360) | copy-start | bytes 393220
  570.4 14.2 %collective-permute-start.4 = (bf16[1,32,16,128]{3,2,1,0:T(8,128)(2,1)S(1)}, bf16[1,32,16,128]{3,2,1,0:T(8,128)(2,1)S(1)}, u32[]{:S(2)}, u32[]{:S(2)}) collective-permute-start(bf16[1,32,16,128]{3,2,1,0:T(8,128)(2,1)S(1)} %get-tuple-element.356), channel_id=1, source_target_pairs={{0,8},{8,16},{16,24},{1,9},{9,17},{17,25},{2,10},{10,18},{18,26},{... | collective-permute-start | bytes 393224 | tf_op jit(solution)/shard_map/ppermute | solution.py:17
  581.8 6.3 collective-permute-start.5
  584.6 5.1 copy-start.8
  588.1 2.9 copy-start.9
  589.7 117.6 %collective-permute-start.7 = (bf16[10,32,1,128]{3,1,2,0:T(8,128)(2,1)}, bf16[10,32,1,128]{3,1,2,0:T(8,128)(2,1)}, u32[]{:S(2)}, u32[]{:S(2)}) collective-permute-start(bf16[10,32,1,128]{3,1,2,0:T(8,128)(2,1)} %copy.61), channel_id=1, source_target_pairs={{1,0},{2,1},{3,2},{4,3},{5,4},{6,5},{7,6},{9,8},{10,9},{11,10},{12... | collective-permute-start | bytes 245768 | tf_op jit(solution)/shard_map/ppermute | solution.py:19
  591.0 117.4 %collective-permute-start.6 = (bf16[10,32,1,128]{3,1,2,0:T(8,128)(2,1)}, bf16[10,32,1,128]{3,1,2,0:T(8,128)(2,1)}, u32[]{:S(2)}, u32[]{:S(2)}) collective-permute-start(bf16[10,32,1,128]{3,1,2,0:T(8,128)(2,1)} %copy.60), channel_id=1, source_target_pairs={{0,1},{1,2},{2,3},{3,4},{4,5},{5,6},{6,7},{8,9},{9,10},{10,11},{11... | collective-permute-start | bytes 245768 | tf_op jit(solution)/shard_map/ppermute | solution.py:17
  706.7 0.6 copy-start.4
  828.4 5.2 copy-start.1
Sparse Core Ops, SparseCore 0:
  244.0 64.0 reduce-scatter.2
  363.7 41.1 all-gather.1
  420.0 61.5 reduce-scatter.4
  707.5 117.7 all-reduce.4
where the time goes:
time: 855 us; the launch traced here: 840 us
  local copies, waits for them, and re-layouts  271 us (32%)
  other arithmetic  213 us (25%)
  loops' own time  118 us (14%)
  waiting for transfers between devices  98.4 us (12%)
  blocking collectives  52.8 us (6%)
  matrix products  39.3 us (5%)
  starting transfers between devices  31.6 us (4%)
  between operations  15.1 us (2%)
    dynamic_slice x24, local copies, waits for them, and re-layouts, columns(): piece = lax.dynamic_slice(padded, index, (1, channels, height, depth))  148 us
    scatter-add x1, other arithmetic, body(): sums = jax.ops.segment_sum(by_voxel, frag_ids, num_segments=frag_row).T  88.6 us
    scatter-add x1, other arithmetic, body(): jax.ops.segment_sum(mask.reshape(-1), frag_ids, num_segments=frag_row)  87.3 us
    another operation x2, loops' own time, convolve(): result = lax.map(one_row, jnp.arange(rows, dtype=jnp.int32))  77.1 us
    gather x2, local copies, waits for them, and re-layouts, body(): jnp.take(mean_all, frag_ids, axis=1).reshape(channels, rows, height, depth)  60 us
    reduce_scatter x1, waiting for transfers between devices, body(): lax.psum_scatter(back_rows.astype(jnp.bfloat16), 'beam', scatter_dimensio...  53.2 us
    another operation x1, loops' own time, body(): lax.scan(accumulate, jnp.zeros((channels, 27 * channels), f32), jnp.arang...  41.3 us
    all_gather x1, waiting for transfers between devices, body(): table = lax.all_gather(own, 'beam', axis=0, tiled=True)  36 us
  transfers between devices with their start and end apart: 12, of which 5 were waited for; matrix products, arithmetic and copies ran while one was open for 31% of the time, Pallas kernels for 0%

commit v1 on v0

v1 whole, which is shorter than its diff:
```python
import jax
import jax.numpy as jnp
from jax import lax
from jax.experimental import pallas as pl
from jax.experimental.pallas import tpu as pltpu
from jax.sharding import PartitionSpec as P

BLOCK = 8
REACH = 3
SPARE = 8
LIMIT = 56 * 1024 * 1024
bf16 = jnp.bfloat16
f32 = jnp.float32


def contract(left, right, dims):
    return lax.dot_general(left, right, ((dims[0], dims[1]), ((), ())), preferred_element_type=f32)


def plain(left, right):
    return contract(left, right, ((1,), (0,)))


def by_last(left, right):
    return contract(left, right, ((1,), (1,)))


def by_first(left, right):
    return contract(left, right, ((0,), (0,)))


def slope_of(value, sig):
    return sig * (1.0 + value * (1.0 - sig))


def one_hot(index, count):
    places = lax.broadcasted_iota(jnp.int32, (count, index.shape[-1]), 0)
    return jnp.where(places == index, 1.0, 0.0).astype(bf16)


def spread(values, owner, owners):
    parts = [jnp.where(owner == h, values, 0.0).astype(bf16) for h in range(owners)]
    return jnp.concatenate(parts, 0)


def pick(stacked, owner, owners):
    width = stacked.shape[0] // owners
    total = jnp.where(owner == 0, stacked[:width], 0.0)
    for h in range(1, owners):
        total = total + jnp.where(owner == h, stacked[h * width : (h + 1) * width], 0.0)
    return total


def store_taps(taps, row, first, tiles):
    count, channels, depth = tiles.shape
    flat = tiles.reshape(count * channels, depth)
    lane = lax.broadcasted_iota(jnp.int32, flat.shape, 1)
    before = jnp.where(lane == 0, 0.0, pltpu.roll(flat, 1, 1))
    after = jnp.where(lane == depth - 1, 0.0, pltpu.roll(flat, depth - 1, 1))
    for place, value in enumerate((before, flat, after)):
        taps[row, first : first + count, place * channels : (place + 1) * channels, :] = (
            value.reshape(count, channels, depth).astype(bf16)
        )


def columns(taps, row, first, count):
    wide = []
    for y in range(first, first + count):
        pieces = [taps[row + a, y + b] for a in range(REACH) for b in range(REACH)]
        wide.append(jnp.concatenate(pieces, 0))
    return jnp.concatenate(wide, 1)


def convolve_row(taps, weight, row, height):
    return jnp.concatenate(
        [plain(weight, columns(taps, row, y, 2)) for y in range(0, height, 2)], 1
    )


def forward_kernel(
    feat, x_low, x_high, y_low, y_high, mask, owner, local, weight, taps, slopes, partial, total
):
    rows, channels, height, depth = feat.shape
    owners, _, frag_dev = partial.shape

    def turned(block):
        return jnp.swapaxes(block.astype(f32), 0, 1)

    store_taps(taps, 0, 1, turned(x_low[...]))
    store_taps(taps, rows + 1, 1, turned(x_high[...]))

    def fill(x, _):
        tiles = turned(feat[x])
        live = mask[x]
        gates = [live[:, y * depth : (y + 1) * depth] for y in range(height)]
        gates = jnp.concatenate([jnp.broadcast_to(g, (1, channels, depth)) for g in gates], 0)
        store_taps(taps, x + 1, 1, tiles * gates)
        return 0

    lax.fori_loop(0, rows, fill, 0)

    def edges(x, _):
        store_taps(taps, x, 0, y_low[x].astype(f32)[None])
        store_taps(taps, x, height + 1, y_high[x].astype(f32)[None])
        return 0

    lax.fori_loop(0, rows + 2, edges, 0)
    total[...] = jnp.zeros_like(total)

    def one_row(x, _):
        conv = convolve_row(taps, weight[...], x, height)
        active = jnp.concatenate(
            [taps[x + 1, y + 1, channels : 2 * channels, :] for y in range(height)], 1
        )
        live = mask[x]
        sig = jax.nn.sigmoid(conv)
        hidden = live * (active.astype(f32) + conv * sig)
        slopes[x] = live * slope_of(conv, sig)
        tallies = lax.broadcasted_iota(jnp.int32, (total.shape[0] - owners * channels, 1), 0)
        heads = jnp.where(tallies == owner[x], live, 0.0).astype(bf16)
        rising = jnp.concatenate([spread(hidden, owner[x], owners), heads], 0)
        total[...] += by_last(rising, one_hot(local[x], frag_dev))
        return 0

    lax.fori_loop(0, rows, one_row, 0)
    for h in range(owners):
        partial[h, :channels] = total[h * channels : (h + 1) * channels]
        place = owners * channels + h
        tally = total[place : place + 1]
        partial[h, channels:] = jnp.broadcast_to(tally, (SPARE, frag_dev))


def pool_kernel(parts, pooled, divisor):
    sums = parts[0]
    for h in range(1, parts.shape[0]):
        sums = sums + parts[h]
    channels = pooled.shape[1]
    below = jnp.maximum(sums[channels:], 1.0)
    divisor[...] = below
    result = (sums[:channels] / below[:1]).astype(bf16)
    for h in range(pooled.shape[0]):
        pooled[h] = result


def fragment_kernel(
    table, mine, embed, message, update, cotangent, owner, local, target, out, partial, direct
):
    owners, channels, frag_dev = table.shape
    flat = table[...].reshape(owners * channels, frag_dev)
    from_local = one_hot(local[...], frag_dev)
    source = pick(plain(flat, from_local), owner[...], owners).astype(bf16)
    pre_source = by_first(source, embed[...])
    sig_source = jax.nn.sigmoid(pre_source)
    own_source = (pre_source * sig_source).astype(bf16)
    pre_msg = plain(own_source, message[...])
    sig_msg = jax.nn.sigmoid(pre_msg)
    messages = (pre_msg * sig_msg).astype(bf16)
    to_target = one_hot(target[...], frag_dev)
    gathered = plain(to_target, messages).astype(bf16)
    pre_own = by_first(mine[...], embed[...])
    sig_own = jax.nn.sigmoid(pre_own)
    own = (pre_own * sig_own).astype(bf16)
    out[...] = (own.astype(f32) + plain(gathered, update[...])).astype(bf16)
    back_agg = by_last(cotangent[...], update[...]).astype(bf16)
    back_edge = by_first(to_target, back_agg)
    back_pre = (back_edge * slope_of(pre_msg, sig_msg)).astype(bf16)
    back_source = by_last(back_pre, message[...]) * slope_of(pre_source, sig_source)
    back_pooled = by_last(embed[...], back_source.astype(bf16))
    scattered = by_last(spread(back_pooled, owner[...], owners), from_local)
    partial[...] = scattered.reshape(partial.shape).astype(partial.dtype)
    near = cotangent[...].astype(f32) * slope_of(pre_own, sig_own)
    rough = near.astype(bf16)
    rest = (near - rough.astype(f32)).astype(bf16)
    direct[...] = by_last(embed[...], rough) + by_last(embed[...], rest)


def mean_kernel(parts, direct, divisor, mean):
    total = direct[...]
    for h in range(parts.shape[0]):
        total = total + parts[h].astype(f32)
    result = (total / divisor[:1]).astype(bf16)
    for h in range(mean.shape[0]):
        mean[h] = result


def hidden_kernel(table, owner, local, mask, slopes, back_hidden, back_conv):
    owners, channels, frag_dev = table.shape
    rows, height, _, depth = back_conv.shape
    flat = table[...].reshape(owners * channels, frag_dev)

    def one_row(x, _):
        found = plain(flat, one_hot(local[x], frag_dev))
        hidden = pick(found, owner[x], owners)
        back_hidden[x] = mask[x] * hidden
        grad = (hidden * slopes[x]).astype(bf16)
        for y in range(height):
            back_conv[x, y] = grad[:, y * depth : (y + 1) * depth]
        return 0

    lax.fori_loop(0, rows, one_row, 0)


def weight_kernel(taps, back_conv, grad):
    rows, height, _, _ = back_conv.shape
    grad[...] = jnp.zeros_like(grad)

    def one_row(x, _):
        total = None
        for y in range(0, height, 2):
            slab = jnp.concatenate([back_conv[x, y], back_conv[x, y + 1]], 1)
            term = by_last(slab, columns(taps, x, y, 2))
            total = term if total is None else total + term
        grad[...] += total
        return 0

    lax.fori_loop(0, rows, one_row, 0)


def backward_kernel(
    back_conv, x_low, x_high, y_low, y_high, back_hidden, mask, weight, grad, taps
):
    rows, height, channels, depth = back_conv.shape
    store_taps(taps, 0, 1, x_low[...].astype(f32))
    store_taps(taps, rows + 1, 1, x_high[...].astype(f32))

    def fill(x, _):
        store_taps(taps, x + 1, 1, back_conv[x].astype(f32))
        return 0

    lax.fori_loop(0, rows, fill, 0)

    def edges(x, _):
        store_taps(taps, x, 0, y_low[x].astype(f32)[None])
        store_taps(taps, x, height + 1, y_high[x].astype(f32)[None])
        return 0

    lax.fori_loop(0, rows + 2, edges, 0)

    def one_row(x, _):
        result = mask[x] * (back_hidden[x] + convolve_row(taps, weight[...], x, height))
        tiles = [result[:, y * depth : (y + 1) * depth][None] for y in range(height)]
        grad[x] = jnp.swapaxes(jnp.concatenate(tiles, 0), 0, 1)
        return 0

    lax.fori_loop(0, rows, one_row, 0)


def call(kernel, shapes, *operands, scratch=()):
    return pl.pallas_call(
        kernel,
        out_shape=[jax.ShapeDtypeStruct(shape, kind) for shape, kind in shapes],
        scratch_shapes=list(scratch),
        compiler_params=pltpu.CompilerParams(vmem_limit_bytes=LIMIT),
    )(*operands)


def pass_on(low, high, axis):
    count = lax.axis_size(axis)
    up = [(i, i + 1) for i in range(count - 1)]
    down = [(i + 1, i) for i in range(count - 1)]
    return lax.ppermute(high, axis, up), lax.ppermute(low, axis, down)


def exchange(parts, axes):
    return lax.all_to_all(parts, axes, 0, 0, tiled=True)


def sum_everywhere(values, axes):
    count = lax.axis_size(axes)
    flat = values.reshape(-1)
    share = -(-flat.shape[0] // count)
    flat = jnp.pad(flat, (0, share * count - flat.shape[0])).reshape(count, share)
    mine = exchange(flat, axes).sum(0)
    back = exchange(jnp.broadcast_to(mine[None], flat.shape), axes)
    return back.reshape(-1)[: values.size].reshape(values.shape)


def body(
    features,
    occupied,
    voxel_fragment,
    conv_weight,
    embed_weight,
    message_weight,
    update_weight,
    edge_source,
    edge_target,
    out_cotangent,
):
    rows, channels, height, depth = features.shape
    frag_dev, hid = out_cotangent.shape
    owners = lax.axis_size("beam")
    edge_count = edge_source.shape[0]
    plane = height * depth
    mask = jnp.repeat(jnp.repeat(jnp.repeat(occupied, BLOCK, 0), BLOCK, 1), BLOCK, 2)
    gate = mask.astype(bf16)

    x_low, x_high = pass_on(
        features[0] * gate[0][None], features[-1] * gate[-1][None], "drift"
    )
    ends = []
    for y in (0, height - 1):
        side = features[:, :, y] * gate[:, None, y]
        ends.append(jnp.concatenate([x_low[None, :, y], side, x_high[None, :, y]], 0))
    y_low, y_high = pass_on(ends[0], ends[1], "beam")

    live = mask.astype(f32).reshape(rows, 1, plane)
    owner = (voxel_fragment // frag_dev).reshape(rows, 1, plane)
    local = (voxel_fragment % frag_dev).reshape(rows, 1, plane)
    heads = -(-owners // 16) * 16
    padded = (rows + 2, height + 2, REACH * channels, depth)
    taps, slopes, partial = call(
        forward_kernel,
        [
            (padded, bf16),
            ((rows, channels, plane), f32),
            ((owners, channels + SPARE, frag_dev), f32),
        ],
        features, x_low, x_high, y_low, y_high, live, owner, local, conv_weight,
        scratch=[pltpu.VMEM((owners * channels + heads, frag_dev), f32)],
    )
    spread_shape = (owners, channels, frag_dev)
    pooled, divisor = call(
        pool_kernel,
        [(spread_shape, bf16), ((SPARE, frag_dev), f32)],
        exchange(partial, "beam"),
    )
    table = exchange(pooled, "beam")
    fragment_out, back_parts, direct = call(
        fragment_kernel,
        [((frag_dev, hid), bf16), (spread_shape, f32), ((channels, frag_dev), f32)],
        table, pooled[0], embed_weight, message_weight, update_weight, out_cotangent,
        (edge_source // frag_dev).reshape(1, edge_count),
        (edge_source % frag_dev).reshape(1, edge_count),
        edge_target.reshape(1, edge_count),
    )
    (mean,) = call(
        mean_kernel, [(spread_shape, bf16)], exchange(back_parts, "beam"), direct, divisor
    )
    back_hidden, back_conv = call(
        hidden_kernel,
        [((rows, channels, plane), f32), ((rows, height, channels, depth), bf16)],
        exchange(mean, "beam"), owner, local, live, slopes,
    )
    gx_low, gx_high = pass_on(back_conv[0], back_conv[-1], "drift")
    ends = [
        jnp.concatenate([gx_low[None, y], back_conv[:, y], gx_high[None, y]], 0)
        for y in (0, height - 1)
    ]
    gy_low, gy_high = pass_on(ends[0], ends[1], "beam")
    (local_grad,) = call(weight_kernel, [(conv_weight.shape, f32)], taps, back_conv)
    taps_count = REACH * REACH * REACH
    flipped = (
        conv_weight.reshape(channels, taps_count, channels)[:, ::-1, :]
        .transpose(2, 1, 0)
        .reshape(channels, taps_count * channels)
    )
    (grad_features,) = call(
        backward_kernel,
        [(features.shape, f32)],
        back_conv, gx_low, gx_high, gy_low, gy_high, back_hidden, live, flipped,
        scratch=[pltpu.VMEM(padded, bf16)],
    )
    grad_conv = sum_everywhere(local_grad, ("drift", "beam"))
    return fragment_out, grad_features, grad_conv


def solution(mesh):
    return jax.shard_map(
        body,
        mesh=mesh,
        in_specs=(
            P("drift", None, "beam", None),
            P("drift", "beam", None),
            P("drift", "beam", None),
            P(),
            P(),
            P(),
            P(),
            P(("drift", "beam")),
            P(("drift", "beam")),
            P(("drift", "beam"), None),
        ),
        out_specs=(P(("drift", "beam"), None), P("drift", None, "beam", None), P()),
        check_vma=False,
    )
```

time: 855 us -> 160 us (0.19); the launches traced: 840 us -> 158 us
  local copies, waits for them, and re-layouts: 271 us -> 14.6 us
  other arithmetic: 213 us -> 3.14 us
  loops' own time: 118 us -> 0 us
  waiting for transfers between devices: 98.4 us -> 9.93 us
  Pallas kernels: 0 us -> 53.6 us
  matrix products: 39.3 us -> 0 us
  between operations: 15.1 us -> 0.93 us
  blocking collectives: 52.8 us -> 39.9 us
    scatter-add x4 -> x0, other arithmetic: 190 us -> none  [the longest x1 88.6 us: body(): sums = jax.ops.segment_sum(by_voxel, frag_ids, num_segments=frag_row).T]
    dynamic_slice x48 -> x0, local copies, waits for them, and re-layouts: 162 us -> none  [the longest x24 148 us: columns(): piece = lax.dynamic_slice(padded, index, (1, channels, height, depth))]
    another operation x3 -> x0, loops' own time: 118 us -> none  [the longest x2 77.1 us: convolve(): result = lax.map(one_row, jnp.arange(rows, dtype=jnp.int32))]
    gather x4 -> x0, local copies, waits for them, and re-layouts: 68.8 us -> none  [the longest x2 60 us: body(): jnp.take(mean_all, frag_ids, axis=1).reshape(channels, rows, height, depth)]
    pallas_call x0 -> x7, Pallas kernels: none -> 53.6 us  [call(): pl.pallas_call(kernel, out_shape=[jax.ShapeDtypeStruct(shape, kind) for s...]
    reduce_scatter x2 -> x0, waiting for transfers between devices: 53.2 us -> none  [the longest x1 53.2 us: body(): lax.psum_scatter(back_rows.astype(jnp.bfloat16), 'beam', scatter_dimensio...]
    all_to_all x0 -> x3, blocking collectives: none -> 39.9 us  [exchange(): return lax.all_to_all(parts, axes, 0, 0, tiled=True)]
    dot_general x30 -> x0, matrix products: 39.3 us -> none  [the longest x16 22.9 us: one_row(): jnp.dot(weight, columns(padded, row), preferred_element_type=jnp.float32)]
  transfers between devices with their start and end apart: 12 -> 11, of which waited for: 5 -> 4; matrix products, arithmetic and copies ran while one was open for 31% -> 6% of each run, Pallas kernels for 0% -> 7%
where the time goes in v1:
time: 160 us; the launch traced here: 158 us
  Pallas kernels  53.6 us (34%)
  blocking collectives  39.9 us (25%)
  starting transfers between devices  35.6 us (22%)
  local copies, waits for them, and re-layouts  14.6 us (9%)
  waiting for transfers between devices  9.93 us (6%)
  other arithmetic  3.14 us (2%)
    pallas_call x7, Pallas kernels, call(): pl.pallas_call(kernel, out_shape=[jax.ShapeDtypeStruct(shape, kind) for s...  53.6 us
    all_to_all x3, blocking collectives, exchange(): return lax.all_to_all(parts, axes, 0, 0, tiled=True)  39.9 us
    ppermute x8, starting transfers between devices, pass_on(): return (lax.ppermute(high, axis, up), lax.ppermute(low, axis, down))  22.5 us
    all_to_all x3, starting transfers between devices, exchange(): return lax.all_to_all(parts, axes, 0, 0, tiled=True)  13.1 us
    ppermute x8, waiting for transfers between devices, pass_on(): return (lax.ppermute(high, axis, up), lax.ppermute(low, axis, down))  5.58 us
    all_to_all x3, waiting for transfers between devices, exchange(): return lax.all_to_all(parts, axes, 0, 0, tiled=True)  4.34 us
  transfers between devices with their start and end apart: 11, of which 4 were waited for; matrix products, arithmetic and copies ran while one was open for 6% of the time, Pallas kernels for 7%

profile of v1, /device:TPU:1, one launch (start us, length us, event | category | flops | bytes accessed | tf_op | source)
XLA Modules:
  0.0 157.6 jit_solution(3580692511984622659)
XLA Ops:
  0.6 0.8 convert_bitcast_fusion
  1.4 0.1 copy.34
  1.5 0.1 copy.35
  1.6 1.0 fusion.9
  2.6 0.1 fusion
  2.6 4.5 %collective-permute-start = (bf16[32,16,128]{2,0,1:T(8,128)(2,1)S(1)}, bf16[32,16,128]{2,0,1:T(8,128)(2,1)S(1)}, u32[]{:S(2)}, u32[]{:S(2)}) collective-permute-start(bf16[32,16,128]{2,0,1:T(8,128)(2,1)S(1)} %get-tuple-element.46), channel_id=1, source_target_pairs={{0,8},{8,16},{16,24},{1,9},{9,17},{17,25},{2,10},{10,18},{18,26},{... | collective-permute-start | bytes 393224 | tf_op jit(solution)/shard_map/ppermute | solution.py:261
  7.2 1.9 %collective-permute-start.1 = (bf16[32,16,128]{2,0,1:T(8,128)(2,1)S(1)}, bf16[32,16,128]{2,0,1:T(8,128)(2,1)S(1)}, u32[]{:S(2)}, u32[]{:S(2)}) collective-permute-start(bf16[32,16,128]{2,0,1:T(8,128)(2,1)S(1)} %get-tuple-element.45), channel_id=1, source_target_pairs={{8,0},{16,8},{24,16},{9,1},{17,9},{25,17},{10,2},{18,10},{26,18},{... | collective-permute-start | bytes 393224 | tf_op jit(solution)/shard_map/ppermute | solution.py:261
  9.1 1.5 fusion.8
  10.6 0.1 broadcast_in_dim.26
  10.6 0.1 slice.85
  10.7 0.1 broadcast_in_dim.25
  10.8 0.1 slice.79
  10.9 1.6 add_select_fusion
  12.5 0.0 collective-permute-done
  12.5 0.9 collective-permute-done.1
  13.5 1.3 collective-permute-start.3
  14.8 4.0 %collective-permute-start.2 = (bf16[10,32,128]{2,1,0:T(8,128)(2,1)S(1)}, bf16[10,32,128]{2,1,0:T(8,128)(2,1)S(1)}, u32[]{:S(2)}, u32[]{:S(2)}) collective-permute-start(bf16[10,32,128]{2,1,0:T(8,128)(2,1)S(1)} %pad_maximum_fusion), channel_id=1, source_target_pairs={{0,1},{1,2},{2,3},{3,4},{4,5},{5,6},{6,7},{8,9},{9,10},{10,11},{11... | collective-permute-start | bytes 245768 | tf_op jit(solution)/shard_map/ppermute | solution.py:261
  18.8 0.1 broadcast_in_dim.28
  18.9 0.1 convert_element_type.40
  19.0 0.7 copy.39.x_low
  19.7 0.7 copy.40.x_high
  20.4 0.0 collective-permute-done.3.y_high
  20.4 0.0 collective-permute-done.2.y_low
  20.4 0.0 copy-start.5
  20.4 0.7 broadcast_in_dim.29.mask
  21.1 14.9 %shard_map.121 = (bf16[10,18,96,128]{3,2,1,0:T(8,128)(2,1)}, f32[8,32,2048]{2,1,0:T(8,128)}, f32[8,40,256]{2,1,0:T(8,128)}) custom-call(bf16[8,32,16,128]{3,2,1,0:T(8,128)(2,1)} %feat.1, bf16[32,16,128]{2,1,0:T(8,128)(2,1)} %copy.39.x_low, bf16[32,16,128]{2,1,0:T(8,128)(2,1)} %copy.40.x_high, bf16[10,32,128]{2,1,0:T(8,128)(2,1)} %copy-done.5, ...), custom_call_target="tpu_custom_call" | custom-call | tf_op jit(solution)/shard_map/pallas_call | solution.py:249
  36.0 17.4 %all_to_all.38.parts = f32[8,40,256]{2,1,0:T(8,128)} all-to-all(f32[8,40,256]{2,1,0:T(8,128)} %get-tuple-element.13), channel_id=1, replica_groups=mesh['drift'=4,'beam'=8] {'beam'}, dimensions={0} | all-to-all | bytes 655360 | tf_op jit(solution)/shard_map/all_to_all | solution.py:265
  53.4 1.7 %shard_map.122 = (bf16[8,32,256]{2,1,0:T(8,128)(2,1)}, f32[8,256]{1,0:T(8,128)}) custom-call(f32[8,40,256]{2,1,0:T(8,128)} %all_to_all.38.parts), custom_call_target="tpu_custom_call" | custom-call | tf_op jit(solution)/shard_map/pallas_call | solution.py:249
  55.1 3.4 %all-to-all-start.1 = ((bf16[8,32,256]{2,1,0:T(8,128)(2,1)}), bf16[8,32,256]{2,1,0:T(8,128)(2,1)S(1)}, u32[]{:S(2)}, u32[]{:S(2)}) async-start(bf16[8,32,256]{2,1,0:T(8,128)(2,1)} %get-tuple-element.14), calls=%async_computation.1 | async-start | bytes 262144 | tf_op jit(solution)/shard_map/all_to_all | solution.py:265
  58.5 0.6 add_select_fusion.2
  59.1 1.3 slice_bitcast_fusion.4.mine
  60.4 4.3 %all-to-all-done.1.table = bf16[8,32,256]{2,1,0:T(8,128)(2,1)S(1)} async-done(((bf16[8,32,256]{2,1,0:T(8,128)(2,1)}), bf16[8,32,256]{2,1,0:T(8,128)(2,1)S(1)}, u32[]{:S(2)}, u32[]{:S(2)}) %all-to-all-start.1) | async-done | bytes 131104 | tf_op jit(solution)/shard_map/all_to_all | solution.py:265
  64.7 0.6 copy-done
  65.4 4.3 %shard_map.123 = (bf16[256,256]{1,0:T(8,128)(2,1)}, f32[8,32,256]{2,1,0:T(8,128)}, f32[32,256]{1,0:T(8,128)}) custom-call(bf16[8,32,256]{2,1,0:T(8,128)(2,1)} %copy-done, bf16[32,256]{1,0:T(8,128)(2,1)} %slice_bitcast_fusion.4.mine, bf16[32,256]{1,0:T(8,128)(2,1)} %embed.1, bf16[256,256]{1,0:T(8,128)(2,1)} %message.1, bf16[256,256]{1,0:T(8,128)(2,1)} %update.1, ...), custom_call_target="tpu_custom_call" | custom-call | tf_op jit(solution)/shard_map/pallas_call | solution.py:249
  69.6 11.2 %all_to_all.39.parts = f32[8,32,256]{2,1,0:T(8,128)} all-to-all(f32[8,32,256]{2,1,0:T(8,128)} %get-tuple-element.16), channel_id=1, replica_groups=mesh['drift'=4,'beam'=8] {'beam'}, dimensions={0} | all-to-all | bytes 524288 | tf_op jit(solution)/shard_map/all_to_all | solution.py:265
  80.9 1.6 %shard_map.124 = bf16[8,32,256]{2,1,0:T(8,128)(2,1)} custom-call(f32[8,32,256]{2,1,0:T(8,128)} %all_to_all.39.parts, f32[32,256]{1,0:T(8,128)} %get-tuple-element.17.direct, f32[8,256]{1,0:T(8,128)} %get-tuple-element.18.divisor), custom_call_target="tpu_custom_call" | custom-call | tf_op jit(solution)/shard_map/pallas_call | solution.py:249
  82.5 11.2 %all_to_all.40.table = bf16[8,32,256]{2,1,0:T(8,128)(2,1)} all-to-all(bf16[8,32,256]{2,1,0:T(8,128)(2,1)} %shard_map.124), channel_id=1, replica_groups=mesh['drift'=4,'beam'=8] {'beam'}, dimensions={0} | all-to-all | bytes 262144 | tf_op jit(solution)/shard_map/all_to_all | solution.py:265
  93.7 7.8 %shard_map.125 = (f32[8,32,2048]{2,1,0:T(8,128)}, bf16[8,16,32,128]{3,2,1,0:T(8,128)(2,1)}) custom-call(bf16[8,32,256]{2,1,0:T(8,128)(2,1)} %all_to_all.40.table, s32[8,1,2048]{2,1,0:T(1,128)} %bitcast.62, s32[8,1,2048]{2,1,0:T(1,128)} %bitcast.60, f32[8,1,2048]{2,1,0:T(1,128)} %broadcast_in_dim.29.mask, f32[8,32,2048]{2,1,0:T(8,128)} %get-tuple-element.19.slopes), custom_call_target="tpu_custom_call" | custom-call | tf_op jit(solution)/shard_map/pallas_call | solution.py:249
  101.5 1.0 slice_bitcast_fusion
  102.5 0.0 copy-start.1
  102.5 12.0 %shard_map.127 = f32[32,864]{1,0:T(8,128)} custom-call(bf16[10,18,96,128]{3,2,1,0:T(8,128)(2,1)} %get-tuple-element.22.taps, bf16[8,16,32,128]{3,2,1,0:T(8,128)(2,1)} %get-tuple-element.20.back_conv), custom_call_target="tpu_custom_call" | custom-call | tf_op jit(solution)/shard_map/pallas_call | solution.py:249
  114.5 1.7 %copy.44 = f32[32,1,864]{2,1,0:T(1,128)} copy(f32[32,1,864]{2,0,1:T(8,128)} %bitcast.63) | data formatting | bytes 221184 | tf_op jit(solution)/shard_map/all_to_all | solution.py:265
  116.2 5.1 %all-to-all-start.4 = ((f32[32,1,864]{2,1,0:T(1,128)}), f32[32,1,864]{2,1,0:T(1,128)S(1)}, u32[]{:S(2)}, u32[]{:S(2)}) async-start(f32[32,1,864]{2,1,0:T(1,128)} %copy.44), calls=%async_computation.4 | async-start | bytes 229376 | tf_op jit(solution)/shard_map/all_to_all | solution.py:265
  121.3 3.5 %collective-permute-start.4 = (bf16[16,32,128]{2,1,0:T(8,128)(2,1)S(1)}, bf16[16,32,128]{2,1,0:T(8,128)(2,1)S(1)}, u32[]{:S(2)}, u32[]{:S(2)}) collective-permute-start(bf16[16,32,128]{2,1,0:T(8,128)(2,1)S(1)} %get-tuple-element.26), channel_id=1, source_target_pairs={{0,8},{8,16},{16,24},{1,9},{9,17},{17,25},{2,10},{10,18},{18,26},{... | collective-permute-start | bytes 393224 | tf_op jit(solution)/shard_map/ppermute | solution.py:261
  124.9 1.9 %collective-permute-start.5 = (bf16[16,32,128]{2,1,0:T(8,128)(2,1)S(1)}, bf16[16,32,128]{2,1,0:T(8,128)(2,1)S(1)}, u32[]{:S(2)}, u32[]{:S(2)}) collective-permute-start(bf16[16,32,128]{2,1,0:T(8,128)(2,1)S(1)} %get-tuple-element.25), channel_id=1, source_target_pairs={{8,0},{16,8},{24,16},{9,1},{17,9},{25,17},{10,2},{18,10},{26,18},{... | collective-permute-start | bytes 393224 | tf_op jit(solution)/shard_map/ppermute | solution.py:261
  126.8 0.9 slice_bitcast_fusion.2
  127.7 0.0 collective-permute-done.4.x_low
  127.7 3.4 %collective-permute-done.5.x_high = bf16[16,32,128]{2,1,0:T(8,128)(2,1)S(1)} collective-permute-done((bf16[16,32,128]{2,1,0:T(8,128)(2,1)S(1)}, bf16[16,32,128]{2,1,0:T(8,128)(2,1)S(1)}, u32[]{:S(2)}, u32[]{:S(2)}) %collective-permute-start.5) | collective-permute-done | bytes 131104 | tf_op jit(solution)/shard_map/ppermute | solution.py:261
  131.2 0.0 all-to-all-done.4
  131.2 0.1 reduce_sum.9
  131.3 0.7 broadcast_in_dim.30
  132.0 4.6 %all-to-all-start.5 = ((f32[32,1,864]{2,1,0:T(1,128)}), f32[32,1,864]{2,1,0:T(1,128)S(1)}, u32[]{:S(2)}, u32[]{:S(2)}) async-start(f32[32,1,864]{2,1,0:T(1,128)} %broadcast_in_dim.30), calls=%async_computation.5 | async-start | bytes 229376 | tf_op jit(solution)/shard_map/all_to_all | solution.py:265
  136.6 1.3 collective-permute-start.7
  137.9 4.0 %collective-permute-start.6 = (bf16[10,32,128]{2,1,0:T(8,128)(2,1)S(1)}, bf16[10,32,128]{2,1,0:T(8,128)(2,1)S(1)}, u32[]{:S(2)}, u32[]{:S(2)}) collective-permute-start(bf16[10,32,128]{2,1,0:T(8,128)(2,1)S(1)} %pad_maximum_fusion.2), channel_id=1, source_target_pairs={{0,1},{1,2},{2,3},{3,4},{4,5},{5,6},{6,7},{8,9},{9,10},{10,11},{11... | collective-permute-start | bytes 245768 | tf_op jit(solution)/shard_map/ppermute | solution.py:261
  141.9 0.2 reshape.68
  142.2 0.2 rev.3
  142.4 0.6 copy.43
  142.9 0.9 reshape.69.weight
  143.8 0.0 collective-permute-done.7.y_high
  143.8 1.2 collective-permute-done.6.y_low
  145.0 0.6 copy-done.7
  145.7 11.3 %shard_map.126 = f32[8,32,16,128]{3,2,1,0:T(8,128)} custom-call(bf16[8,16,32,128]{3,2,1,0:T(8,128)(2,1)} %get-tuple-element.20.back_conv, bf16[16,32,128]{2,1,0:T(8,128)(2,1)} %copy-done.2, bf16[16,32,128]{2,1,0:T(8,128)(2,1)} %copy-done.3, bf16[10,32,128]{2,1,0:T(8,128)(2,1)} %copy-done.7, bf16[10,32,128]{2,1,0:T(8,128)(2,1)} %copy-done.6, ...), custom_call_target="tpu_custom_call" | custom-call | tf_op jit(solution)/shard_map/pallas_call | solution.py:249
  157.0 0.0 all-to-all-done.5
  157.0 0.7 copy.65
  (28 shorter events, 0.1 us)
Async XLA Ops:
  2.6 9.9 %collective-permute-start = (bf16[32,16,128]{2,0,1:T(8,128)(2,1)S(1)}, bf16[32,16,128]{2,0,1:T(8,128)(2,1)S(1)}, u32[]{:S(2)}, u32[]{:S(2)}) collective-permute-start(bf16[32,16,128]{2,0,1:T(8,128)(2,1)S(1)} %get-tuple-element.46), channel_id=1, source_target_pairs={{0,8},{8,16},{16,24},{1,9},{9,17},{17,25},{2,10},{10,18},{18,26},{... | collective-permute-start | bytes 393224 | tf_op jit(solution)/shard_map/ppermute | solution.py:261
  7.2 6.3 %collective-permute-start.1 = (bf16[32,16,128]{2,0,1:T(8,128)(2,1)S(1)}, bf16[32,16,128]{2,0,1:T(8,128)(2,1)S(1)}, u32[]{:S(2)}, u32[]{:S(2)}) collective-permute-start(bf16[32,16,128]{2,0,1:T(8,128)(2,1)S(1)} %get-tuple-element.45), channel_id=1, source_target_pairs={{8,0},{16,8},{24,16},{9,1},{17,9},{25,17},{10,2},{18,10},{26,18},{... | collective-permute-start | bytes 393224 | tf_op jit(solution)/shard_map/ppermute | solution.py:261
  13.4 45.0 %copy-start.8 = (s32[1024]{0:T(1024)S(1)}, s32[1024]{0:T(1024)}, u32[]{:S(2)}) copy-start(s32[1024]{0:T(1024)} %param.17) | copy-start | bytes 12292
  13.5 7.0 %collective-permute-start.3 = (bf16[10,32,128]{2,1,0:T(8,128)(2,1)S(1)}, bf16[10,32,128]{2,1,0:T(8,128)(2,1)S(1)}, u32[]{:S(2)}, u32[]{:S(2)}) collective-permute-start(bf16[10,32,128]{2,1,0:T(8,128)(2,1)S(1)} %pad_maximum_fusion.1), channel_id=1, source_target_pairs={{1,0},{2,1},{3,2},{4,3},{5,4},{6,5},{7,6},{9,8},{10,9},{11,10},{12... | collective-permute-start | bytes 245768 | tf_op jit(solution)/shard_map/ppermute | solution.py:261
  14.8 5.6 %collective-permute-start.2 = (bf16[10,32,128]{2,1,0:T(8,128)(2,1)S(1)}, bf16[10,32,128]{2,1,0:T(8,128)(2,1)S(1)}, u32[]{:S(2)}, u32[]{:S(2)}) collective-permute-start(bf16[10,32,128]{2,1,0:T(8,128)(2,1)S(1)} %pad_maximum_fusion), channel_id=1, source_target_pairs={{0,1},{1,2},{2,3},{3,4},{4,5},{5,6},{6,7},{8,9},{9,10},{10,11},{11... | collective-permute-start | bytes 245768 | tf_op jit(solution)/shard_map/ppermute | solution.py:261
  20.4 0.7 copy-start.4
  20.4 0.7 copy-start.5
  55.1 9.6 %all-to-all-start.1 = ((bf16[8,32,256]{2,1,0:T(8,128)(2,1)}), bf16[8,32,256]{2,1,0:T(8,128)(2,1)S(1)}, u32[]{:S(2)}, u32[]{:S(2)}) async-start(bf16[8,32,256]{2,1,0:T(8,128)(2,1)} %get-tuple-element.14), calls=%async_computation.1 | async-start | bytes 262144 | tf_op jit(solution)/shard_map/all_to_all | solution.py:265
  64.7 0.6 copy-start
  102.5 39.5 %copy-start.1 = (bf16[32,864]{1,0:T(8,128)(2,1)S(1)}, bf16[32,864]{1,0:T(8,128)(2,1)}, u32[]{:S(2)}) copy-start(bf16[32,864]{1,0:T(8,128)(2,1)} %weight.1) | copy-start | bytes 165892
  116.2 15.0 %all-to-all-start.4 = ((f32[32,1,864]{2,1,0:T(1,128)}), f32[32,1,864]{2,1,0:T(1,128)S(1)}, u32[]{:S(2)}, u32[]{:S(2)}) async-start(f32[32,1,864]{2,1,0:T(1,128)} %copy.44), calls=%async_computation.4 | async-start | bytes 229376 | tf_op jit(solution)/shard_map/all_to_all | solution.py:265
  121.3 6.4 %collective-permute-start.4 = (bf16[16,32,128]{2,1,0:T(8,128)(2,1)S(1)}, bf16[16,32,128]{2,1,0:T(8,128)(2,1)S(1)}, u32[]{:S(2)}, u32[]{:S(2)}) collective-permute-start(bf16[16,32,128]{2,1,0:T(8,128)(2,1)S(1)} %get-tuple-element.26), channel_id=1, source_target_pairs={{0,8},{8,16},{16,24},{1,9},{9,17},{17,25},{2,10},{10,18},{18,26},{... | collective-permute-start | bytes 393224 | tf_op jit(solution)/shard_map/ppermute | solution.py:261
  124.9 6.3 %collective-permute-start.5 = (bf16[16,32,128]{2,1,0:T(8,128)(2,1)S(1)}, bf16[16,32,128]{2,1,0:T(8,128)(2,1)S(1)}, u32[]{:S(2)}, u32[]{:S(2)}) collective-permute-start(bf16[16,32,128]{2,1,0:T(8,128)(2,1)S(1)} %get-tuple-element.25), channel_id=1, source_target_pairs={{8,0},{16,8},{24,16},{9,1},{17,9},{25,17},{10,2},{18,10},{26,18},{... | collective-permute-start | bytes 393224 | tf_op jit(solution)/shard_map/ppermute | solution.py:261
  127.7 17.3 %copy-start.2 = (bf16[16,32,128]{2,1,0:T(8,128)(2,1)}, bf16[16,32,128]{2,1,0:T(8,128)(2,1)S(1)}, u32[]{:S(2)}) copy-start(bf16[16,32,128]{2,1,0:T(8,128)(2,1)S(1)} %collective-permute-done.4.x_low) | copy-start | bytes 393220
  131.2 13.9 %copy-start.3 = (bf16[16,32,128]{2,1,0:T(8,128)(2,1)}, bf16[16,32,128]{2,1,0:T(8,128)(2,1)S(1)}, u32[]{:S(2)}) copy-start(bf16[16,32,128]{2,1,0:T(8,128)(2,1)S(1)} %collective-permute-done.5.x_high) | copy-start | bytes 393220
  132.0 25.0 %all-to-all-start.5 = ((f32[32,1,864]{2,1,0:T(1,128)}), f32[32,1,864]{2,1,0:T(1,128)S(1)}, u32[]{:S(2)}, u32[]{:S(2)}) async-start(f32[32,1,864]{2,1,0:T(1,128)} %broadcast_in_dim.30), calls=%async_computation.5 | async-start | bytes 229376 | tf_op jit(solution)/shard_map/all_to_all | solution.py:265
  136.6 7.2 %collective-permute-start.7 = (bf16[10,32,128]{2,1,0:T(8,128)(2,1)S(1)}, bf16[10,32,128]{2,1,0:T(8,128)(2,1)S(1)}, u32[]{:S(2)}, u32[]{:S(2)}) collective-permute-start(bf16[10,32,128]{2,1,0:T(8,128)(2,1)S(1)} %pad_maximum_fusion.3), channel_id=1, source_target_pairs={{1,0},{2,1},{3,2},{4,3},{5,4},{6,5},{7,6},{9,8},{10,9},{11,10},{12... | collective-permute-start | bytes 245768 | tf_op jit(solution)/shard_map/ppermute | solution.py:261
  137.9 7.1 %collective-permute-start.6 = (bf16[10,32,128]{2,1,0:T(8,128)(2,1)S(1)}, bf16[10,32,128]{2,1,0:T(8,128)(2,1)S(1)}, u32[]{:S(2)}, u32[]{:S(2)}) collective-permute-start(bf16[10,32,128]{2,1,0:T(8,128)(2,1)S(1)} %pad_maximum_fusion.2), channel_id=1, source_target_pairs={{0,1},{1,2},{2,3},{3,4},{4,5},{5,6},{6,7},{8,9},{9,10},{10,11},{11... | collective-permute-start | bytes 245768 | tf_op jit(solution)/shard_map/ppermute | solution.py:261
  143.8 1.2 copy-start.6
  145.0 0.6 copy-start.7

commit v2 on v1

--- a/solution.py
+++ b/solution.py
@@ -7,7 +7,8 @@
 
 BLOCK = 8
 REACH = 3
-SPARE = 8
+SPARE = 16
+DIGIT = 128.0
 LIMIT = 56 * 1024 * 1024
 bf16 = jnp.bfloat16
 f32 = jnp.float32
@@ -45,9 +46,9 @@
 
 def pick(stacked, owner, owners):
     width = stacked.shape[0] // owners
-    total = jnp.where(owner == 0, stacked[:width], 0.0)
+    total = stacked[:width]
     for h in range(1, owners):
-        total = total + jnp.where(owner == h, stacked[h * width : (h + 1) * width], 0.0)
+        total = jnp.where(owner == h, stacked[h * width : (h + 1) * width], total)
     return total
 
 
@@ -66,15 +67,22 @@
 def columns(taps, row, first, count):
     wide = []
     for y in range(first, first + count):
-        pieces = [taps[row + a, y + b] for a in range(REACH) for b in range(REACH)]
-        wide.append(jnp.concatenate(pieces, 0))
+        wide.append(jnp.concatenate([taps[row + a, y] for a in range(REACH)], 0))
     return jnp.concatenate(wide, 1)
 
 
 def convolve_row(taps, weight, row, height):
-    return jnp.concatenate(
-        [plain(weight, columns(taps, row, y, 2)) for y in range(0, height, 2)], 1
-    )
+    depth = taps.shape[-1]
+    channels = weight.shape[0] // REACH
+    wide = height * depth
+    found = jnp.concatenate(
+        [plain(weight, columns(taps, row, y, 2)) for y in range(0, height + REACH - 1, 2)], 1
+    )
+    total = found[:channels, :wide]
+    for b in range(1, REACH):
+        part = found[b * channels : (b + 1) * channels, b * depth : b * depth + wide]
+        total = total + part
+    return total
 
 
 def forward_kernel(
@@ -123,21 +131,34 @@
         return 0
 
     lax.fori_loop(0, rows, one_row, 0)
+    line = lax.broadcasted_iota(jnp.int32, (SPARE, frag_dev), 0)
     for h in range(owners):
-        partial[h, :channels] = total[h * channels : (h + 1) * channels]
+        partial[h, :channels] = total[h * channels : (h + 1) * channels].astype(bf16)
         place = owners * channels + h
-        tally = total[place : place + 1]
-        partial[h, channels:] = jnp.broadcast_to(tally, (SPARE, frag_dev))
+        rest = jnp.broadcast_to(total[place : place + 1], (SPARE, frag_dev))
+        digits = jnp.zeros_like(rest)
+        for d in range(SPARE):
+            higher = jnp.floor(rest * (1.0 / DIGIT))
+            digits = jnp.where(line == d, rest - higher * DIGIT, digits)
+            rest = higher
+            if DIGIT ** (d + 1) > rows * height * depth:
+                break
+        partial[h, channels:] = digits.astype(bf16)
 
 
 def pool_kernel(parts, pooled, divisor):
-    sums = parts[0]
+    sums = parts[0].astype(f32)
     for h in range(1, parts.shape[0]):
-        sums = sums + parts[h]
+        sums = sums + parts[h].astype(f32)
     channels = pooled.shape[1]
-    below = jnp.maximum(sums[channels:], 1.0)
-    divisor[...] = below
-    result = (sums[:channels] / below[:1]).astype(bf16)
+    line = lax.broadcasted_iota(jnp.int32, (SPARE, sums.shape[1]), 0)
+    scale = jnp.zeros_like(sums[channels:])
+    for d in range(4):
+        scale = jnp.where(line == d, DIGIT**d, scale)
+    counts = jnp.sum(sums[channels:] * scale, axis=0, keepdims=True)
+    below = jnp.maximum(counts, 1.0)
+    divisor[...] = jnp.broadcast_to(below, divisor.shape)
+    result = (sums[:channels] / below).astype(bf16)
     for h in range(pooled.shape[0]):
         pooled[h] = result
 
@@ -201,14 +222,19 @@
 
 
 def weight_kernel(taps, back_conv, grad):
-    rows, height, _, _ = back_conv.shape
+    rows, height, channels, depth = back_conv.shape
+    empty = jnp.zeros((channels, depth), bf16)
     grad[...] = jnp.zeros_like(grad)
 
     def one_row(x, _):
+        slabs = [back_conv[x, y] for y in range(height)]
+        lines = []
+        for b in range(REACH):
+            lines.append(jnp.concatenate([empty] * b + slabs + [empty] * (REACH - 1 - b), 1))
+        stacked = jnp.concatenate(lines, 0)
         total = None
-        for y in range(0, height, 2):
-            slab = jnp.concatenate([back_conv[x, y], back_conv[x, y + 1]], 1)
-            term = by_last(slab, columns(taps, x, y, 2))
+        for y in range(0, height + REACH - 1, 2):
+            term = by_last(stacked[:, y * depth : (y + 2) * depth], columns(taps, x, y, 2))
             total = term if total is None else total + term
         grad[...] += total
         return 0
@@ -245,11 +271,14 @@
     lax.fori_loop(0, rows, one_row, 0)
 
 
-def call(kernel, shapes, *operands, scratch=()):
+def call(kernel, shapes, *operands, scratch=(), micros=2):
     return pl.pallas_call(
         kernel,
         out_shape=[jax.ShapeDtypeStruct(shape, kind) for shape, kind in shapes],
         scratch_shapes=list(scratch),
+        cost_estimate=pl.CostEstimate(
+            flops=micros * 10**9, bytes_accessed=micros * 3 * 10**6, transcendentals=0
+        ),
         compiler_params=pltpu.CompilerParams(vmem_limit_bytes=LIMIT),
     )(*operands)
 
@@ -295,6 +324,11 @@
     mask = jnp.repeat(jnp.repeat(jnp.repeat(occupied, BLOCK, 0), BLOCK, 1), BLOCK, 2)
     gate = mask.astype(bf16)
 
+    split = conv_weight.reshape(channels, REACH, REACH, REACH, channels)
+    stacked_shape = (REACH * channels, REACH * REACH * channels)
+    stacked = split.transpose(2, 0, 1, 3, 4).reshape(stacked_shape)
+    flipped = split[:, ::-1, ::-1, ::-1].transpose(2, 4, 1, 3, 0).reshape(stacked_shape)
+
     x_low, x_high = pass_on(
         features[0] * gate[0][None], features[-1] * gate[-1][None], "drift"
     )
@@ -314,21 +348,21 @@
         [
             (padded, bf16),
             ((rows, channels, plane), f32),
-            ((owners, channels + SPARE, frag_dev), f32),
+            ((owners, channels + SPARE, frag_dev), bf16),
         ],
-        features, x_low, x_high, y_low, y_high, live, owner, local, conv_weight,
+        features, x_low, x_high, y_low, y_high, live, owner, local, stacked, micros=12,
         scratch=[pltpu.VMEM((owners * channels + heads, frag_dev), f32)],
     )
     spread_shape = (owners, channels, frag_dev)
     pooled, divisor = call(
         pool_kernel,
-        [(spread_shape, bf16), ((SPARE, frag_dev), f32)],
+        [(spread_shape, bf16), ((8, frag_dev), f32)],
         exchange(partial, "beam"),
     )
     table = exchange(pooled, "beam")
     fragment_out, back_parts, direct = call(
         fragment_kernel,
-        [((frag_dev, hid), bf16), (spread_shape, f32), ((channels, frag_dev), f32)],
+        [((frag_dev, hid), bf16), (spread_shape, bf16), ((channels, frag_dev), f32)],
         table, pooled[0], embed_weight, message_weight, update_weight, out_cotangent,
         (edge_source // frag_dev).reshape(1, edge_count),
         (edge_source % frag_dev).reshape(1, edge_count),
@@ -340,7 +374,7 @@
     back_hidden, back_conv = call(
         hidden_kernel,
         [((rows, channels, plane), f32), ((rows, height, channels, depth), bf16)],
-        exchange(mean, "beam"), owner, local, live, slopes,
+        exchange(mean, "beam"), owner, local, live, slopes, micros=7,
     )
     gx_low, gx_high = pass_on(back_conv[0], back_conv[-1], "drift")
     ends = [
@@ -348,20 +382,19 @@
         for y in (0, height - 1)
     ]
     gy_low, gy_high = pass_on(ends[0], ends[1], "beam")
-    (local_grad,) = call(weight_kernel, [(conv_weight.shape, f32)], taps, back_conv)
-    taps_count = REACH * REACH * REACH
-    flipped = (
-        conv_weight.reshape(channels, taps_count, channels)[:, ::-1, :]
-        .transpose(2, 1, 0)
-        .reshape(channels, taps_count * channels)
-    )
+    (stacked_grad,) = call(weight_kernel, [(stacked_shape, f32)], taps, back_conv, micros=8)
     (grad_features,) = call(
         backward_kernel,
         [(features.shape, f32)],
-        back_conv, gx_low, gx_high, gy_low, gy_high, back_hidden, live, flipped,
+        back_conv, gx_low, gx_high, gy_low, gy_high, back_hidden, live, flipped, micros=10,
         scratch=[pltpu.VMEM(padded, bf16)],
     )
-    grad_conv = sum_everywhere(local_grad, ("drift", "beam"))
+    grad_conv = (
+        sum_everywhere(stacked_grad, ("drift", "beam"))
+        .reshape(REACH, channels, REACH, REACH, channels)
+        .transpose(1, 2, 0, 3, 4)
+        .reshape(conv_weight.shape)
+    )
     return fragment_out, grad_features, grad_conv
 
 

time: 160 us -> 148 us (0.925)
  Pallas kernels: 53.6 us -> 45 us
  blocking collectives: 39.9 us -> 32.6 us
  starting transfers between devices: 35.6 us -> 40.4 us
  waiting for transfers between devices: 9.93 us -> 7.41 us
  local copies, waits for them, and re-layouts: 14.6 us -> 16.4 us
    pallas_call x7, Pallas kernels: 53.6 us -> 45 us  [call(): pl.pallas_call(kernel, out_shape=[jax.ShapeDtypeStruct(shape, kind) for s...]
    all_to_all x3, blocking collectives: 39.9 us -> 32.6 us  [exchange(): return lax.all_to_all(parts, axes, 0, 0, tiled=True)]
    all_to_all x3, starting transfers between devices: 13.1 us -> 19.4 us  [exchange(): return lax.all_to_all(parts, axes, 0, 0, tiled=True)]
    ppermute x8, waiting for transfers between devices: 5.58 us -> 3.14 us  [pass_on(): return (lax.ppermute(high, axis, up), lax.ppermute(low, axis, down))]
    reshape x2 -> x4, local copies, waits for them, and re-layouts: 1.08 us -> 2.76 us  [the longest x1 0.92 us: body(): grad_conv = sum_everywhere(stacked_grad, ('drift', 'beam')).reshape(REACH...]
  transfers between devices with their start and end apart: 11 -> 11, of which waited for: 4 -> 4; matrix products, arithmetic and copies ran while one was open for 6% -> 8% of each run, Pallas kernels for 7% -> 6%
where the time goes in v2:
time: 148 us; the launch traced here: 146 us
  Pallas kernels  45 us (30%)
  starting transfers between devices  40.4 us (27%)
  blocking collectives  32.6 us (22%)
  local copies, waits for them, and re-layouts  16.4 us (11%)
  waiting for transfers between devices  7.41 us (5%)
  other arithmetic  3.44 us (2%)
    pallas_call x7, Pallas kernels, call(): pl.pallas_call(kernel, out_shape=[jax.ShapeDtypeStruct(shape, kind) for s...  45 us
    all_to_all x3, blocking collectives, exchange(): return lax.all_to_all(parts, axes, 0, 0, tiled=True)  32.6 us
    ppermute x8, starting transfers between devices, pass_on(): return (lax.ppermute(high, axis, up), lax.ppermute(low, axis, down))  21 us
    all_to_all x3, starting transfers between devices, exchange(): return lax.all_to_all(parts, axes, 0, 0, tiled=True)  19.4 us
    all_to_all x3, waiting for transfers between devices, exchange(): return lax.all_to_all(parts, axes, 0, 0, tiled=True)  4.27 us
    ppermute x8, waiting for transfers between devices, pass_on(): return (lax.ppermute(high, axis, up), lax.ppermute(low, axis, down))  3.14 us
  transfers between devices with their start and end apart: 11, of which 4 were waited for; matrix products, arithmetic and copies ran while one was open for 8% of the time, Pallas kernels for 6%

profile of v2, /device:TPU:1, one launch (start us, length us, event | category | flops | bytes accessed | tf_op | source)
XLA Modules:
  0.0 146.3 jit_solution(9599420568072890415)
XLA Ops:
  0.6 0.8 convert_bitcast_fusion
  1.4 0.1 copy.37
  1.5 0.1 copy.38
  1.6 1.0 fusion.9
  2.6 0.1 fusion
  2.6 2.0 %collective-permute-start.1 = (bf16[32,16,128]{2,0,1:T(8,128)(2,1)S(1)}, bf16[32,16,128]{2,0,1:T(8,128)(2,1)S(1)}, u32[]{:S(2)}, u32[]{:S(2)}) collective-permute-start(bf16[32,16,128]{2,0,1:T(8,128)(2,1)S(1)} %get-tuple-element.45), channel_id=1, source_target_pairs={{8,0},{16,8},{24,16},{9,1},{17,9},{25,17},{10,2},{18,10},{26,18},{... | collective-permute-start | bytes 393224 | tf_op jit(solution)/shard_map/ppermute | solution.py:290
  4.6 4.5 %collective-permute-start = (bf16[32,16,128]{2,0,1:T(8,128)(2,1)S(1)}, bf16[32,16,128]{2,0,1:T(8,128)(2,1)S(1)}, u32[]{:S(2)}, u32[]{:S(2)}) collective-permute-start(bf16[32,16,128]{2,0,1:T(8,128)(2,1)S(1)} %get-tuple-element.46), channel_id=1, source_target_pairs={{0,8},{8,16},{16,24},{1,9},{9,17},{17,25},{2,10},{10,18},{18,26},{... | collective-permute-start | bytes 393224 | tf_op jit(solution)/shard_map/ppermute | solution.py:290
  9.1 1.5 fusion.8
  10.6 0.1 broadcast_in_dim.26
  10.6 0.1 slice.85
  10.7 0.1 broadcast_in_dim.25
  10.8 0.1 slice.79
  10.9 1.6 %add_select_fusion = (s32[8,16,128]{2,1,0:T(8,128)}, s32[8,16,128]{2,1,0:T(8,128)}) fusion(s32[8,16,128]{2,1,0:T(8,128)} %param.12), kind=kLoop, calls=%fused_computation.6 | loop fusion | flops 311296 | bytes 196608 | tf_op jit(solution)/shard_map/jit(remainder)/select_n | solution.py:343
  12.5 0.0 collective-permute-done.1
  12.5 0.0 collective-permute-done
  12.6 3.1 %collective-permute-start.2 = (bf16[10,32,128]{2,1,0:T(8,128)(2,1)S(1)}, bf16[10,32,128]{2,1,0:T(8,128)(2,1)S(1)}, u32[]{:S(2)}, u32[]{:S(2)}) collective-permute-start(bf16[10,32,128]{2,1,0:T(8,128)(2,1)S(1)} %pad_maximum_fusion), channel_id=1, source_target_pairs={{0,1},{1,2},{2,3},{3,4},{4,5},{5,6},{6,7},{8,9},{9,10},{10,11},{11... | collective-permute-start | bytes 245768 | tf_op jit(solution)/shard_map/ppermute | solution.py:290
  15.8 1.3 collective-permute-start.3
  17.1 0.1 broadcast_in_dim.28
  17.2 0.1 convert_element_type.40
  17.3 0.2 reshape.74
  17.5 0.1 copy.42
  17.6 0.8 reshape.75.weight
  18.4 0.7 copy.44.x_high
  19.2 0.7 copy.43.x_low
  19.9 0.0 collective-permute-done.2.y_low
  19.9 2.1 %collective-permute-done.3.y_high = bf16[10,32,128]{2,1,0:T(8,128)(2,1)S(1)} collective-permute-done((bf16[10,32,128]{2,1,0:T(8,128)(2,1)S(1)}, bf16[10,32,128]{2,1,0:T(8,128)(2,1)S(1)}, u32[]{:S(2)}, u32[]{:S(2)}) %collective-permute-start.3) | collective-permute-done | bytes 81952 | tf_op jit(solution)/shard_map/ppermute | solution.py:290
  22.0 0.7 broadcast_in_dim.29.mask
  22.7 13.2 %shard_map.121 = (bf16[10,18,96,128]{3,2,1,0:T(8,128)(2,1)}, f32[8,32,2048]{2,1,0:T(8,128)}, bf16[8,48,256]{2,1,0:T(8,128)(2,1)}) custom-call(bf16[8,32,16,128]{3,2,1,0:T(8,128)(2,1)} %feat.1, bf16[32,16,128]{2,1,0:T(8,128)(2,1)} %copy.43.x_low, bf16[32,16,128]{2,1,0:T(8,128)(2,1)} %copy.44.x_high, bf16[10,32,128]{2,1,0:T(8,128)(2,1)} %copy-done.6, ...), custom_call_target="tpu_custom_call" | custom-call | flops 12000000000 | bytes 36000000 | tf_op jit(solution)/shard_map/pallas_call | solution.py:275
  35.9 12.2 %all_to_all.36.parts = bf16[8,48,256]{2,1,0:T(8,128)(2,1)} all-to-all(bf16[8,48,256]{2,1,0:T(8,128)(2,1)} %get-tuple-element.13), channel_id=1, replica_groups=mesh['drift'=4,'beam'=8] {'beam'}, dimensions={0} | all-to-all | bytes 393216 | tf_op jit(solution)/shard_map/all_to_all | solution.py:294
  48.1 1.6 %shard_map.122 = (bf16[8,32,256]{2,1,0:T(8,128)(2,1)}, f32[8,256]{1,0:T(8,128)}) custom-call(bf16[8,48,256]{2,1,0:T(8,128)(2,1)} %all_to_all.36.parts), custom_call_target="tpu_custom_call" | custom-call | flops 2000000000 | bytes 6000000 | tf_op jit(solution)/shard_map/pallas_call | solution.py:275
  49.8 4.2 %all-to-all-start.1 = ((bf16[8,32,256]{2,1,0:T(8,128)(2,1)}), bf16[8,32,256]{2,1,0:T(8,128)(2,1)S(1)}, u32[]{:S(2)}, u32[]{:S(2)}) async-start(bf16[8,32,256]{2,1,0:T(8,128)(2,1)} %get-tuple-element.14), calls=%async_computation.1 | async-start | bytes 262144 | tf_op jit(solution)/shard_map/all_to_all | solution.py:294
  54.0 0.6 add_select_fusion.2
  54.6 1.3 slice_bitcast_fusion.4.mine
  55.9 4.3 %all-to-all-done.1.table = bf16[8,32,256]{2,1,0:T(8,128)(2,1)S(1)} async-done(((bf16[8,32,256]{2,1,0:T(8,128)(2,1)}), bf16[8,32,256]{2,1,0:T(8,128)(2,1)S(1)}, u32[]{:S(2)}, u32[]{:S(2)}) %all-to-all-start.1) | async-done | bytes 131104 | tf_op jit(solution)/shard_map/all_to_all | solution.py:294
  60.1 0.7 copy-done
  60.8 4.2 %shard_map.123 = (bf16[256,256]{1,0:T(8,128)(2,1)}, bf16[8,32,256]{2,1,0:T(8,128)(2,1)}, f32[32,256]{1,0:T(8,128)}) custom-call(bf16[8,32,256]{2,1,0:T(8,128)(2,1)} %copy-done, bf16[32,256]{1,0:T(8,128)(2,1)} %slice_bitcast_fusion.4.mine, bf16[32,256]{1,0:T(8,128)(2,1)} %embed.1, bf16[256,256]{1,0:T(8,128)(2,1)} %message.1, bf16[256,256]{1,0:T(8,128)(2,1)} %update.1, ...), custom_call_target="tpu_custom_call" | custom-call | flops 2000000000 | bytes 6000000 | tf_op jit(solution)/shard_map/pallas_call | solution.py:275
  65.0 10.2 %all_to_all.37.parts = bf16[8,32,256]{2,1,0:T(8,128)(2,1)} all-to-all(bf16[8,32,256]{2,1,0:T(8,128)(2,1)} %get-tuple-element.16), channel_id=1, replica_groups=mesh['drift'=4,'beam'=8] {'beam'}, dimensions={0} | all-to-all | bytes 262144 | tf_op jit(solution)/shard_map/all_to_all | solution.py:294
  75.2 1.6 %shard_map.124 = bf16[8,32,256]{2,1,0:T(8,128)(2,1)} custom-call(bf16[8,32,256]{2,1,0:T(8,128)(2,1)} %all_to_all.37.parts, f32[32,256]{1,0:T(8,128)} %get-tuple-element.17.direct, f32[8,256]{1,0:T(8,128)} %get-tuple-element.18.divisor), custom_call_target="tpu_custom_call" | custom-call | flops 2000000000 | bytes 6000000 | tf_op jit(solution)/shard_map/pallas_call | solution.py:275
  76.8 10.2 %all_to_all.38.table = bf16[8,32,256]{2,1,0:T(8,128)(2,1)} all-to-all(bf16[8,32,256]{2,1,0:T(8,128)(2,1)} %shard_map.124), channel_id=1, replica_groups=mesh['drift'=4,'beam'=8] {'beam'}, dimensions={0} | all-to-all | bytes 262144 | tf_op jit(solution)/shard_map/all_to_all | solution.py:294
  87.0 7.5 %shard_map.125 = (f32[8,32,2048]{2,1,0:T(8,128)}, bf16[8,16,32,128]{3,2,1,0:T(8,128)(2,1)}) custom-call(bf16[8,32,256]{2,1,0:T(8,128)(2,1)} %all_to_all.38.table, s32[8,1,2048]{2,1,0:T(1,128)} %bitcast.62, s32[8,1,2048]{2,1,0:T(1,128)} %bitcast.60, f32[8,1,2048]{2,1,0:T(1,128)} %broadcast_in_dim.29.mask, f32[8,32,2048]{2,1,0:T(8,128)} %get-tuple-element.19.slopes), custom_call_target="tpu_custom_call" | custom-call | flops 7000000000 | bytes 21000000 | tf_op jit(solution)/shard_map/pallas_call | solution.py:275
  94.4 1.0 slice_bitcast_fusion
  95.4 7.9 %shard_map.127 = f32[96,288]{1,0:T(8,128)} custom-call(bf16[10,18,96,128]{3,2,1,0:T(8,128)(2,1)} %get-tuple-element.22.taps, bf16[8,16,32,128]{3,2,1,0:T(8,128)(2,1)} %get-tuple-element.20.back_conv), custom_call_target="tpu_custom_call" | custom-call | flops 8000000000 | bytes 24000000 | tf_op jit(solution)/shard_map/pallas_call | solution.py:275
  103.4 1.7 %all_to_all.29 = f32[32,1,864]{2,1,0:T(1,128)} reshape(f32[96,288]{1,0:T(8,128)} %shard_map.127) | data formatting | bytes 221184 | tf_op jit(solution)/shard_map/all_to_all | solution.py:294
  105.1 7.0 %all-to-all-start.4 = ((f32[32,1,864]{2,1,0:T(1,128)}), f32[32,1,864]{2,1,0:T(1,128)S(1)}, u32[]{:S(2)}, u32[]{:S(2)}) async-start(f32[32,1,864]{2,1,0:T(1,128)} %all_to_all.29), calls=%async_computation.4 | async-start | bytes 229376 | tf_op jit(solution)/shard_map/all_to_all | solution.py:294
  112.1 2.3 %collective-permute-start.5 = (bf16[16,32,128]{2,1,0:T(8,128)(2,1)S(1)}, bf16[16,32,128]{2,1,0:T(8,128)(2,1)S(1)}, u32[]{:S(2)}, u32[]{:S(2)}) collective-permute-start(bf16[16,32,128]{2,1,0:T(8,128)(2,1)S(1)} %get-tuple-element.25), channel_id=1, source_target_pairs={{8,0},{16,8},{24,16},{9,1},{17,9},{25,17},{10,2},{18,10},{26,18},{... | collective-permute-start | bytes 393224 | tf_op jit(solution)/shard_map/ppermute | solution.py:290
  114.4 3.3 %collective-permute-start.4 = (bf16[16,32,128]{2,1,0:T(8,128)(2,1)S(1)}, bf16[16,32,128]{2,1,0:T(8,128)(2,1)S(1)}, u32[]{:S(2)}, u32[]{:S(2)}) collective-permute-start(bf16[16,32,128]{2,1,0:T(8,128)(2,1)S(1)} %get-tuple-element.26), channel_id=1, source_target_pairs={{0,8},{8,16},{16,24},{1,9},{9,17},{17,25},{2,10},{10,18},{18,26},{... | collective-permute-start | bytes 393224 | tf_op jit(solution)/shard_map/ppermute | solution.py:290
  117.7 0.9 slice_bitcast_fusion.2
  118.6 0.5 collective-permute-done.5.x_high
  119.1 0.5 collective-permute-done.4.x_low
  119.7 3.3 %collective-permute-start.6 = (bf16[10,32,128]{2,1,0:T(8,128)(2,1)S(1)}, bf16[10,32,128]{2,1,0:T(8,128)(2,1)S(1)}, u32[]{:S(2)}, u32[]{:S(2)}) collective-permute-start(bf16[10,32,128]{2,1,0:T(8,128)(2,1)S(1)} %pad_maximum_fusion.2), channel_id=1, source_target_pairs={{0,1},{1,2},{2,3},{3,4},{4,5},{5,6},{6,7},{8,9},{9,10},{10,11},{11... | collective-permute-start | bytes 245768 | tf_op jit(solution)/shard_map/ppermute | solution.py:290
  123.0 1.3 collective-permute-start.7
  124.3 0.7 rev.3
  125.0 0.2 copy.47
  125.2 0.8 reshape.79.weight
  126.1 0.1 reduce_sum.9
  126.2 0.7 broadcast_in_dim.30
  126.9 8.2 %all-to-all-start.5 = ((f32[32,1,864]{2,1,0:T(1,128)}), f32[32,1,864]{2,1,0:T(1,128)S(1)}, u32[]{:S(2)}, u32[]{:S(2)}) async-start(f32[32,1,864]{2,1,0:T(1,128)} %broadcast_in_dim.30), calls=%async_computation.5 | async-start | bytes 229376 | tf_op jit(solution)/shard_map/all_to_all | solution.py:294
  135.1 0.6 copy-done.5
  135.7 0.0 copy-done.7
  135.7 8.9 %shard_map.126 = f32[8,32,16,128]{3,2,1,0:T(8,128)} custom-call(bf16[8,16,32,128]{3,2,1,0:T(8,128)(2,1)} %get-tuple-element.20.back_conv, bf16[16,32,128]{2,1,0:T(8,128)(2,1)} %copy-done.4, bf16[16,32,128]{2,1,0:T(8,128)(2,1)} %copy-done.3, bf16[10,32,128]{2,1,0:T(8,128)(2,1)} %copy-done.5, bf16[10,32,128]{2,1,0:T(8,128)(2,1)} %copy-done.7, ...), custom_call_target="tpu_custom_call" | custom-call | flops 10000000000 | bytes 30000000 | tf_op jit(solution)/shard_map/pallas_call | solution.py:275
  144.7 0.3 reduce.1
  144.9 0.3 reshape_reshape_reshape.3
  145.2 0.1 copy.49
  145.4 0.9 reshape.80
  (33 shorter events, 0.2 us)
Async XLA Ops:
  0.6 16.7 %copy-start.1 = (bf16[32,864]{1,0:T(8,128)(2,1)S(1)}, bf16[32,864]{1,0:T(8,128)(2,1)}, u32[]{:S(2)}) copy-start(bf16[32,864]{1,0:T(8,128)(2,1)} %param.13) | copy-start | bytes 165892
  2.6 9.9 %collective-permute-start.1 = (bf16[32,16,128]{2,0,1:T(8,128)(2,1)S(1)}, bf16[32,16,128]{2,0,1:T(8,128)(2,1)S(1)}, u32[]{:S(2)}, u32[]{:S(2)}) collective-permute-start(bf16[32,16,128]{2,0,1:T(8,128)(2,1)S(1)} %get-tuple-element.45), channel_id=1, source_target_pairs={{8,0},{16,8},{24,16},{9,1},{17,9},{25,17},{10,2},{18,10},{26,18},{... | collective-permute-start | bytes 393224 | tf_op jit(solution)/shard_map/ppermute | solution.py:290
  4.6 7.9 %collective-permute-start = (bf16[32,16,128]{2,0,1:T(8,128)(2,1)S(1)}, bf16[32,16,128]{2,0,1:T(8,128)(2,1)S(1)}, u32[]{:S(2)}, u32[]{:S(2)}) collective-permute-start(bf16[32,16,128]{2,0,1:T(8,128)(2,1)S(1)} %get-tuple-element.46), channel_id=1, source_target_pairs={{0,8},{8,16},{16,24},{1,9},{9,17},{17,25},{2,10},{10,18},{18,26},{... | collective-permute-start | bytes 393224 | tf_op jit(solution)/shard_map/ppermute | solution.py:290
  12.6 7.3 %collective-permute-start.2 = (bf16[10,32,128]{2,1,0:T(8,128)(2,1)S(1)}, bf16[10,32,128]{2,1,0:T(8,128)(2,1)S(1)}, u32[]{:S(2)}, u32[]{:S(2)}) collective-permute-start(bf16[10,32,128]{2,1,0:T(8,128)(2,1)S(1)} %pad_maximum_fusion), channel_id=1, source_target_pairs={{0,1},{1,2},{2,3},{3,4},{4,5},{5,6},{6,7},{8,9},{9,10},{10,11},{11... | collective-permute-start | bytes 245768 | tf_op jit(solution)/shard_map/ppermute | solution.py:290
  15.8 6.2 %collective-permute-start.3 = (bf16[10,32,128]{2,1,0:T(8,128)(2,1)S(1)}, bf16[10,32,128]{2,1,0:T(8,128)(2,1)S(1)}, u32[]{:S(2)}, u32[]{:S(2)}) collective-permute-start(bf16[10,32,128]{2,1,0:T(8,128)(2,1)S(1)} %pad_maximum_fusion.1), channel_id=1, source_target_pairs={{1,0},{2,1},{3,2},{4,3},{5,4},{6,5},{7,6},{9,8},{10,9},{11,10},{12... | collective-permute-start | bytes 245768 | tf_op jit(solution)/shard_map/ppermute | solution.py:290
  19.9 2.8 %copy-start.6 = (bf16[10,32,128]{2,1,0:T(8,128)(2,1)}, bf16[10,32,128]{2,1,0:T(8,128)(2,1)S(1)}, u32[]{:S(2)}) copy-start(bf16[10,32,128]{2,1,0:T(8,128)(2,1)S(1)} %collective-permute-done.2.y_low) | copy-start | bytes 245764
  22.0 0.7 copy-start.8
  48.1 5.8 %copy-start.2 = (s32[1024]{0:T(1024)S(1)}, s32[1024]{0:T(1024)}, u32[]{:S(2)}) copy-start(s32[1024]{0:T(1024)} %param.17) | copy-start | bytes 12292
  49.8 10.4 %all-to-all-start.1 = ((bf16[8,32,256]{2,1,0:T(8,128)(2,1)}), bf16[8,32,256]{2,1,0:T(8,128)(2,1)S(1)}, u32[]{:S(2)}, u32[]{:S(2)}) async-start(bf16[8,32,256]{2,1,0:T(8,128)(2,1)} %get-tuple-element.14), calls=%async_computation.1 | async-start | bytes 262144 | tf_op jit(solution)/shard_map/all_to_all | solution.py:294
  60.1 0.7 copy-start
  105.1 20.9 %all-to-all-start.4 = ((f32[32,1,864]{2,1,0:T(1,128)}), f32[32,1,864]{2,1,0:T(1,128)S(1)}, u32[]{:S(2)}, u32[]{:S(2)}) async-start(f32[32,1,864]{2,1,0:T(1,128)} %all_to_all.29), calls=%async_computation.4 | async-start | bytes 229376 | tf_op jit(solution)/shard_map/all_to_all | solution.py:294
  112.1 7.0 %collective-permute-start.5 = (bf16[16,32,128]{2,1,0:T(8,128)(2,1)S(1)}, bf16[16,32,128]{2,1,0:T(8,128)(2,1)S(1)}, u32[]{:S(2)}, u32[]{:S(2)}) collective-permute-start(bf16[16,32,128]{2,1,0:T(8,128)(2,1)S(1)} %get-tuple-element.25), channel_id=1, source_target_pairs={{8,0},{16,8},{24,16},{9,1},{17,9},{25,17},{10,2},{18,10},{26,18},{... | collective-permute-start | bytes 393224 | tf_op jit(solution)/shard_map/ppermute | solution.py:290
  114.4 5.2 %collective-permute-start.4 = (bf16[16,32,128]{2,1,0:T(8,128)(2,1)S(1)}, bf16[16,32,128]{2,1,0:T(8,128)(2,1)S(1)}, u32[]{:S(2)}, u32[]{:S(2)}) collective-permute-start(bf16[16,32,128]{2,1,0:T(8,128)(2,1)S(1)} %get-tuple-element.26), channel_id=1, source_target_pairs={{0,8},{8,16},{16,24},{1,9},{9,17},{17,25},{2,10},{10,18},{18,26},{... | collective-permute-start | bytes 393224 | tf_op jit(solution)/shard_map/ppermute | solution.py:290
  119.1 16.0 %copy-start.3 = (bf16[16,32,128]{2,1,0:T(8,128)(2,1)}, bf16[16,32,128]{2,1,0:T(8,128)(2,1)S(1)}, u32[]{:S(2)}) copy-start(bf16[16,32,128]{2,1,0:T(8,128)(2,1)S(1)} %collective-permute-done.5.x_high) | copy-start | bytes 393220
  119.6 15.5 %copy-start.4 = (bf16[16,32,128]{2,1,0:T(8,128)(2,1)}, bf16[16,32,128]{2,1,0:T(8,128)(2,1)S(1)}, u32[]{:S(2)}) copy-start(bf16[16,32,128]{2,1,0:T(8,128)(2,1)S(1)} %collective-permute-done.4.x_low) | copy-start | bytes 393220
  119.7 15.4 %collective-permute-start.6 = (bf16[10,32,128]{2,1,0:T(8,128)(2,1)S(1)}, bf16[10,32,128]{2,1,0:T(8,128)(2,1)S(1)}, u32[]{:S(2)}, u32[]{:S(2)}) collective-permute-start(bf16[10,32,128]{2,1,0:T(8,128)(2,1)S(1)} %pad_maximum_fusion.2), channel_id=1, source_target_pairs={{0,1},{1,2},{2,3},{3,4},{4,5},{5,6},{6,7},{8,9},{9,10},{10,11},{11... | collective-permute-start | bytes 245768 | tf_op jit(solution)/shard_map/ppermute | solution.py:290
  123.0 12.1 %collective-permute-start.7 = (bf16[10,32,128]{2,1,0:T(8,128)(2,1)S(1)}, bf16[10,32,128]{2,1,0:T(8,128)(2,1)S(1)}, u32[]{:S(2)}, u32[]{:S(2)}) collective-permute-start(bf16[10,32,128]{2,1,0:T(8,128)(2,1)S(1)} %pad_maximum_fusion.3), channel_id=1, source_target_pairs={{1,0},{2,1},{3,2},{4,3},{5,4},{6,5},{7,6},{9,8},{10,9},{11,10},{12... | collective-permute-start | bytes 245768 | tf_op jit(solution)/shard_map/ppermute | solution.py:290
  126.9 17.8 %all-to-all-start.5 = ((f32[32,1,864]{2,1,0:T(1,128)}), f32[32,1,864]{2,1,0:T(1,128)S(1)}, u32[]{:S(2)}, u32[]{:S(2)}) async-start(f32[32,1,864]{2,1,0:T(1,128)} %broadcast_in_dim.30), calls=%async_computation.5 | async-start | bytes 229376 | tf_op jit(solution)/shard_map/all_to_all | solution.py:294
  135.1 0.6 copy-start.5
  135.1 0.6 copy-start.7

commit v3 on v2

--- a/solution.py
+++ b/solution.py
@@ -1,3 +1,5 @@
+import functools
+
 import jax
 import jax.numpy as jnp
 from jax import lax
@@ -8,6 +10,8 @@
 BLOCK = 8
 REACH = 3
 SPARE = 16
+LANES = 128
+SUBLANES = 8
 DIGIT = 128.0
 LIMIT = 56 * 1024 * 1024
 bf16 = jnp.bfloat16
@@ -32,6 +36,21 @@
 
 def slope_of(value, sig):
     return sig * (1.0 + value * (1.0 - sig))
+
+
+def line_of(block):
+    return jnp.concatenate([block[y : y + 1] for y in range(block.shape[0])], 1)
+
+
+def live_line(lanes, row, height):
+    bands = lanes[row // BLOCK]
+    return jnp.concatenate([bands[y // BLOCK : y // BLOCK + 1] for y in range(height)], 1)
+
+
+def owner_and_local(index, size):
+    if size & (size - 1) == 0:
+        return index >> (size.bit_length() - 1), index & (size - 1)
+    return index // size, index % size
 
 
 def one_hot(index, count):
@@ -55,13 +74,35 @@
 def store_taps(taps, row, first, tiles):
     count, channels, depth = tiles.shape
     flat = tiles.reshape(count * channels, depth)
-    lane = lax.broadcasted_iota(jnp.int32, flat.shape, 1)
-    before = jnp.where(lane == 0, 0.0, pltpu.roll(flat, 1, 1))
-    after = jnp.where(lane == depth - 1, 0.0, pltpu.roll(flat, depth - 1, 1))
+    lane = lax.broadcasted_iota(jnp.int32, (1, depth), 1)
+    after_first = jnp.where(lane == 0, 0.0, 1.0).astype(bf16)
+    before_last = jnp.where(lane == depth - 1, 0.0, 1.0).astype(bf16)
+    before = pltpu.roll(flat, 1, 1) * after_first
+    after = pltpu.roll(flat, depth - 1, 1) * before_last
     for place, value in enumerate((before, flat, after)):
         taps[row, first : first + count, place * channels : (place + 1) * channels, :] = (
-            value.reshape(count, channels, depth).astype(bf16)
+            value.reshape(count, channels, depth)
         )
+
+
+def row_copy(source, target, arrived):
+    return lambda x: pltpu.make_async_copy(source.at[x], target.at[x], arrived.at[x])
+
+
+def start_rows(copy, rows):
+    def step(x, _):
+        copy(x).start()
+        return 0
+
+    lax.fori_loop(0, rows, step, 0)
+
+
+def wait_rows(copy, rows):
+    def step(x, _):
+        copy(x).wait()
+        return 0
+
+    lax.fori_loop(0, rows, step, 0)
 
 
 def columns(taps, row, first, count):
@@ -86,7 +127,8 @@
 
 
 def forward_kernel(
-    feat, x_low, x_high, y_low, y_high, mask, owner, local, weight, taps, slopes, partial, total
+    feat, x_low, x_high, y_low, y_high, lanes, fragment, weight, taps_out, slopes_out, partial,
+    taps, slopes, total, taps_sent, slopes_sent
 ):
     rows, channels, height, depth = feat.shape
     owners, _, frag_dev = partial.shape
@@ -94,25 +136,29 @@
     def turned(block):
         return jnp.swapaxes(block.astype(f32), 0, 1)
 
-    store_taps(taps, 0, 1, turned(x_low[...]))
-    store_taps(taps, rows + 1, 1, turned(x_high[...]))
+    send_taps = row_copy(taps, taps_out, taps_sent)
+    send_slopes = row_copy(slopes, slopes_out, slopes_sent)
+
+    store_taps(taps, 0, 1, turned(x_low[...]).astype(bf16))
+    store_taps(taps, rows + 1, 1, turned(x_high[...]).astype(bf16))
 
     def fill(x, _):
         tiles = turned(feat[x])
-        live = mask[x]
+        live = live_line(lanes, x, height)
         gates = [live[:, y * depth : (y + 1) * depth] for y in range(height)]
         gates = jnp.concatenate([jnp.broadcast_to(g, (1, channels, depth)) for g in gates], 0)
-        store_taps(taps, x + 1, 1, tiles * gates)
+        store_taps(taps, x + 1, 1, (tiles * gates).astype(bf16))
         return 0
 
     lax.fori_loop(0, rows, fill, 0)
 
     def edges(x, _):
-        store_taps(taps, x, 0, y_low[x].astype(f32)[None])
-        store_taps(taps, x, height + 1, y_high[x].astype(f32)[None])
+        store_taps(taps, x, 0, y_low[x][None])
+        store_taps(taps, x, height + 1, y_high[x][None])
         return 0
 
     lax.fori_loop(0, rows + 2, edges, 0)
+    start_rows(send_taps, rows + 2)
     total[...] = jnp.zeros_like(total)
 
     def one_row(x, _):
@@ -120,14 +166,16 @@
         active = jnp.concatenate(
             [taps[x + 1, y + 1, channels : 2 * channels, :] for y in range(height)], 1
         )
-        live = mask[x]
+        live = live_line(lanes, x, height)
+        owner, local = owner_and_local(line_of(fragment[x]), frag_dev)
         sig = jax.nn.sigmoid(conv)
         hidden = live * (active.astype(f32) + conv * sig)
-        slopes[x] = live * slope_of(conv, sig)
+        slopes[x] = (live * slope_of(conv, sig)).astype(bf16)
+        send_slopes(x).start()
         tallies = lax.broadcasted_iota(jnp.int32, (total.shape[0] - owners * channels, 1), 0)
-        heads = jnp.where(tallies == owner[x], live, 0.0).astype(bf16)
-        rising = jnp.concatenate([spread(hidden, owner[x], owners), heads], 0)
-        total[...] += by_last(rising, one_hot(local[x], frag_dev))
+        heads = jnp.where(tallies == owner, live, 0.0).astype(bf16)
+        rising = jnp.concatenate([spread(hidden, owner, owners), heads], 0)
+        total[...] += by_last(rising, one_hot(local, frag_dev))
         return 0
 
     lax.fori_loop(0, rows, one_row, 0)
@@ -144,6 +192,8 @@
             if DIGIT ** (d + 1) > rows * height * depth:
                 break
         partial[h, channels:] = digits.astype(bf16)
+    wait_rows(send_taps, rows + 2)
+    wait_rows(send_slopes, rows)
 
 
 def pool_kernel(parts, pooled, divisor):
@@ -164,12 +214,13 @@
 
 
 def fragment_kernel(
-    table, mine, embed, message, update, cotangent, owner, local, target, out, partial, direct
+    table, mine, embed, message, update, cotangent, edge_from, target, out, partial, direct
 ):
     owners, channels, frag_dev = table.shape
     flat = table[...].reshape(owners * channels, frag_dev)
-    from_local = one_hot(local[...], frag_dev)
-    source = pick(plain(flat, from_local), owner[...], owners).astype(bf16)
+    owner, local = owner_and_local(edge_from[...], frag_dev)
+    from_local = one_hot(local, frag_dev)
+    source = pick(plain(flat, from_local), owner, owners).astype(bf16)
     pre_source = by_first(source, embed[...])
     sig_source = jax.nn.sigmoid(pre_source)
     own_source = (pre_source * sig_source).astype(bf16)
@@ -187,7 +238,7 @@
     back_pre = (back_edge * slope_of(pre_msg, sig_msg)).astype(bf16)
     back_source = by_last(back_pre, message[...]) * slope_of(pre_source, sig_source)
     back_pooled = by_last(embed[...], back_source.astype(bf16))
-    scattered = by_last(spread(back_pooled, owner[...], owners), from_local)
+    scattered = by_last(spread(back_pooled, owner, owners), from_local)
     partial[...] = scattered.reshape(partial.shape).astype(partial.dtype)
     near = cotangent[...].astype(f32) * slope_of(pre_own, sig_own)
     rough = near.astype(bf16)
@@ -204,29 +255,51 @@
         mean[h] = result
 
 
-def hidden_kernel(table, owner, local, mask, slopes, back_hidden, back_conv):
+def hidden_kernel(
+    table, fragment, lanes, slopes_in, hidden_out, conv_out,
+    slopes, back_hidden, back_conv, slopes_here, hidden_sent, conv_sent
+):
     owners, channels, frag_dev = table.shape
     rows, height, _, depth = back_conv.shape
     flat = table[...].reshape(owners * channels, frag_dev)
+    fetch = row_copy(slopes_in, slopes, slopes_here)
+    send_hidden = row_copy(back_hidden, hidden_out, hidden_sent)
+    send_conv = row_copy(back_conv, conv_out, conv_sent)
+    start_rows(fetch, rows)
 
     def one_row(x, _):
-        found = plain(flat, one_hot(local[x], frag_dev))
-        hidden = pick(found, owner[x], owners)
-        back_hidden[x] = mask[x] * hidden
-        grad = (hidden * slopes[x]).astype(bf16)
+        owner, local = owner_and_local(line_of(fragment[x]), frag_dev)
+        found = plain(flat, one_hot(local, frag_dev))
+        hidden = pick(found, owner, owners)
+        back_hidden[x] = (live_line(lanes, x, height) * hidden).astype(bf16)
+        send_hidden(x).start()
+        fetch(x).wait()
+        grad = (hidden * slopes[x].astype(f32)).astype(bf16)
         for y in range(height):
             back_conv[x, y] = grad[:, y * depth : (y + 1) * depth]
+        send_conv(x).start()
         return 0
 
     lax.fori_loop(0, rows, one_row, 0)
-
-
-def weight_kernel(taps, back_conv, grad):
+    wait_rows(send_hidden, rows)
+    wait_rows(send_conv, rows)
+
+
+def weight_kernel(taps, back_conv, packed, grad, near, arrived):
     rows, height, channels, depth = back_conv.shape
     empty = jnp.zeros((channels, depth), bf16)
     grad[...] = jnp.zeros_like(grad)
 
+    def fetch(x):
+        return pltpu.make_async_copy(taps.at[x], near.at[x], arrived.at[x])
+
+    for x in range(rows + REACH - 1):
+        fetch(x).start()
+    for x in range(REACH - 1):
+        fetch(x).wait()
+
     def one_row(x, _):
+        fetch(x + REACH - 1).wait()
         slabs = [back_conv[x, y] for y in range(height)]
         lines = []
         for b in range(REACH):
@@ -234,51 +307,110 @@
         stacked = jnp.concatenate(lines, 0)
         total = None
         for y in range(0, height + REACH - 1, 2):
-            term = by_last(stacked[:, y * depth : (y + 2) * depth], columns(taps, x, y, 2))
+            term = by_last(stacked[:, y * depth : (y + 2) * depth], columns(near, x, y, 2))
             total = term if total is None else total + term
         grad[...] += total
         return 0
 
     lax.fori_loop(0, rows, one_row, 0)
+    packed[...] = jnp.zeros_like(packed)
+    for place, part in packed_parts(grad.shape):
+        height = part[0].stop - part[0].start
+        width = part[1].stop - part[1].start
+        packed[place[0] : place[0] + height, place[1] : place[1] + width] = grad[part]
+
+
+def packed_parts(shape):
+    height, width = shape
+    full = width // LANES * LANES
+    rest = width - full
+    parts = []
+    for left in range(0, full, LANES):
+        parts.append(((left // LANES * height, 0), (slice(0, height), slice(left, left + LANES))))
+    if rest:
+        folds = LANES // rest
+        step = height // folds
+        for k in range(folds):
+            source = (slice(k * step, (k + 1) * step), slice(full, width))
+            parts.append(((full // LANES * height, k * rest), source))
+    return parts
+
+
+def unpack(packed, shape):
+    height, width = shape
+    full = width // LANES * LANES
+    rest = width - full
+    blocks = [packed[left // LANES * height :][:height] for left in range(0, full, LANES)]
+    if rest:
+        folds = LANES // rest
+        step = height // folds
+        tail = packed[full // LANES * height :][:step]
+        blocks.append(tail.reshape(step, folds, rest).swapaxes(0, 1).reshape(height, rest))
+    return jnp.concatenate(blocks, 1)
+
+
+def weight_call(taps, back_conv, shape, lines):
+    whole = pl.BlockSpec(memory_space=pltpu.VMEM)
+    return pl.pallas_call(
+        weight_kernel,
+        in_specs=[pl.BlockSpec(memory_space=pl.ANY), whole],
+        out_specs=whole,
+        out_shape=jax.ShapeDtypeStruct((lines, LANES), f32),
+        scratch_shapes=[pltpu.VMEM(shape, f32), pltpu.VMEM(taps.shape, bf16), pltpu.SemaphoreType.DMA((taps.shape[0],))],
+        cost_estimate=cost(8),
+        compiler_params=pltpu.CompilerParams(vmem_limit_bytes=LIMIT),
+    )(taps, back_conv)
 
 
 def backward_kernel(
-    back_conv, x_low, x_high, y_low, y_high, back_hidden, mask, weight, grad, taps
+    back_conv, x_low, x_high, y_low, y_high, back_hidden, lanes, weight, grad_out,
+    grad, taps, sent
 ):
     rows, height, channels, depth = back_conv.shape
-    store_taps(taps, 0, 1, x_low[...].astype(f32))
-    store_taps(taps, rows + 1, 1, x_high[...].astype(f32))
+    send = row_copy(grad, grad_out, sent)
+    store_taps(taps, 0, 1, x_low[...])
+    store_taps(taps, rows + 1, 1, x_high[...])
 
     def fill(x, _):
-        store_taps(taps, x + 1, 1, back_conv[x].astype(f32))
+        store_taps(taps, x + 1, 1, back_conv[x])
         return 0
 
     lax.fori_loop(0, rows, fill, 0)
 
     def edges(x, _):
-        store_taps(taps, x, 0, y_low[x].astype(f32)[None])
-        store_taps(taps, x, height + 1, y_high[x].astype(f32)[None])
-        return 0
-
-    lax.fori_loop(0, rows + 2, edges, 0)
+        store_taps(taps, x, 0, y_low[x][None])
+        store_taps(taps, x, height + 1, y_high[x][None])
+        return 0
+
+    lax.fori_loop(0, rows + REACH - 1, edges, 0)
 
     def one_row(x, _):
-        result = mask[x] * (back_hidden[x] + convolve_row(taps, weight[...], x, height))
+        live = live_line(lanes, x, height)
+        result = live * (back_hidden[x].astype(f32) + convolve_row(taps, weight[...], x, height))
         tiles = [result[:, y * depth : (y + 1) * depth][None] for y in range(height)]
         grad[x] = jnp.swapaxes(jnp.concatenate(tiles, 0), 0, 1)
+        send(x).start()
         return 0
 
     lax.fori_loop(0, rows, one_row, 0)
-
-
-def call(kernel, shapes, *operands, scratch=(), micros=2):
+    wait_rows(send, rows)
+
+
+def cost(micros):
+    return pl.CostEstimate(
+        flops=micros * 10**9, bytes_accessed=micros * 3 * 10**6, transcendentals=0
+    )
+
+
+def call(kernel, shapes, *operands, scratch=(), micros=2, far_in=(), far_out=()):
+    here, there = pl.BlockSpec(memory_space=pltpu.VMEM), pl.BlockSpec(memory_space=pl.ANY)
     return pl.pallas_call(
         kernel,
+        in_specs=[there if i in far_in else here for i in range(len(operands))],
+        out_specs=[there if i in far_out else here for i in range(len(shapes))],
         out_shape=[jax.ShapeDtypeStruct(shape, kind) for shape, kind in shapes],
         scratch_shapes=list(scratch),
-        cost_estimate=pl.CostEstimate(
-            flops=micros * 10**9, bytes_accessed=micros * 3 * 10**6, transcendentals=0
-        ),
+        cost_estimate=cost(micros),
         compiler_params=pltpu.CompilerParams(vmem_limit_bytes=LIMIT),
     )(*operands)
 
@@ -292,16 +424,6 @@
 
 def exchange(parts, axes):
     return lax.all_to_all(parts, axes, 0, 0, tiled=True)
-
-
-def sum_everywhere(values, axes):
-    count = lax.axis_size(axes)
-    flat = values.reshape(-1)
-    share = -(-flat.shape[0] // count)
-    flat = jnp.pad(flat, (0, share * count - flat.shape[0])).reshape(count, share)
-    mine = exchange(flat, axes).sum(0)
-    back = exchange(jnp.broadcast_to(mine[None], flat.shape), axes)
-    return back.reshape(-1)[: values.size].reshape(values.shape)
 
 
 def body(
@@ -321,8 +443,8 @@
     owners = lax.axis_size("beam")
     edge_count = edge_source.shape[0]
     plane = height * depth
-    mask = jnp.repeat(jnp.repeat(jnp.repeat(occupied, BLOCK, 0), BLOCK, 1), BLOCK, 2)
-    gate = mask.astype(bf16)
+    lanes = jnp.repeat(occupied, BLOCK, 2).astype(f32)
+    gate = jnp.repeat(jnp.repeat(lanes, BLOCK, 0), BLOCK, 1).astype(bf16)
 
     split = conv_weight.reshape(channels, REACH, REACH, REACH, channels)
     stacked_shape = (REACH * channels, REACH * REACH * channels)
@@ -338,20 +460,24 @@
         ends.append(jnp.concatenate([x_low[None, :, y], side, x_high[None, :, y]], 0))
     y_low, y_high = pass_on(ends[0], ends[1], "beam")
 
-    live = mask.astype(f32).reshape(rows, 1, plane)
-    owner = (voxel_fragment // frag_dev).reshape(rows, 1, plane)
-    local = (voxel_fragment % frag_dev).reshape(rows, 1, plane)
     heads = -(-owners // 16) * 16
+    line_shape = (rows, channels, plane)
+    conv_shape = (rows, height, channels, depth)
+    dma = lambda count: pltpu.SemaphoreType.DMA((count,))
     padded = (rows + 2, height + 2, REACH * channels, depth)
     taps, slopes, partial = call(
         forward_kernel,
         [
             (padded, bf16),
-            ((rows, channels, plane), f32),
+            (line_shape, bf16),
             ((owners, channels + SPARE, frag_dev), bf16),
         ],
-        features, x_low, x_high, y_low, y_high, live, owner, local, stacked, micros=12,
-        scratch=[pltpu.VMEM((owners * channels + heads, frag_dev), f32)],
+        features, x_low, x_high, y_low, y_high, lanes, voxel_fragment, stacked, micros=12,
+        scratch=[
+            pltpu.VMEM(padded, bf16), pltpu.VMEM(line_shape, bf16),
+            pltpu.VMEM((owners * channels + heads, frag_dev), f32), dma(rows + 2), dma(rows),
+        ],
+        far_out=(0, 1),
     )
     spread_shape = (owners, channels, frag_dev)
     pooled, divisor = call(
@@ -364,8 +490,7 @@
         fragment_kernel,
         [((frag_dev, hid), bf16), (spread_shape, bf16), ((channels, frag_dev), f32)],
         table, pooled[0], embed_weight, message_weight, update_weight, out_cotangent,
-        (edge_source // frag_dev).reshape(1, edge_count),
-        (edge_source % frag_dev).reshape(1, edge_count),
+        edge_source.reshape(1, edge_count),
         edge_target.reshape(1, edge_count),
     )
     (mean,) = call(
@@ -373,24 +498,36 @@
     )
     back_hidden, back_conv = call(
         hidden_kernel,
-        [((rows, channels, plane), f32), ((rows, height, channels, depth), bf16)],
-        exchange(mean, "beam"), owner, local, live, slopes, micros=7,
+        [(line_shape, bf16), (conv_shape, bf16)],
+        exchange(mean, "beam"), voxel_fragment, lanes, slopes, micros=7,
+        scratch=[
+            pltpu.VMEM(line_shape, bf16), pltpu.VMEM(line_shape, bf16),
+            pltpu.VMEM(conv_shape, bf16), dma(rows), dma(rows), dma(rows),
+        ],
+        far_in=(3,), far_out=(0, 1),
     )
     gx_low, gx_high = pass_on(back_conv[0], back_conv[-1], "drift")
+    everyone = ("drift", "beam")
+    devices = lax.axis_size(everyone)
+    tile = SUBLANES * LANES
+    share = -(-conv_weight.size // (devices * tile)) * SUBLANES
+    packed = weight_call(taps, back_conv, stacked_shape, devices * share)
     ends = [
         jnp.concatenate([gx_low[None, y], back_conv[:, y], gx_high[None, y]], 0)
         for y in (0, height - 1)
     ]
     gy_low, gy_high = pass_on(ends[0], ends[1], "beam")
-    (stacked_grad,) = call(weight_kernel, [(stacked_shape, f32)], taps, back_conv, micros=8)
     (grad_features,) = call(
         backward_kernel,
         [(features.shape, f32)],
-        back_conv, gx_low, gx_high, gy_low, gy_high, back_hidden, live, flipped, micros=10,
-        scratch=[pltpu.VMEM(padded, bf16)],
-    )
+        back_conv, gx_low, gx_high, gy_low, gy_high, back_hidden, lanes, flipped, micros=10,
+        scratch=[pltpu.VMEM(features.shape, f32), pltpu.VMEM(padded, bf16), dma(rows)],
+        far_out=(0,),
+    )
+    parts = exchange(packed, everyone).reshape(devices, share, LANES)
+    full = exchange(jnp.broadcast_to(parts.sum(0)[None], parts.shape), everyone)
     grad_conv = (
-        sum_everywhere(stacked_grad, ("drift", "beam"))
+        unpack(full.reshape(devices * share, LANES), stacked_shape)
         .reshape(REACH, channels, REACH, REACH, channels)
         .transpose(1, 2, 0, 3, 4)
         .reshape(conv_weight.shape)

time: 148 us -> 143 us (0.966)
  other arithmetic: 3.44 us -> 0.88 us
  Pallas kernels: 45 us -> 42.6 us
  blocking collectives: 32.6 us -> 34.6 us
    pallas_call x7, Pallas kernels: 45 us -> 42.6 us  [the longest x6 34.5 us: call(): pl.pallas_call(kernel, in_specs=[there if i in far_in else here for i in...]
    select_n x2 -> x0, other arithmetic: 2.18 us -> none  [the longest x1 1.57 us: body(): local = (voxel_fragment % frag_dev).reshape(rows, 1, plane)]
    all_to_all x3, blocking collectives: 32.6 us -> 34.6 us  [exchange(): return lax.all_to_all(parts, axes, 0, 0, tiled=True)]
    all_to_all x1 -> x0, local copies, waits for them, and re-layouts: 1.74 us -> none  [exchange(): return lax.all_to_all(parts, axes, 0, 0, tiled=True)]
  transfers between devices with their start and end apart: 11 -> 11, of which waited for: 4 -> 5; matrix products, arithmetic and copies ran while one was open for 8% -> 7% of each run, Pallas kernels for 6% -> 6%
where the time goes in v3:
time: 143 us; the launch traced here: 142 us
  Pallas kernels  42.6 us (30%)
  starting transfers between devices  40.2 us (28%)
  blocking collectives  34.6 us (24%)
  local copies, waits for them, and re-layouts  15.8 us (11%)
  waiting for transfers between devices  6.8 us (5%)
    all_to_all x3, blocking collectives, exchange(): return lax.all_to_all(parts, axes, 0, 0, tiled=True)  34.6 us
    pallas_call x6, Pallas kernels, call(): pl.pallas_call(kernel, in_specs=[there if i in far_in else here for i in...  34.5 us
    ppermute x8, starting transfers between devices, pass_on(): return (lax.ppermute(high, axis, up), lax.ppermute(low, axis, down))  21 us
    all_to_all x3, starting transfers between devices, exchange(): return lax.all_to_all(parts, axes, 0, 0, tiled=True)  19.2 us
    pallas_call x1, Pallas kernels, weight_call(): pl.pallas_call(weight_kernel, in_specs=[pl.BlockSpec(memory_space=pl.ANY)...  8.04 us
    all_to_all x3, waiting for transfers between devices, exchange(): return lax.all_to_all(parts, axes, 0, 0, tiled=True)  4.9 us
  transfers between devices with their start and end apart: 11, of which 5 were waited for; matrix products, arithmetic and copies ran while one was open for 7% of the time, Pallas kernels for 6%

profile of v3, /device:TPU:1, one launch (start us, length us, event | category | flops | bytes accessed | tf_op | source)
XLA Modules:
  0.0 141.9 jit_solution(14062637394394377636)
XLA Ops:
  0.6 0.7 convert_bitcast_fusion
  1.3 0.1 broadcast_in_dim.15
  1.4 0.1 convert_element_type.25
  1.5 1.0 fusion.6
  2.5 0.1 fusion
  2.6 2.0 %collective-permute-start.1 = (bf16[32,16,128]{2,0,1:T(8,128)(2,1)S(1)}, bf16[32,16,128]{2,0,1:T(8,128)(2,1)S(1)}, u32[]{:S(2)}, u32[]{:S(2)}) collective-permute-start(bf16[32,16,128]{2,0,1:T(8,128)(2,1)S(1)} %get-tuple-element.43), channel_id=1, source_target_pairs={{8,0},{16,8},{24,16},{9,1},{17,9},{25,17},{10,2},{18,10},{26,18},{... | collective-permute-start | bytes 393224 | tf_op jit(solution)/shard_map/ppermute | solution.py:422
  4.5 4.5 %collective-permute-start = (bf16[32,16,128]{2,0,1:T(8,128)(2,1)S(1)}, bf16[32,16,128]{2,0,1:T(8,128)(2,1)S(1)}, u32[]{:S(2)}, u32[]{:S(2)}) collective-permute-start(bf16[32,16,128]{2,0,1:T(8,128)(2,1)S(1)} %get-tuple-element.44), channel_id=1, source_target_pairs={{0,8},{8,16},{16,24},{1,9},{9,17},{17,25},{2,10},{10,18},{18,26},{... | collective-permute-start | bytes 393224 | tf_op jit(solution)/shard_map/ppermute | solution.py:422
  9.0 1.5 %fusion.5 = (bf16[8,32,1,128]{3,2,1,0:T(2,128)(2,1)S(1)}, bf16[8,32,1,128]{3,2,1,0:T(2,128)(2,1)S(1)}) fusion(bf16[8,32,16,128]{3,2,1,0:T(8,128)(2,1)} %feat.1), kind=kLoop, calls=%fused_computation.30 | loop fusion | bytes 262144 | tf_op jit(solution)/shard_map/slice | solution.py:459
  10.5 0.0 collective-permute-done.1
  10.5 0.4 collective-permute-done
  10.9 3.1 %collective-permute-start.2 = (bf16[10,32,128]{2,1,0:T(8,128)(2,1)S(1)}, bf16[10,32,128]{2,1,0:T(8,128)(2,1)S(1)}, u32[]{:S(2)}, u32[]{:S(2)}) collective-permute-start(bf16[10,32,128]{2,1,0:T(8,128)(2,1)S(1)} %pad_maximum_fusion.1), channel_id=1, source_target_pairs={{0,1},{1,2},{2,3},{3,4},{4,5},{5,6},{6,7},{8,9},{9,10},{10,11},{11... | collective-permute-start | bytes 245768 | tf_op jit(solution)/shard_map/ppermute | solution.py:422
  14.1 1.3 collective-permute-start.3
  15.4 0.1 broadcast_in_dim.17
  15.5 0.7 convert_element_type.28.lanes
  16.2 1.0 reshape.77
  17.2 0.1 copy.39
  17.3 0.8 reshape.78.weight
  18.1 0.7 copy.41.x_high
  18.9 0.7 copy.40.x_low
  19.6 0.0 collective-permute-done.2.y_low
  19.6 0.5 collective-permute-done.3.y_high
  20.0 0.2 copy-done.5
  20.2 0.6 copy-done.6
  20.8 12.5 %shard_map.121 = (bf16[10,18,96,128]{3,2,1,0:T(8,128)(2,1)}, bf16[8,32,2048]{2,1,0:T(8,128)(2,1)}, bf16[8,48,256]{2,1,0:T(8,128)(2,1)}) custom-call(bf16[8,32,16,128]{3,2,1,0:T(8,128)(2,1)} %feat.1, bf16[32,16,128]{2,1,0:T(8,128)(2,1)} %copy.40.x_low, bf16[32,16,128]{2,1,0:T(8,128)(2,1)} %copy.41.x_high, bf16[10,32,128]{2,1,0:T(8,128)(2,1)} %copy-done.5, ...), custom_call_target="tpu_custom_call" | custom-call | flops 12000000000 | bytes 36000000 | tf_op jit(solution)/shard_map/pallas_call | solution.py:407
  33.4 14.1 %all_to_all.34.parts = bf16[8,48,256]{2,1,0:T(8,128)(2,1)} all-to-all(bf16[8,48,256]{2,1,0:T(8,128)(2,1)} %get-tuple-element.13), channel_id=1, replica_groups=mesh['drift'=4,'beam'=8] {'beam'}, dimensions={0} | all-to-all | bytes 393216 | tf_op jit(solution)/shard_map/all_to_all | solution.py:426
  47.5 1.6 %shard_map.122 = (bf16[8,32,256]{2,1,0:T(8,128)(2,1)}, f32[8,256]{1,0:T(8,128)}) custom-call(bf16[8,48,256]{2,1,0:T(8,128)(2,1)} %all_to_all.34.parts), custom_call_target="tpu_custom_call" | custom-call | flops 2000000000 | bytes 6000000 | tf_op jit(solution)/shard_map/pallas_call | solution.py:407
  49.1 3.7 %all-to-all-start.1 = ((bf16[8,32,256]{2,1,0:T(8,128)(2,1)}), bf16[8,32,256]{2,1,0:T(8,128)(2,1)S(1)}, u32[]{:S(2)}, u32[]{:S(2)}) async-start(bf16[8,32,256]{2,1,0:T(8,128)(2,1)} %get-tuple-element.14), calls=%async_computation.1 | async-start | bytes 262144 | tf_op jit(solution)/shard_map/all_to_all | solution.py:426
  52.9 1.3 slice_bitcast_fusion.6.mine
  54.2 4.9 %all-to-all-done.1.table = bf16[8,32,256]{2,1,0:T(8,128)(2,1)S(1)} async-done(((bf16[8,32,256]{2,1,0:T(8,128)(2,1)}), bf16[8,32,256]{2,1,0:T(8,128)(2,1)S(1)}, u32[]{:S(2)}, u32[]{:S(2)}) %all-to-all-start.1) | async-done | bytes 131104 | tf_op jit(solution)/shard_map/all_to_all | solution.py:426
  59.1 0.7 copy-done
  59.7 4.2 %shard_map.123 = (bf16[256,256]{1,0:T(8,128)(2,1)}, bf16[8,32,256]{2,1,0:T(8,128)(2,1)}, f32[32,256]{1,0:T(8,128)}) custom-call(bf16[8,32,256]{2,1,0:T(8,128)(2,1)} %copy-done, bf16[32,256]{1,0:T(8,128)(2,1)} %slice_bitcast_fusion.6.mine, bf16[32,256]{1,0:T(8,128)(2,1)} %embed.1, bf16[256,256]{1,0:T(8,128)(2,1)} %message.1, bf16[256,256]{1,0:T(8,128)(2,1)} %update.1, ...), custom_call_target="tpu_custom_call" | custom-call | flops 2000000000 | bytes 6000000 | tf_op jit(solution)/shard_map/pallas_call | solution.py:407
  64.0 10.3 %all_to_all.35.parts = bf16[8,32,256]{2,1,0:T(8,128)(2,1)} all-to-all(bf16[8,32,256]{2,1,0:T(8,128)(2,1)} %get-tuple-element.16), channel_id=1, replica_groups=mesh['drift'=4,'beam'=8] {'beam'}, dimensions={0} | all-to-all | bytes 262144 | tf_op jit(solution)/shard_map/all_to_all | solution.py:426
  74.2 1.6 %shard_map.124 = bf16[8,32,256]{2,1,0:T(8,128)(2,1)} custom-call(bf16[8,32,256]{2,1,0:T(8,128)(2,1)} %all_to_all.35.parts, f32[32,256]{1,0:T(8,128)} %get-tuple-element.17.direct, f32[8,256]{1,0:T(8,128)} %get-tuple-element.18.divisor), custom_call_target="tpu_custom_call" | custom-call | flops 2000000000 | bytes 6000000 | tf_op jit(solution)/shard_map/pallas_call | solution.py:407
  75.9 10.2 %all_to_all.36.table = bf16[8,32,256]{2,1,0:T(8,128)(2,1)} all-to-all(bf16[8,32,256]{2,1,0:T(8,128)(2,1)} %shard_map.124), channel_id=1, replica_groups=mesh['drift'=4,'beam'=8] {'beam'}, dimensions={0} | all-to-all | bytes 262144 | tf_op jit(solution)/shard_map/all_to_all | solution.py:426
  86.0 6.5 %shard_map.125 = (bf16[8,32,2048]{2,1,0:T(8,128)(2,1)}, bf16[8,16,32,128]{3,2,1,0:T(8,128)(2,1)}) custom-call(bf16[8,32,256]{2,1,0:T(8,128)(2,1)} %all_to_all.36.table, s32[8,16,128]{2,1,0:T(8,128)} %fragment.3, f32[1,2,128]{2,1,0:T(2,128)} %convert_element_type.28.lanes, bf16[8,32,2048]{2,1,0:T(8,128)(2,1)} %get-tuple-element.19.slopes_in), custom_call_target="tpu_custom_call" | custom-call | flops 7000000000 | bytes 21000000 | tf_op jit(solution)/shard_map/pallas_call | solution.py:407
  92.6 1.0 slice_bitcast_fusion
  93.5 8.0 %shard_map.127 = f32[256,128]{1,0:T(8,128)} custom-call(bf16[10,18,96,128]{3,2,1,0:T(8,128)(2,1)} %get-tuple-element.22.taps, bf16[8,16,32,128]{3,2,1,0:T(8,128)(2,1)} %get-tuple-element.20.back_conv), custom_call_target="tpu_custom_call" | custom-call | flops 8000000000 | bytes 24000000 | tf_op jit(solution)/shard_map/pallas_call | solution.py:354
  101.6 7.4 %all-to-all-start.4 = ((f32[32,8,128]{2,1,0:T(8,128)}), f32[32,8,128]{2,1,0:T(8,128)S(1)}, u32[]{:S(2)}, u32[]{:S(2)}) async-start(f32[32,8,128]{2,1,0:T(8,128)} %bitcast.61), calls=%async_computation.4 | async-start | bytes 262144 | tf_op jit(solution)/shard_map/all_to_all | solution.py:426
  109.0 2.2 %collective-permute-start.5 = (bf16[16,32,128]{2,1,0:T(8,128)(2,1)S(1)}, bf16[16,32,128]{2,1,0:T(8,128)(2,1)S(1)}, u32[]{:S(2)}, u32[]{:S(2)}) collective-permute-start(bf16[16,32,128]{2,1,0:T(8,128)(2,1)S(1)} %get-tuple-element.25), channel_id=1, source_target_pairs={{8,0},{16,8},{24,16},{9,1},{17,9},{25,17},{10,2},{18,10},{26,18},{... | collective-permute-start | bytes 393224 | tf_op jit(solution)/shard_map/ppermute | solution.py:422
  111.2 3.4 %collective-permute-start.4 = (bf16[16,32,128]{2,1,0:T(8,128)(2,1)S(1)}, bf16[16,32,128]{2,1,0:T(8,128)(2,1)S(1)}, u32[]{:S(2)}, u32[]{:S(2)}) collective-permute-start(bf16[16,32,128]{2,1,0:T(8,128)(2,1)S(1)} %get-tuple-element.26), channel_id=1, source_target_pairs={{0,8},{8,16},{16,24},{1,9},{9,17},{17,25},{2,10},{10,18},{18,26},{... | collective-permute-start | bytes 393224 | tf_op jit(solution)/shard_map/ppermute | solution.py:422
  114.6 0.9 slice_bitcast_fusion.2
  115.5 0.6 collective-permute-done.5.x_high
  116.0 0.5 collective-permute-done.4.x_low
  116.5 3.3 %collective-permute-start.6 = (bf16[10,32,128]{2,1,0:T(8,128)(2,1)S(1)}, bf16[10,32,128]{2,1,0:T(8,128)(2,1)S(1)}, u32[]{:S(2)}, u32[]{:S(2)}) collective-permute-start(bf16[10,32,128]{2,1,0:T(8,128)(2,1)S(1)} %pad_maximum_fusion.3), channel_id=1, source_target_pairs={{0,1},{1,2},{2,3},{3,4},{4,5},{5,6},{6,7},{8,9},{9,10},{10,11},{11... | collective-permute-start | bytes 245768 | tf_op jit(solution)/shard_map/ppermute | solution.py:422
  119.8 1.3 collective-permute-start.7
  121.1 0.7 rev.3
  121.8 0.2 copy.44
  122.1 0.8 reshape.81.weight
  122.9 0.0 all-to-all-done.4
  123.0 0.7 broadcast_in_dim.18
  123.6 8.1 %all-to-all-start.5 = ((f32[32,8,128]{2,1,0:T(8,128)}), f32[32,8,128]{2,1,0:T(8,128)S(1)}, u32[]{:S(2)}, u32[]{:S(2)}) async-start(f32[32,8,128]{2,1,0:T(8,128)} %broadcast_in_dim.18), calls=%async_computation.5 | async-start | bytes 262144 | tf_op jit(solution)/shard_map/all_to_all | solution.py:426
  131.7 0.0 collective-permute-done.6.y_low
  131.7 0.0 copy-start.3
  131.7 0.0 collective-permute-done.7.y_high
  131.8 0.0 copy-start.4
  131.8 0.0 copy-done.1
  131.8 0.6 copy-done.3
  132.4 0.0 copy-done.4
  132.4 8.0 %shard_map.126 = f32[8,32,16,128]{3,2,1,0:T(8,128)} custom-call(bf16[8,16,32,128]{3,2,1,0:T(8,128)(2,1)} %get-tuple-element.20.back_conv, bf16[16,32,128]{2,1,0:T(8,128)(2,1)} %copy-done.2, bf16[16,32,128]{2,1,0:T(8,128)(2,1)} %copy-done.1, bf16[10,32,128]{2,1,0:T(8,128)(2,1)} %copy-done.3, bf16[10,32,128]{2,1,0:T(8,128)(2,1)} %copy-done.4, ...), custom_call_target="tpu_custom_call" | custom-call | flops 10000000000 | bytes 30000000 | tf_op jit(solution)/shard_map/pallas_call | solution.py:407
  140.4 0.0 all-to-all-done.5
  140.5 0.1 reshape.82
  140.6 0.2 reshape.84
  140.9 0.1 copy.47
  141.0 0.9 reshape.85
  (23 shorter events, 0.2 us)
Async XLA Ops:
  2.6 8.0 %collective-permute-start.1 = (bf16[32,16,128]{2,0,1:T(8,128)(2,1)S(1)}, bf16[32,16,128]{2,0,1:T(8,128)(2,1)S(1)}, u32[]{:S(2)}, u32[]{:S(2)}) collective-permute-start(bf16[32,16,128]{2,0,1:T(8,128)(2,1)S(1)} %get-tuple-element.43), channel_id=1, source_target_pairs={{8,0},{16,8},{24,16},{9,1},{17,9},{25,17},{10,2},{18,10},{26,18},{... | collective-permute-start | bytes 393224 | tf_op jit(solution)/shard_map/ppermute | solution.py:422
  4.5 6.4 %collective-permute-start = (bf16[32,16,128]{2,0,1:T(8,128)(2,1)S(1)}, bf16[32,16,128]{2,0,1:T(8,128)(2,1)S(1)}, u32[]{:S(2)}, u32[]{:S(2)}) collective-permute-start(bf16[32,16,128]{2,0,1:T(8,128)(2,1)S(1)} %get-tuple-element.44), channel_id=1, source_target_pairs={{0,8},{8,16},{16,24},{1,9},{9,17},{17,25},{2,10},{10,18},{18,26},{... | collective-permute-start | bytes 393224 | tf_op jit(solution)/shard_map/ppermute | solution.py:422
  10.9 8.6 %collective-permute-start.2 = (bf16[10,32,128]{2,1,0:T(8,128)(2,1)S(1)}, bf16[10,32,128]{2,1,0:T(8,128)(2,1)S(1)}, u32[]{:S(2)}, u32[]{:S(2)}) collective-permute-start(bf16[10,32,128]{2,1,0:T(8,128)(2,1)S(1)} %pad_maximum_fusion.1), channel_id=1, source_target_pairs={{0,1},{1,2},{2,3},{3,4},{4,5},{5,6},{6,7},{8,9},{9,10},{10,11},{11... | collective-permute-start | bytes 245768 | tf_op jit(solution)/shard_map/ppermute | solution.py:422
  14.1 5.9 %collective-permute-start.3 = (bf16[10,32,128]{2,1,0:T(8,128)(2,1)S(1)}, bf16[10,32,128]{2,1,0:T(8,128)(2,1)S(1)}, u32[]{:S(2)}, u32[]{:S(2)}) collective-permute-start(bf16[10,32,128]{2,1,0:T(8,128)(2,1)S(1)} %pad_maximum_fusion.2), channel_id=1, source_target_pairs={{1,0},{2,1},{3,2},{4,3},{5,4},{6,5},{7,6},{9,8},{10,9},{11,10},{12... | collective-permute-start | bytes 245768 | tf_op jit(solution)/shard_map/ppermute | solution.py:422
  19.6 0.6 copy-start.5
  20.2 0.6 copy-start.6
  49.1 9.9 %all-to-all-start.1 = ((bf16[8,32,256]{2,1,0:T(8,128)(2,1)}), bf16[8,32,256]{2,1,0:T(8,128)(2,1)S(1)}, u32[]{:S(2)}, u32[]{:S(2)}) async-start(bf16[8,32,256]{2,1,0:T(8,128)(2,1)} %get-tuple-element.14), calls=%async_computation.1 | async-start | bytes 262144 | tf_op jit(solution)/shard_map/all_to_all | solution.py:426
  59.1 0.7 copy-start
  101.6 21.3 %all-to-all-start.4 = ((f32[32,8,128]{2,1,0:T(8,128)}), f32[32,8,128]{2,1,0:T(8,128)S(1)}, u32[]{:S(2)}, u32[]{:S(2)}) async-start(f32[32,8,128]{2,1,0:T(8,128)} %bitcast.61), calls=%async_computation.4 | async-start | bytes 262144 | tf_op jit(solution)/shard_map/all_to_all | solution.py:426
  109.0 7.0 %collective-permute-start.5 = (bf16[16,32,128]{2,1,0:T(8,128)(2,1)S(1)}, bf16[16,32,128]{2,1,0:T(8,128)(2,1)S(1)}, u32[]{:S(2)}, u32[]{:S(2)}) collective-permute-start(bf16[16,32,128]{2,1,0:T(8,128)(2,1)S(1)} %get-tuple-element.25), channel_id=1, source_target_pairs={{8,0},{16,8},{24,16},{9,1},{17,9},{25,17},{10,2},{18,10},{26,18},{... | collective-permute-start | bytes 393224 | tf_op jit(solution)/shard_map/ppermute | solution.py:422
  111.2 5.3 %collective-permute-start.4 = (bf16[16,32,128]{2,1,0:T(8,128)(2,1)S(1)}, bf16[16,32,128]{2,1,0:T(8,128)(2,1)S(1)}, u32[]{:S(2)}, u32[]{:S(2)}) collective-permute-start(bf16[16,32,128]{2,1,0:T(8,128)(2,1)S(1)} %get-tuple-element.26), channel_id=1, source_target_pairs={{0,8},{8,16},{16,24},{1,9},{9,17},{17,25},{2,10},{10,18},{18,26},{... | collective-permute-start | bytes 393224 | tf_op jit(solution)/shard_map/ppermute | solution.py:422
  116.0 15.7 %copy-start.1 = (bf16[16,32,128]{2,1,0:T(8,128)(2,1)}, bf16[16,32,128]{2,1,0:T(8,128)(2,1)S(1)}, u32[]{:S(2)}) copy-start(bf16[16,32,128]{2,1,0:T(8,128)(2,1)S(1)} %collective-permute-done.5.x_high) | copy-start | bytes 393220
  116.5 15.3 %copy-start.2 = (bf16[16,32,128]{2,1,0:T(8,128)(2,1)}, bf16[16,32,128]{2,1,0:T(8,128)(2,1)S(1)}, u32[]{:S(2)}) copy-start(bf16[16,32,128]{2,1,0:T(8,128)(2,1)S(1)} %collective-permute-done.4.x_low) | copy-start | bytes 393220
  116.5 15.2 %collective-permute-start.6 = (bf16[10,32,128]{2,1,0:T(8,128)(2,1)S(1)}, bf16[10,32,128]{2,1,0:T(8,128)(2,1)S(1)}, u32[]{:S(2)}, u32[]{:S(2)}) collective-permute-start(bf16[10,32,128]{2,1,0:T(8,128)(2,1)S(1)} %pad_maximum_fusion.3), channel_id=1, source_target_pairs={{0,1},{1,2},{2,3},{3,4},{4,5},{5,6},{6,7},{8,9},{9,10},{10,11},{11... | collective-permute-start | bytes 245768 | tf_op jit(solution)/shard_map/ppermute | solution.py:422
  119.8 11.9 %collective-permute-start.7 = (bf16[10,32,128]{2,1,0:T(8,128)(2,1)S(1)}, bf16[10,32,128]{2,1,0:T(8,128)(2,1)S(1)}, u32[]{:S(2)}, u32[]{:S(2)}) collective-permute-start(bf16[10,32,128]{2,1,0:T(8,128)(2,1)S(1)} %pad_maximum_fusion.4), channel_id=1, source_target_pairs={{1,0},{2,1},{3,2},{4,3},{5,4},{6,5},{7,6},{9,8},{10,9},{11,10},{12... | collective-permute-start | bytes 245768 | tf_op jit(solution)/shard_map/ppermute | solution.py:422
  123.6 16.8 %all-to-all-start.5 = ((f32[32,8,128]{2,1,0:T(8,128)}), f32[32,8,128]{2,1,0:T(8,128)S(1)}, u32[]{:S(2)}, u32[]{:S(2)}) async-start(f32[32,8,128]{2,1,0:T(8,128)} %broadcast_in_dim.18), calls=%async_computation.5 | async-start | bytes 262144 | tf_op jit(solution)/shard_map/all_to_all | solution.py:426
  131.7 0.6 copy-start.3
  131.8 0.7 copy-start.4

commit v4 on v3

--- a/solution.py
+++ b/solution.py
@@ -9,6 +9,7 @@
 
 BLOCK = 8
 REACH = 3
+RIM = 2
 SPARE = 16
 LANES = 128
 SUBLANES = 8
@@ -45,6 +46,10 @@
 def live_line(lanes, row, height):
     bands = lanes[row // BLOCK]
     return jnp.concatenate([bands[y // BLOCK : y // BLOCK + 1] for y in range(height)], 1)
+
+
+def with_rims(line, sides, place):
+    return jnp.concatenate([sides[0, pl.ds(place, 1)], line, sides[1, pl.ds(place, 1)]], 1)
 
 
 def owner_and_local(index, size):
@@ -128,7 +133,7 @@
 
 def forward_kernel(
     feat, x_low, x_high, y_low, y_high, lanes, fragment, weight, taps_out, slopes_out, partial,
-    taps, slopes, total, taps_sent, slopes_sent
+    sides, taps, slopes, total, rims, taps_sent, slopes_sent, rims_here
 ):
     rows, channels, height, depth = feat.shape
     owners, _, frag_dev = partial.shape
@@ -139,39 +144,49 @@
     send_taps = row_copy(taps, taps_out, taps_sent)
     send_slopes = row_copy(slopes, slopes_out, slopes_sent)
 
-    store_taps(taps, 0, 1, turned(x_low[...]).astype(bf16))
-    store_taps(taps, rows + 1, 1, turned(x_high[...]).astype(bf16))
+    get_low = pltpu.make_async_copy(y_low, rims.at[0], rims_here.at[0])
+    get_high = pltpu.make_async_copy(y_high, rims.at[1], rims_here.at[1])
+    get_low.start()
+    get_high.start()
+    store_taps(taps, 0, RIM, turned(x_low[...]).astype(bf16))
+    store_taps(taps, rows + 1, RIM, turned(x_high[...]).astype(bf16))
 
     def fill(x, _):
         tiles = turned(feat[x])
         live = live_line(lanes, x, height)
         gates = [live[:, y * depth : (y + 1) * depth] for y in range(height)]
         gates = jnp.concatenate([jnp.broadcast_to(g, (1, channels, depth)) for g in gates], 0)
-        store_taps(taps, x + 1, 1, (tiles * gates).astype(bf16))
+        store_taps(taps, x + 1, RIM, (tiles * gates).astype(bf16))
         return 0
 
     lax.fori_loop(0, rows, fill, 0)
+    get_low.wait()
+    get_high.wait()
 
     def edges(x, _):
-        store_taps(taps, x, 0, y_low[x][None])
-        store_taps(taps, x, height + 1, y_high[x][None])
+        store_taps(taps, x, 0, rims[0, pl.ds(RIM * x, RIM)])
+        store_taps(taps, x, height + RIM, rims[1, pl.ds(RIM * x, RIM)])
         return 0
 
     lax.fori_loop(0, rows + 2, edges, 0)
+    for side in range(2):
+        sides[side] = rims[side, RIM * (rows + 2)].astype(f32)
     start_rows(send_taps, rows + 2)
     total[...] = jnp.zeros_like(total)
 
     def one_row(x, _):
-        conv = convolve_row(taps, weight[...], x, height)
+        wide = convolve_row(taps, weight[...], x, height + 2)
         active = jnp.concatenate(
-            [taps[x + 1, y + 1, channels : 2 * channels, :] for y in range(height)], 1
+            [taps[x + 1, y + RIM, channels : 2 * channels, :] for y in range(height)], 1
         )
         live = live_line(lanes, x, height)
         owner, local = owner_and_local(line_of(fragment[x]), frag_dev)
-        sig = jax.nn.sigmoid(conv)
-        hidden = live * (active.astype(f32) + conv * sig)
-        slopes[x] = (live * slope_of(conv, sig)).astype(bf16)
+        sig = jax.nn.sigmoid(wide)
+        slopes[x] = (with_rims(live, sides, 2 * rows + x) * slope_of(wide, sig)).astype(bf16)
         send_slopes(x).start()
+        inner = slice(depth, depth + height * depth)
+        conv = wide[:, inner]
+        hidden = live * (active.astype(f32) + conv * sig[:, inner])
         tallies = lax.broadcasted_iota(jnp.int32, (total.shape[0] - owners * channels, 1), 0)
         heads = jnp.where(tallies == owner, live, 0.0).astype(bf16)
         rising = jnp.concatenate([spread(hidden, owner, owners), heads], 0)
@@ -256,68 +271,61 @@
 
 
 def hidden_kernel(
-    table, fragment, lanes, slopes_in, hidden_out, conv_out,
-    slopes, back_hidden, back_conv, slopes_here, hidden_sent, conv_sent
+    table, fragment, lanes, sides, slopes_in, taps_in,
+    hidden_out, conv_out, face_low, face_high, packed,
+    slopes, back_hidden, back_conv, taps, grad, slopes_here, hidden_sent, conv_sent, taps_here
 ):
     owners, channels, frag_dev = table.shape
-    rows, height, _, depth = back_conv.shape
+    rows, wide_height, _, depth = back_conv.shape
+    height = wide_height - 2
     flat = table[...].reshape(owners * channels, frag_dev)
     fetch = row_copy(slopes_in, slopes, slopes_here)
+    fetch_taps = row_copy(taps_in, taps, taps_here)
     send_hidden = row_copy(back_hidden, hidden_out, hidden_sent)
     send_conv = row_copy(back_conv, conv_out, conv_sent)
     start_rows(fetch, rows)
+    start_rows(fetch_taps, rows + REACH - 1)
+    empty = jnp.zeros((channels, depth), bf16)
+    grad[...] = jnp.zeros_like(grad)
+    wait_rows(fetch_taps, REACH - 1)
 
     def one_row(x, _):
         owner, local = owner_and_local(line_of(fragment[x]), frag_dev)
+        owner = with_rims(owner.astype(f32), sides, x).astype(jnp.int32)
+        local = with_rims(local.astype(f32), sides, rows + x).astype(jnp.int32)
         found = plain(flat, one_hot(local, frag_dev))
         hidden = pick(found, owner, owners)
-        back_hidden[x] = (live_line(lanes, x, height) * hidden).astype(bf16)
+        inner = hidden[:, depth : depth + height * depth]
+        back_hidden[x] = (live_line(lanes, x, height) * inner).astype(bf16)
         send_hidden(x).start()
         fetch(x).wait()
-        grad = (hidden * slopes[x].astype(f32)).astype(bf16)
-        for y in range(height):
-            back_conv[x, y] = grad[:, y * depth : (y + 1) * depth]
+        conv = (hidden * slopes[x].astype(f32)).astype(bf16)
+        for y in range(wide_height):
+            back_conv[x, y] = conv[:, y * depth : (y + 1) * depth]
         send_conv(x).start()
+        fetch_taps(x + REACH - 1).wait()
+        lines = []
+        for b in range(REACH):
+            parts = [empty] * b + [conv[:, depth : depth + height * depth]]
+            lines.append(jnp.concatenate(parts + [empty] * (REACH - 1 - b), 1))
+        stacked = jnp.concatenate(lines, 0)
+        total = None
+        for y in range(0, wide_height, 2):
+            term = by_last(stacked[:, y * depth : (y + 2) * depth], columns(taps, x, y + 1, 2))
+            total = term if total is None else total + term
+        grad[...] += total
         return 0
 
     lax.fori_loop(0, rows, one_row, 0)
+    face_low[...] = back_conv[0]
+    face_high[...] = back_conv[rows - 1]
+    packed[...] = jnp.zeros_like(packed)
+    for place, part in packed_parts(grad.shape):
+        high = part[0].stop - part[0].start
+        width = part[1].stop - part[1].start
+        packed[place[0] : place[0] + high, place[1] : place[1] + width] = grad[part]
     wait_rows(send_hidden, rows)
     wait_rows(send_conv, rows)
-
-
-def weight_kernel(taps, back_conv, packed, grad, near, arrived):
-    rows, height, channels, depth = back_conv.shape
-    empty = jnp.zeros((channels, depth), bf16)
-    grad[...] = jnp.zeros_like(grad)
-
-    def fetch(x):
-        return pltpu.make_async_copy(taps.at[x], near.at[x], arrived.at[x])
-
-    for x in range(rows + REACH - 1):
-        fetch(x).start()
-    for x in range(REACH - 1):
-        fetch(x).wait()
-
-    def one_row(x, _):
-        fetch(x + REACH - 1).wait()
-        slabs = [back_conv[x, y] for y in range(height)]
-        lines = []
-        for b in range(REACH):
-            lines.append(jnp.concatenate([empty] * b + slabs + [empty] * (REACH - 1 - b), 1))
-        stacked = jnp.concatenate(lines, 0)
-        total = None
-        for y in range(0, height + REACH - 1, 2):
-            term = by_last(stacked[:, y * depth : (y + 2) * depth], columns(near, x, y, 2))
-            total = term if total is None else total + term
-        grad[...] += total
-        return 0
-
-    lax.fori_loop(0, rows, one_row, 0)
-    packed[...] = jnp.zeros_like(packed)
-    for place, part in packed_parts(grad.shape):
-        height = part[0].stop - part[0].start
-        width = part[1].stop - part[1].start
-        packed[place[0] : place[0] + height, place[1] : place[1] + width] = grad[part]
 
 
 def packed_parts(shape):
@@ -349,44 +357,32 @@
     return jnp.concatenate(blocks, 1)
 
 
-def weight_call(taps, back_conv, shape, lines):
-    whole = pl.BlockSpec(memory_space=pltpu.VMEM)
-    return pl.pallas_call(
-        weight_kernel,
-        in_specs=[pl.BlockSpec(memory_space=pl.ANY), whole],
-        out_specs=whole,
-        out_shape=jax.ShapeDtypeStruct((lines, LANES), f32),
-        scratch_shapes=[pltpu.VMEM(shape, f32), pltpu.VMEM(taps.shape, bf16), pltpu.SemaphoreType.DMA((taps.shape[0],))],
-        cost_estimate=cost(8),
-        compiler_params=pltpu.CompilerParams(vmem_limit_bytes=LIMIT),
-    )(taps, back_conv)
-
-
 def backward_kernel(
-    back_conv, x_low, x_high, y_low, y_high, back_hidden, lanes, weight, grad_out,
-    grad, taps, sent
+    back_conv, x_low, x_high, back_hidden, lanes, weight, grad_out,
+    grad, taps, faces, sent, faces_here
 ):
-    rows, height, channels, depth = back_conv.shape
+    rows, wide_height, channels, depth = back_conv.shape
+    height = wide_height - 2
     send = row_copy(grad, grad_out, sent)
-    store_taps(taps, 0, 1, x_low[...])
-    store_taps(taps, rows + 1, 1, x_high[...])
+    get_low = pltpu.make_async_copy(x_low, faces.at[0], faces_here.at[0])
+    get_high = pltpu.make_async_copy(x_high, faces.at[1], faces_here.at[1])
+    get_low.start()
+    get_high.start()
 
     def fill(x, _):
-        store_taps(taps, x + 1, 1, back_conv[x])
+        store_taps(taps, x + 1, 0, back_conv[x])
         return 0
 
     lax.fori_loop(0, rows, fill, 0)
-
-    def edges(x, _):
-        store_taps(taps, x, 0, y_low[x][None])
-        store_taps(taps, x, height + 1, y_high[x][None])
-        return 0
-
-    lax.fori_loop(0, rows + REACH - 1, edges, 0)
+    get_low.wait()
+    get_high.wait()
+    store_taps(taps, 0, 0, faces[0])
+    store_taps(taps, rows + 1, 0, faces[1])
 
     def one_row(x, _):
         live = live_line(lanes, x, height)
-        result = live * (back_hidden[x].astype(f32) + convolve_row(taps, weight[...], x, height))
+        found = convolve_row(taps, weight[...], x, height)
+        result = live * (back_hidden[x].astype(f32) + found)
         tiles = [result[:, y * depth : (y + 1) * depth][None] for y in range(height)]
         grad[x] = jnp.swapaxes(jnp.concatenate(tiles, 0), 0, 1)
         send(x).start()
@@ -454,30 +450,42 @@
     x_low, x_high = pass_on(
         features[0] * gate[0][None], features[-1] * gate[-1][None], "drift"
     )
+    owner, local = owner_and_local(voxel_fragment, frag_dev)
     ends = []
-    for y in (0, height - 1):
-        side = features[:, :, y] * gate[:, None, y]
-        ends.append(jnp.concatenate([x_low[None, :, y], side, x_high[None, :, y]], 0))
+    for edge, first in ((0, 0), (height - 1, height - RIM)):
+        layers = slice(first, first + RIM)
+        side = (features[:, :, layers] * gate[:, None, layers]).transpose(0, 2, 1, 3)
+        outer = [x[:, layers].transpose(1, 0, 2) for x in (x_low, x_high)]
+        notes = [owner[:, edge].astype(bf16), local[:, edge].astype(bf16), gate[:, edge]]
+        notes.append(jnp.zeros((channels - 3 * rows, depth), bf16))
+        flat = side.reshape(RIM * rows, channels, depth)
+        ends.append(
+            jnp.concatenate([outer[0], flat, outer[1], jnp.concatenate(notes, 0)[None]], 0)
+        )
     y_low, y_high = pass_on(ends[0], ends[1], "beam")
 
     heads = -(-owners // 16) * 16
     line_shape = (rows, channels, plane)
-    conv_shape = (rows, height, channels, depth)
+    wide_shape = (rows, channels, plane + 2 * depth)
+    conv_shape = (rows, height + 2, channels, depth)
     dma = lambda count: pltpu.SemaphoreType.DMA((count,))
-    padded = (rows + 2, height + 2, REACH * channels, depth)
-    taps, slopes, partial = call(
+    tapped = (rows + 2, height + 2, REACH * channels, depth)
+    padded = (rows + 2, height + 2 * RIM, REACH * channels, depth)
+    taps, slopes, partial, sides = call(
         forward_kernel,
         [
             (padded, bf16),
-            (line_shape, bf16),
+            (wide_shape, bf16),
             ((owners, channels + SPARE, frag_dev), bf16),
+            ((2, channels, depth), f32),
         ],
         features, x_low, x_high, y_low, y_high, lanes, voxel_fragment, stacked, micros=12,
         scratch=[
-            pltpu.VMEM(padded, bf16), pltpu.VMEM(line_shape, bf16),
-            pltpu.VMEM((owners * channels + heads, frag_dev), f32), dma(rows + 2), dma(rows),
+            pltpu.VMEM(padded, bf16), pltpu.VMEM(wide_shape, bf16),
+            pltpu.VMEM((owners * channels + heads, frag_dev), f32),
+            pltpu.VMEM((2,) + y_low.shape, bf16), dma(rows + 2), dma(rows), dma(2),
         ],
-        far_out=(0, 1),
+        far_in=(3, 4), far_out=(0, 1),
     )
     spread_shape = (owners, channels, frag_dev)
     pooled, divisor = call(
@@ -496,33 +504,34 @@
     (mean,) = call(
         mean_kernel, [(spread_shape, bf16)], exchange(back_parts, "beam"), direct, divisor
     )
-    back_hidden, back_conv = call(
-        hidden_kernel,
-        [(line_shape, bf16), (conv_shape, bf16)],
-        exchange(mean, "beam"), voxel_fragment, lanes, slopes, micros=7,
-        scratch=[
-            pltpu.VMEM(line_shape, bf16), pltpu.VMEM(line_shape, bf16),
-            pltpu.VMEM(conv_shape, bf16), dma(rows), dma(rows), dma(rows),
-        ],
-        far_in=(3,), far_out=(0, 1),
-    )
-    gx_low, gx_high = pass_on(back_conv[0], back_conv[-1], "drift")
     everyone = ("drift", "beam")
     devices = lax.axis_size(everyone)
     tile = SUBLANES * LANES
     share = -(-conv_weight.size // (devices * tile)) * SUBLANES
-    packed = weight_call(taps, back_conv, stacked_shape, devices * share)
-    ends = [
-        jnp.concatenate([gx_low[None, y], back_conv[:, y], gx_high[None, y]], 0)
-        for y in (0, height - 1)
-    ]
-    gy_low, gy_high = pass_on(ends[0], ends[1], "beam")
+    back_hidden, back_conv, face_low, face_high, packed = call(
+        hidden_kernel,
+        [
+            (line_shape, bf16), (conv_shape, bf16), (conv_shape[1:], bf16), (conv_shape[1:], bf16),
+            ((devices * share, LANES), f32),
+        ],
+        exchange(mean, "beam"), voxel_fragment, lanes, sides, slopes, taps, micros=14,
+        scratch=[
+            pltpu.VMEM(wide_shape, bf16), pltpu.VMEM(line_shape, bf16),
+            pltpu.VMEM(conv_shape, bf16), pltpu.VMEM(padded, bf16),
+            pltpu.VMEM(stacked_shape, f32), dma(rows), dma(rows), dma(rows), dma(rows + 2),
+        ],
+        far_in=(4, 5), far_out=(0, 1),
+    )
+    gx_low, gx_high = pass_on(face_low, face_high, "drift")
     (grad_features,) = call(
         backward_kernel,
         [(features.shape, f32)],
-        back_conv, gx_low, gx_high, gy_low, gy_high, back_hidden, lanes, flipped, micros=10,
-        scratch=[pltpu.VMEM(features.shape, f32), pltpu.VMEM(padded, bf16), dma(rows)],
-        far_out=(0,),
+        back_conv, gx_low, gx_high, back_hidden, lanes, flipped, micros=10,
+        scratch=[
+            pltpu.VMEM(features.shape, f32), pltpu.VMEM(tapped, bf16),
+            pltpu.VMEM((2,) + conv_shape[1:], bf16), dma(rows), dma(2),
+        ],
+        far_in=(1, 2), far_out=(0,),
     )
     parts = exchange(packed, everyone).reshape(devices, share, LANES)
     full = exchange(jnp.broadcast_to(parts.sum(0)[None], parts.shape), everyone)

time: 143 us -> 135 us (0.944)
  starting transfers between devices: 40.2 us -> 32.9 us
  local copies, waits for them, and re-layouts: 15.8 us -> 11.7 us
  other arithmetic: 0.88 us -> 3.31 us
  waiting for transfers between devices: 6.8 us -> 8.93 us
    pallas_call x1 -> x0, Pallas kernels: 8.04 us -> none  [weight_call(): pl.pallas_call(weight_kernel, in_specs=[pl.BlockSpec(memory_space=pl.ANY)...]
    pallas_call x6, Pallas kernels: 34.5 us -> 42.3 us  [call(): pl.pallas_call(kernel, in_specs=[there if i in far_in else here for i in...]
    ppermute x8 -> x6, starting transfers between devices: 21 us -> 16.3 us  [pass_on(): return (lax.ppermute(high, axis, up), lax.ppermute(low, axis, down))]
    all_to_all x3, starting transfers between devices: 19.2 us -> 16.6 us  [exchange(): return lax.all_to_all(parts, axes, 0, 0, tiled=True)]
    squeeze x2, local copies, waits for them, and re-layouts: 1.88 us -> 0.01 us  [body(): gate[:, edge]]
    ppermute x8 -> x6, waiting for transfers between devices: 1.9 us -> 3.56 us  [pass_on(): return (lax.ppermute(high, axis, up), lax.ppermute(low, axis, down))]
    transpose x0 -> x1, other arithmetic: none -> 1.49 us  [body(): (features[:, :, layers] * gate[:, None, layers]).transpose(0, 2, 1, 3)]
    slice x4 -> x2, local copies, waits for them, and re-layouts: 1.46 us -> 0.01 us  [the longest x1 0.01 us: body(): gate[:, None, layers]]
  transfers between devices with their start and end apart: 11 -> 9, of which waited for: 5 -> 3; matrix products, arithmetic and copies ran while one was open for 7% -> 7% of each run, Pallas kernels for 6% -> 5%
where the time goes in v4:
time: 135 us; the launch traced here: 133 us
  Pallas kernels  42.3 us (31%)
  blocking collectives  33.3 us (25%)
  starting transfers between devices  32.9 us (24%)
  local copies, waits for them, and re-layouts  11.7 us (9%)
  waiting for transfers between devices  8.93 us (7%)
  other arithmetic  3.31 us (2%)
    pallas_call x6, Pallas kernels, call(): pl.pallas_call(kernel, in_specs=[there if i in far_in else here for i in...  42.3 us
    all_to_all x3, blocking collectives, exchange(): return lax.all_to_all(parts, axes, 0, 0, tiled=True)  33.3 us
    all_to_all x3, starting transfers between devices, exchange(): return lax.all_to_all(parts, axes, 0, 0, tiled=True)  16.6 us
    ppermute x6, starting transfers between devices, pass_on(): return (lax.ppermute(high, axis, up), lax.ppermute(low, axis, down))  16.3 us
    all_to_all x3, waiting for transfers between devices, exchange(): return lax.all_to_all(parts, axes, 0, 0, tiled=True)  5.37 us
    ppermute x6, waiting for transfers between devices, pass_on(): return (lax.ppermute(high, axis, up), lax.ppermute(low, axis, down))  3.56 us
  transfers between devices with their start and end apart: 9, of which 3 were waited for; matrix products, arithmetic and copies ran while one was open for 7% of the time, Pallas kernels for 5%

profile of v4, /device:TPU:1, one launch (start us, length us, event | category | flops | bytes accessed | tf_op | source)
XLA Modules:
  0.0 133.4 jit_solution(9902661905330503506)
XLA Ops:
  0.6 0.0 copy-start.1
  0.6 0.7 convert_bitcast_fusion
  1.3 0.1 broadcast_in_dim.23
  1.4 0.1 convert_element_type.41
  1.5 1.0 fusion.3
  2.5 0.1 fusion
  2.6 2.0 %collective-permute-start.1 = (bf16[32,16,128]{2,0,1:T(8,128)(2,1)S(1)}, bf16[32,16,128]{2,0,1:T(8,128)(2,1)S(1)}, u32[]{:S(2)}, u32[]{:S(2)}) collective-permute-start(bf16[32,16,128]{2,0,1:T(8,128)(2,1)S(1)} %get-tuple-element.51), channel_id=1, source_target_pairs={{8,0},{16,8},{24,16},{9,1},{17,9},{25,17},{10,2},{18,10},{26,18},{... | collective-permute-start | bytes 393224 | tf_op jit(solution)/shard_map/ppermute | solution.py:418
  4.6 4.5 %collective-permute-start = (bf16[32,16,128]{2,0,1:T(8,128)(2,1)S(1)}, bf16[32,16,128]{2,0,1:T(8,128)(2,1)S(1)}, u32[]{:S(2)}, u32[]{:S(2)}) collective-permute-start(bf16[32,16,128]{2,0,1:T(8,128)(2,1)S(1)} %get-tuple-element.52), channel_id=1, source_target_pairs={{0,8},{8,16},{16,24},{1,9},{9,17},{17,25},{2,10},{10,18},{18,26},{... | collective-permute-start | bytes 393224 | tf_op jit(solution)/shard_map/ppermute | solution.py:418
  9.1 0.9 shift-right-arithmetic_convert_fusion
  9.9 1.5 %multiply_bitcast_fusion = (bf16[8,2,32,128]{3,1,2,0:T(2,128)(2,1)S(1)}, bf16[8,2,32,128]{3,1,2,0:T(2,128)(2,1)S(1)}) fusion(bf16[8,32,16,128]{3,2,1,0:T(8,128)(2,1)} %feat.1, bf16[2,128]{1,0:T(2,128)(2,1)S(1)} %get-tuple-element.47, bf16[2,128]{1,0:T(2,128)(2,1)S(1)} %get-tuple-element.48), kind=kLoop, calls=%fused_computation.7 | loop fusion | flops 131072 | bytes 525312 | tf_op jit(solution)/shard_map/transpose | solution.py:457
  11.5 0.1 pad.18.clone
  11.6 0.1 maximum_bitcast_fusion.1
  11.7 0.0 collective-permute-done.1
  11.7 0.0 collective-permute-done
  11.7 3.2 %collective-permute-start.2 = (bf16[21,32,128]{2,1,0:T(8,128)(2,1)S(1)}, bf16[21,32,128]{2,1,0:T(8,128)(2,1)S(1)}, u32[]{:S(2)}, u32[]{:S(2)}) collective-permute-start(bf16[21,32,128]{2,1,0:T(8,128)(2,1)S(1)} %pad_maximum_fusion), channel_id=1, source_target_pairs={{0,1},{1,2},{2,3},{3,4},{4,5},{5,6},{6,7},{8,9},{9,10},{10,11},{11... | collective-permute-start | bytes 516104 | tf_op jit(solution)/shard_map/ppermute | solution.py:418
  14.9 1.3 collective-permute-start.3
  16.2 0.1 broadcast_in_dim.27
  16.3 0.7 convert_element_type.48.lanes
  17.0 0.0 copy-done.1
  17.0 0.2 reshape.89
  17.2 0.1 copy.41
  17.3 0.8 reshape.90.weight
  18.1 0.7 copy.43.x_high
  18.8 0.7 copy.42.x_low
  19.5 0.0 collective-permute-done.2.y_low
  19.5 0.0 copy-start.2
  19.5 3.5 %collective-permute-done.3.y_high = bf16[21,32,128]{2,1,0:T(8,128)(2,1)S(1)} collective-permute-done((bf16[21,32,128]{2,1,0:T(8,128)(2,1)S(1)}, bf16[21,32,128]{2,1,0:T(8,128)(2,1)S(1)}, u32[]{:S(2)}, u32[]{:S(2)}) %collective-permute-start.3) | collective-permute-done | bytes 172064 | tf_op jit(solution)/shard_map/ppermute | solution.py:418
  23.1 0.0 copy-done.2
  23.1 0.0 copy-start.3
  23.1 0.7 copy-done.3
  23.8 12.6 %shard_map.121 = (bf16[10,20,96,128]{3,2,1,0:T(8,128)(2,1)}, bf16[8,32,2304]{2,1,0:T(8,128)(2,1)}, bf16[8,48,256]{2,1,0:T(8,128)(2,1)}, f32[2,32,128]{2,1,0:T(8,128)}) custom-call(bf16[8,32,16,128]{3,2,1,0:T(8,128)(2,1)} %feat.1, bf16[32,16,128]{2,1,0:T(8,128)(2,1)} %copy.42.x_low, bf16[32,16,128]{2,1,0:T(8,128)(2,1)} %copy.43.x_high, ...), custom_call_target="tpu_custom_call" | custom-call | flops 12000000000 | bytes 36000000 | tf_op jit(solution)/shard_map/pallas_call | solution.py:403
  36.3 12.9 %all_to_all.34.parts = bf16[8,48,256]{2,1,0:T(8,128)(2,1)} all-to-all(bf16[8,48,256]{2,1,0:T(8,128)(2,1)} %get-tuple-element.17), channel_id=1, replica_groups=mesh['drift'=4,'beam'=8] {'beam'}, dimensions={0} | all-to-all | bytes 393216 | tf_op jit(solution)/shard_map/all_to_all | solution.py:422
  49.3 1.6 %shard_map.122 = (bf16[8,32,256]{2,1,0:T(8,128)(2,1)}, f32[8,256]{1,0:T(8,128)}) custom-call(bf16[8,48,256]{2,1,0:T(8,128)(2,1)} %all_to_all.34.parts), custom_call_target="tpu_custom_call" | custom-call | flops 2000000000 | bytes 6000000 | tf_op jit(solution)/shard_map/pallas_call | solution.py:403
  50.9 4.0 %all-to-all-start.1 = ((bf16[8,32,256]{2,1,0:T(8,128)(2,1)}), bf16[8,32,256]{2,1,0:T(8,128)(2,1)S(1)}, u32[]{:S(2)}, u32[]{:S(2)}) async-start(bf16[8,32,256]{2,1,0:T(8,128)(2,1)} %get-tuple-element.18), calls=%async_computation.1 | async-start | bytes 262144 | tf_op jit(solution)/shard_map/all_to_all | solution.py:422
  54.9 1.3 slice_bitcast_fusion.6.mine
  56.2 4.9 %all-to-all-done.1.table = bf16[8,32,256]{2,1,0:T(8,128)(2,1)S(1)} async-done(((bf16[8,32,256]{2,1,0:T(8,128)(2,1)}), bf16[8,32,256]{2,1,0:T(8,128)(2,1)S(1)}, u32[]{:S(2)}, u32[]{:S(2)}) %all-to-all-start.1) | async-done | bytes 131104 | tf_op jit(solution)/shard_map/all_to_all | solution.py:422
  61.1 0.0 copy-start
  61.1 0.7 copy-done
  61.8 4.2 %shard_map.123 = (bf16[256,256]{1,0:T(8,128)(2,1)}, bf16[8,32,256]{2,1,0:T(8,128)(2,1)}, f32[32,256]{1,0:T(8,128)}) custom-call(bf16[8,32,256]{2,1,0:T(8,128)(2,1)} %copy-done, bf16[32,256]{1,0:T(8,128)(2,1)} %slice_bitcast_fusion.6.mine, bf16[32,256]{1,0:T(8,128)(2,1)} %embed.1, bf16[256,256]{1,0:T(8,128)(2,1)} %message.1, bf16[256,256]{1,0:T(8,128)(2,1)} %update.1, ...), custom_call_target="tpu_custom_call" | custom-call | flops 2000000000 | bytes 6000000 | tf_op jit(solution)/shard_map/pallas_call | solution.py:403
  66.0 10.2 %all_to_all.35.parts = bf16[8,32,256]{2,1,0:T(8,128)(2,1)} all-to-all(bf16[8,32,256]{2,1,0:T(8,128)(2,1)} %get-tuple-element.20), channel_id=1, replica_groups=mesh['drift'=4,'beam'=8] {'beam'}, dimensions={0} | all-to-all | bytes 262144 | tf_op jit(solution)/shard_map/all_to_all | solution.py:422
  76.2 1.6 %shard_map.124 = bf16[8,32,256]{2,1,0:T(8,128)(2,1)} custom-call(bf16[8,32,256]{2,1,0:T(8,128)(2,1)} %all_to_all.35.parts, f32[32,256]{1,0:T(8,128)} %get-tuple-element.21.direct, f32[8,256]{1,0:T(8,128)} %get-tuple-element.22.divisor), custom_call_target="tpu_custom_call" | custom-call | flops 2000000000 | bytes 6000000 | tf_op jit(solution)/shard_map/pallas_call | solution.py:403
  77.8 10.2 %all_to_all.36.table = bf16[8,32,256]{2,1,0:T(8,128)(2,1)} all-to-all(bf16[8,32,256]{2,1,0:T(8,128)(2,1)} %shard_map.124), channel_id=1, replica_groups=mesh['drift'=4,'beam'=8] {'beam'}, dimensions={0} | all-to-all | bytes 262144 | tf_op jit(solution)/shard_map/all_to_all | solution.py:422
  87.9 15.0 %shard_map.125 = (bf16[8,32,2048]{2,1,0:T(8,128)(2,1)}, bf16[8,18,32,128]{3,2,1,0:T(8,128)(2,1)}, bf16[18,32,128]{2,1,0:T(8,128)(2,1)}, bf16[18,32,128]{2,1,0:T(8,128)(2,1)}, f32[256,128]{1,0:T(8,128)}) custom-call(bf16[8,32,256]{2,1,0:T(8,128)(2,1)} %all_to_all.36.table, s32[8,16,128]{2,1,0:T(8,128)} %fragment.3, f32[1,2,128]{2,1,0:T(2,128)} %convert_element_type.48.lanes, ...), custom_call_target="tpu_custom_call" | custom-call | flops 14000000000 | bytes 42000000 | tf_op jit(solution)/shard_map/pallas_call | solution.py:403
  103.0 7.0 %all-to-all-start.4 = ((f32[32,8,128]{2,1,0:T(8,128)}), f32[32,8,128]{2,1,0:T(8,128)S(1)}, u32[]{:S(2)}, u32[]{:S(2)}) async-start(f32[32,8,128]{2,1,0:T(8,128)} %bitcast.65), calls=%async_computation.4 | async-start | bytes 262144 | tf_op jit(solution)/shard_map/all_to_all | solution.py:422
  110.0 3.5 %collective-permute-start.4 = (bf16[18,32,128]{2,1,0:T(8,128)(2,1)}, bf16[18,32,128]{2,1,0:T(8,128)(2,1)S(1)}, u32[]{:S(2)}, u32[]{:S(2)}) collective-permute-start(bf16[18,32,128]{2,1,0:T(8,128)(2,1)} %get-tuple-element.27), channel_id=1, source_target_pairs={{0,8},{8,16},{16,24},{1,9},{9,17},{17,25},{2,10},{10,18},{18,26},{... | collective-permute-start | bytes 442376 | tf_op jit(solution)/shard_map/ppermute | solution.py:418
  113.5 1.9 %collective-permute-start.5 = (bf16[18,32,128]{2,1,0:T(8,128)(2,1)}, bf16[18,32,128]{2,1,0:T(8,128)(2,1)S(1)}, u32[]{:S(2)}, u32[]{:S(2)}) collective-permute-start(bf16[18,32,128]{2,1,0:T(8,128)(2,1)} %get-tuple-element.28), channel_id=1, source_target_pairs={{8,0},{16,8},{24,16},{9,1},{17,9},{25,17},{10,2},{18,10},{26,18},{... | collective-permute-start | bytes 442376 | tf_op jit(solution)/shard_map/ppermute | solution.py:418
  115.5 0.7 rev.3
  116.2 0.2 copy.44
  116.4 0.8 reshape.93.weight
  117.2 0.5 all-to-all-done.4
  117.8 0.7 broadcast_in_dim.28
  118.4 5.6 %all-to-all-start.5 = ((f32[32,8,128]{2,1,0:T(8,128)}), f32[32,8,128]{2,1,0:T(8,128)S(1)}, u32[]{:S(2)}, u32[]{:S(2)}) async-start(f32[32,8,128]{2,1,0:T(8,128)} %broadcast_in_dim.28), calls=%async_computation.5 | async-start | bytes 262144 | tf_op jit(solution)/shard_map/all_to_all | solution.py:422
  124.0 0.0 collective-permute-done.4.x_low
  124.0 0.0 copy-start.4
  124.0 0.0 collective-permute-done.5.x_high
  124.0 0.0 copy-start.5
  124.0 0.6 copy-done.4
  124.7 0.0 copy-done.5
  124.7 7.2 %shard_map.126 = f32[8,32,16,128]{3,2,1,0:T(8,128)} custom-call(bf16[8,18,32,128]{3,2,1,0:T(8,128)(2,1)} %get-tuple-element.26.back_conv, bf16[18,32,128]{2,1,0:T(8,128)(2,1)} %copy-done.4, bf16[18,32,128]{2,1,0:T(8,128)(2,1)} %copy-done.5, bf16[8,32,2048]{2,1,0:T(8,128)(2,1)} %get-tuple-element.29.back_hidden, f32[1,2,128]{2,1,0:T(2,128)} %convert_element_type.48.lanes, ...), custom_call_target="tpu_custom_call" | custom-call | flops 10000000000 | bytes 30000000 | tf_op jit(solution)/shard_map/pallas_call | solution.py:403
  132.0 0.0 all-to-all-done.5
  132.0 0.1 reshape.94
  132.1 0.2 reshape.96
  132.4 0.1 copy.47
  132.5 0.9 reshape.97
  (18 shorter events, 0.2 us)
Async XLA Ops:
  0.6 16.3 %copy-start.1 = (bf16[32,864]{1,0:T(8,128)(2,1)S(1)}, bf16[32,864]{1,0:T(8,128)(2,1)}, u32[]{:S(2)}) copy-start(bf16[32,864]{1,0:T(8,128)(2,1)} %param.13) | copy-start | bytes 165892
  2.6 9.1 %collective-permute-start.1 = (bf16[32,16,128]{2,0,1:T(8,128)(2,1)S(1)}, bf16[32,16,128]{2,0,1:T(8,128)(2,1)S(1)}, u32[]{:S(2)}, u32[]{:S(2)}) collective-permute-start(bf16[32,16,128]{2,0,1:T(8,128)(2,1)S(1)} %get-tuple-element.51), channel_id=1, source_target_pairs={{8,0},{16,8},{24,16},{9,1},{17,9},{25,17},{10,2},{18,10},{26,18},{... | collective-permute-start | bytes 393224 | tf_op jit(solution)/shard_map/ppermute | solution.py:418
  4.6 7.1 %collective-permute-start = (bf16[32,16,128]{2,0,1:T(8,128)(2,1)S(1)}, bf16[32,16,128]{2,0,1:T(8,128)(2,1)S(1)}, u32[]{:S(2)}, u32[]{:S(2)}) collective-permute-start(bf16[32,16,128]{2,0,1:T(8,128)(2,1)S(1)} %get-tuple-element.52), channel_id=1, source_target_pairs={{0,8},{8,16},{16,24},{1,9},{9,17},{17,25},{2,10},{10,18},{18,26},{... | collective-permute-start | bytes 393224 | tf_op jit(solution)/shard_map/ppermute | solution.py:418
  11.7 7.8 %collective-permute-start.2 = (bf16[21,32,128]{2,1,0:T(8,128)(2,1)S(1)}, bf16[21,32,128]{2,1,0:T(8,128)(2,1)S(1)}, u32[]{:S(2)}, u32[]{:S(2)}) collective-permute-start(bf16[21,32,128]{2,1,0:T(8,128)(2,1)S(1)} %pad_maximum_fusion), channel_id=1, source_target_pairs={{0,1},{1,2},{2,3},{3,4},{4,5},{5,6},{6,7},{8,9},{9,10},{10,11},{11... | collective-permute-start | bytes 516104 | tf_op jit(solution)/shard_map/ppermute | solution.py:418
  14.9 8.1 %collective-permute-start.3 = (bf16[21,32,128]{2,1,0:T(8,128)(2,1)S(1)}, bf16[21,32,128]{2,1,0:T(8,128)(2,1)S(1)}, u32[]{:S(2)}, u32[]{:S(2)}) collective-permute-start(bf16[21,32,128]{2,1,0:T(8,128)(2,1)S(1)} %pad_maximum_fusion.1), channel_id=1, source_target_pairs={{1,0},{2,1},{3,2},{4,3},{5,4},{6,5},{7,6},{9,8},{10,9},{11,10},{12... | collective-permute-start | bytes 516104 | tf_op jit(solution)/shard_map/ppermute | solution.py:418
  19.5 3.6 %copy-start.2 = (bf16[21,32,128]{2,1,0:T(8,128)(2,1)}, bf16[21,32,128]{2,1,0:T(8,128)(2,1)S(1)}, u32[]{:S(2)}) copy-start(bf16[21,32,128]{2,1,0:T(8,128)(2,1)S(1)} %collective-permute-done.2.y_low) | copy-start | bytes 516100
  23.1 0.7 copy-start.3
  50.9 10.2 %all-to-all-start.1 = ((bf16[8,32,256]{2,1,0:T(8,128)(2,1)}), bf16[8,32,256]{2,1,0:T(8,128)(2,1)S(1)}, u32[]{:S(2)}, u32[]{:S(2)}) async-start(bf16[8,32,256]{2,1,0:T(8,128)(2,1)} %get-tuple-element.18), calls=%async_computation.1 | async-start | bytes 262144 | tf_op jit(solution)/shard_map/all_to_all | solution.py:422
  61.1 0.7 copy-start
  103.0 14.7 %all-to-all-start.4 = ((f32[32,8,128]{2,1,0:T(8,128)}), f32[32,8,128]{2,1,0:T(8,128)S(1)}, u32[]{:S(2)}, u32[]{:S(2)}) async-start(f32[32,8,128]{2,1,0:T(8,128)} %bitcast.65), calls=%async_computation.4 | async-start | bytes 262144 | tf_op jit(solution)/shard_map/all_to_all | solution.py:422
  110.0 14.0 %collective-permute-start.4 = (bf16[18,32,128]{2,1,0:T(8,128)(2,1)}, bf16[18,32,128]{2,1,0:T(8,128)(2,1)S(1)}, u32[]{:S(2)}, u32[]{:S(2)}) collective-permute-start(bf16[18,32,128]{2,1,0:T(8,128)(2,1)} %get-tuple-element.27), channel_id=1, source_target_pairs={{0,8},{8,16},{16,24},{1,9},{9,17},{17,25},{2,10},{10,18},{18,26},{... | collective-permute-start | bytes 442376 | tf_op jit(solution)/shard_map/ppermute | solution.py:418
  113.5 10.5 %collective-permute-start.5 = (bf16[18,32,128]{2,1,0:T(8,128)(2,1)}, bf16[18,32,128]{2,1,0:T(8,128)(2,1)S(1)}, u32[]{:S(2)}, u32[]{:S(2)}) collective-permute-start(bf16[18,32,128]{2,1,0:T(8,128)(2,1)} %get-tuple-element.28), channel_id=1, source_target_pairs={{8,0},{16,8},{24,16},{9,1},{17,9},{25,17},{10,2},{18,10},{26,18},{... | collective-permute-start | bytes 442376 | tf_op jit(solution)/shard_map/ppermute | solution.py:418
  118.4 13.6 %all-to-all-start.5 = ((f32[32,8,128]{2,1,0:T(8,128)}), f32[32,8,128]{2,1,0:T(8,128)S(1)}, u32[]{:S(2)}, u32[]{:S(2)}) async-start(f32[32,8,128]{2,1,0:T(8,128)} %broadcast_in_dim.28), calls=%async_computation.5 | async-start | bytes 262144 | tf_op jit(solution)/shard_map/all_to_all | solution.py:422
  124.0 0.7 copy-start.4
  124.0 0.7 copy-start.5

commit v5 on v4

--- a/solution.py
+++ b/solution.py
@@ -14,7 +14,7 @@
 LANES = 128
 SUBLANES = 8
 DIGIT = 128.0
-LIMIT = 56 * 1024 * 1024
+LIMIT = 32 * 1024 * 1024
 bf16 = jnp.bfloat16
 f32 = jnp.float32
 
@@ -94,14 +94,6 @@
     return lambda x: pltpu.make_async_copy(source.at[x], target.at[x], arrived.at[x])
 
 
-def start_rows(copy, rows):
-    def step(x, _):
-        copy(x).start()
-        return 0
-
-    lax.fori_loop(0, rows, step, 0)
-
-
 def wait_rows(copy, rows):
     def step(x, _):
         copy(x).wait()
@@ -132,17 +124,14 @@
 
 
 def forward_kernel(
-    feat, x_low, x_high, y_low, y_high, lanes, fragment, weight, taps_out, slopes_out, partial,
-    sides, taps, slopes, total, rims, taps_sent, slopes_sent, rims_here
+    feat, x_low, x_high, y_low, y_high, lanes, fragment, weight, _, taps, slopes, partial,
+    sides, total, rims, rims_here
 ):
     rows, channels, height, depth = feat.shape
     owners, _, frag_dev = partial.shape
 
     def turned(block):
         return jnp.swapaxes(block.astype(f32), 0, 1)
-
-    send_taps = row_copy(taps, taps_out, taps_sent)
-    send_slopes = row_copy(slopes, slopes_out, slopes_sent)
 
     get_low = pltpu.make_async_copy(y_low, rims.at[0], rims_here.at[0])
     get_high = pltpu.make_async_copy(y_high, rims.at[1], rims_here.at[1])
@@ -171,7 +160,6 @@
     lax.fori_loop(0, rows + 2, edges, 0)
     for side in range(2):
         sides[side] = rims[side, RIM * (rows + 2)].astype(f32)
-    start_rows(send_taps, rows + 2)
     total[...] = jnp.zeros_like(total)
 
     def one_row(x, _):
@@ -183,7 +171,6 @@
         owner, local = owner_and_local(line_of(fragment[x]), frag_dev)
         sig = jax.nn.sigmoid(wide)
         slopes[x] = (with_rims(live, sides, 2 * rows + x) * slope_of(wide, sig)).astype(bf16)
-        send_slopes(x).start()
         inner = slice(depth, depth + height * depth)
         conv = wide[:, inner]
         hidden = live * (active.astype(f32) + conv * sig[:, inner])
@@ -207,8 +194,6 @@
             if DIGIT ** (d + 1) > rows * height * depth:
                 break
         partial[h, channels:] = digits.astype(bf16)
-    wait_rows(send_taps, rows + 2)
-    wait_rows(send_slopes, rows)
 
 
 def pool_kernel(parts, pooled, divisor):
@@ -271,39 +256,31 @@
 
 
 def hidden_kernel(
-    table, fragment, lanes, sides, slopes_in, taps_in,
-    hidden_out, conv_out, face_low, face_high, packed,
-    slopes, back_hidden, back_conv, taps, grad, slopes_here, hidden_sent, conv_sent, taps_here
+    table, fragment, lanes, sides, slopes, taps,
+    back_hidden, back_conv, face_low, face_high, packed, grad
 ):
     owners, channels, frag_dev = table.shape
     rows, wide_height, _, depth = back_conv.shape
     height = wide_height - 2
     flat = table[...].reshape(owners * channels, frag_dev)
-    fetch = row_copy(slopes_in, slopes, slopes_here)
-    fetch_taps = row_copy(taps_in, taps, taps_here)
-    send_hidden = row_copy(back_hidden, hidden_out, hidden_sent)
-    send_conv = row_copy(back_conv, conv_out, conv_sent)
-    start_rows(fetch, rows)
-    start_rows(fetch_taps, rows + REACH - 1)
     empty = jnp.zeros((channels, depth), bf16)
     grad[...] = jnp.zeros_like(grad)
-    wait_rows(fetch_taps, REACH - 1)
 
     def one_row(x, _):
         owner, local = owner_and_local(line_of(fragment[x]), frag_dev)
         owner = with_rims(owner.astype(f32), sides, x).astype(jnp.int32)
         local = with_rims(local.astype(f32), sides, rows + x).astype(jnp.int32)
-        found = plain(flat, one_hot(local, frag_dev))
-        hidden = pick(found, owner, owners)
+        pieces = []
+        for y in range(0, wide_height, 2):
+            here = slice(y * depth, (y + 2) * depth)
+            found = plain(flat, one_hot(local[:, here], frag_dev))
+            pieces.append(pick(found, owner[:, here], owners))
+        hidden = jnp.concatenate(pieces, 1)
         inner = hidden[:, depth : depth + height * depth]
         back_hidden[x] = (live_line(lanes, x, height) * inner).astype(bf16)
-        send_hidden(x).start()
-        fetch(x).wait()
         conv = (hidden * slopes[x].astype(f32)).astype(bf16)
         for y in range(wide_height):
             back_conv[x, y] = conv[:, y * depth : (y + 1) * depth]
-        send_conv(x).start()
-        fetch_taps(x + REACH - 1).wait()
         lines = []
         for b in range(REACH):
             parts = [empty] * b + [conv[:, depth : depth + height * depth]]
@@ -311,7 +288,8 @@
         stacked = jnp.concatenate(lines, 0)
         total = None
         for y in range(0, wide_height, 2):
-            term = by_last(stacked[:, y * depth : (y + 2) * depth], columns(taps, x, y + 1, 2))
+            near = stacked[:, y * depth : (y + 2) * depth]
+            term = by_last(columns(taps, x, y + 1, 2), near)
             total = term if total is None else total + term
         grad[...] += total
         return 0
@@ -320,12 +298,11 @@
     face_low[...] = back_conv[0]
     face_high[...] = back_conv[rows - 1]
     packed[...] = jnp.zeros_like(packed)
-    for place, part in packed_parts(grad.shape):
+    turned = grad[...].T
+    for place, part in packed_parts(turned.shape):
         high = part[0].stop - part[0].start
         width = part[1].stop - part[1].start
-        packed[place[0] : place[0] + high, place[1] : place[1] + width] = grad[part]
-    wait_rows(send_hidden, rows)
-    wait_rows(send_conv, rows)
+        packed[place[0] : place[0] + high, place[1] : place[1] + width] = turned[part]
 
 
 def packed_parts(shape):
@@ -479,13 +456,12 @@
             ((owners, channels + SPARE, frag_dev), bf16),
             ((2, channels, depth), f32),
         ],
-        features, x_low, x_high, y_low, y_high, lanes, voxel_fragment, stacked, micros=12,
+        features, x_low, x_high, y_low, y_high, lanes, voxel_fragment, stacked, flipped, micros=12,
         scratch=[
-            pltpu.VMEM(padded, bf16), pltpu.VMEM(wide_shape, bf16),
             pltpu.VMEM((owners * channels + heads, frag_dev), f32),
-            pltpu.VMEM((2,) + y_low.shape, bf16), dma(rows + 2), dma(rows), dma(2),
+            pltpu.VMEM((2,) + y_low.shape, bf16), dma(2),
         ],
-        far_in=(3, 4), far_out=(0, 1),
+        far_in=(3, 4, 8),
     )
     spread_shape = (owners, channels, frag_dev)
     pooled, divisor = call(
@@ -515,12 +491,7 @@
             ((devices * share, LANES), f32),
         ],
         exchange(mean, "beam"), voxel_fragment, lanes, sides, slopes, taps, micros=14,
-        scratch=[
-            pltpu.VMEM(wide_shape, bf16), pltpu.VMEM(line_shape, bf16),
-            pltpu.VMEM(conv_shape, bf16), pltpu.VMEM(padded, bf16),
-            pltpu.VMEM(stacked_shape, f32), dma(rows), dma(rows), dma(rows), dma(rows + 2),
-        ],
-        far_in=(4, 5), far_out=(0, 1),
+        scratch=[pltpu.VMEM(stacked_shape[::-1], f32)],
     )
     gx_low, gx_high = pass_on(face_low, face_high, "drift")
     (grad_features,) = call(

time: 135 us -> 115 us (0.85)
  Pallas kernels: 42.3 us -> 28.2 us
  local copies, waits for them, and re-layouts: 11.7 us -> 6 us
  waiting for transfers between devices: 8.93 us -> 14.2 us
  blocking collectives: 33.3 us -> 29.9 us
  starting transfers between devices: 32.9 us -> 31.3 us
    pallas_call x6, Pallas kernels: 42.3 us -> 28.2 us  [call(): pl.pallas_call(kernel, in_specs=[there if i in far_in else here for i in...]
    all_to_all x3, waiting for transfers between devices: 5.37 us -> 9.27 us  [exchange(): return lax.all_to_all(parts, axes, 0, 0, tiled=True)]
    all_to_all x3, blocking collectives: 33.3 us -> 29.9 us  [exchange(): return lax.all_to_all(parts, axes, 0, 0, tiled=True)]
    unnamed x12 -> x28, local copies, waits for them, and re-layouts: 2.03 us -> 0.07 us
    all_to_all x3, starting transfers between devices: 16.6 us -> 14.8 us  [exchange(): return lax.all_to_all(parts, axes, 0, 0, tiled=True)]
    ppermute x6, waiting for transfers between devices: 3.56 us -> 4.92 us  [pass_on(): return (lax.ppermute(high, axis, up), lax.ppermute(low, axis, down))]
  transfers between devices with their start and end apart: 9 -> 9, of which waited for: 3 -> 5; matrix products, arithmetic and copies ran while one was open for 7% -> 5% of each run, Pallas kernels for 5% -> 5%
where the time goes in v5:
time: 115 us; the launch traced here: 114 us
  starting transfers between devices  31.3 us (27%)
  blocking collectives  29.9 us (26%)
  Pallas kernels  28.2 us (25%)
  waiting for transfers between devices  14.2 us (12%)
  local copies, waits for them, and re-layouts  6 us (5%)
  other arithmetic  3.31 us (3%)
    all_to_all x3, blocking collectives, exchange(): return lax.all_to_all(parts, axes, 0, 0, tiled=True)  29.9 us
    pallas_call x6, Pallas kernels, call(): pl.pallas_call(kernel, in_specs=[there if i in far_in else here for i in...  28.2 us
    ppermute x6, starting transfers between devices, pass_on(): return (lax.ppermute(high, axis, up), lax.ppermute(low, axis, down))  16.5 us
    all_to_all x3, starting transfers between devices, exchange(): return lax.all_to_all(parts, axes, 0, 0, tiled=True)  14.8 us
    all_to_all x3, waiting for transfers between devices, exchange(): return lax.all_to_all(parts, axes, 0, 0, tiled=True)  9.27 us
    ppermute x6, waiting for transfers between devices, pass_on(): return (lax.ppermute(high, axis, up), lax.ppermute(low, axis, down))  4.92 us
  transfers between devices with their start and end apart: 9, of which 5 were waited for; matrix products, arithmetic and copies ran while one was open for 5% of the time, Pallas kernels for 5%

profile of v5, /device:TPU:1, one launch (start us, length us, event | category | flops | bytes accessed | tf_op | source)
XLA Modules:
  0.0 114.0 jit_solution(1226001834876790919)
XLA Ops:
  0.6 0.0 copy-start.11
  0.6 0.7 convert_bitcast_fusion
  1.3 0.1 broadcast_in_dim.23
  1.4 0.1 convert_element_type.41
  1.5 1.0 fusion.3
  2.5 0.1 fusion
  2.6 2.0 %collective-permute-start.1 = (bf16[32,16,128]{2,0,1:T(8,128)(2,1)S(1)}, bf16[32,16,128]{2,0,1:T(8,128)(2,1)S(1)}, u32[]{:S(2)}, u32[]{:S(2)}) collective-permute-start(bf16[32,16,128]{2,0,1:T(8,128)(2,1)S(1)} %get-tuple-element.51), channel_id=1, source_target_pairs={{8,0},{16,8},{24,16},{9,1},{17,9},{25,17},{10,2},{18,10},{26,18},{... | collective-permute-start | bytes 393224 | tf_op jit(solution)/shard_map/ppermute | solution.py:395
  4.6 4.5 %collective-permute-start = (bf16[32,16,128]{2,0,1:T(8,128)(2,1)S(1)}, bf16[32,16,128]{2,0,1:T(8,128)(2,1)S(1)}, u32[]{:S(2)}, u32[]{:S(2)}) collective-permute-start(bf16[32,16,128]{2,0,1:T(8,128)(2,1)S(1)} %get-tuple-element.52), channel_id=1, source_target_pairs={{0,8},{8,16},{16,24},{1,9},{9,17},{17,25},{2,10},{10,18},{18,26},{... | collective-permute-start | bytes 393224 | tf_op jit(solution)/shard_map/ppermute | solution.py:395
  9.1 0.9 shift-right-arithmetic_convert_fusion
  9.9 1.5 %multiply_bitcast_fusion = (bf16[8,2,32,128]{3,1,2,0:T(2,128)(2,1)S(1)}, bf16[8,2,32,128]{3,1,2,0:T(2,128)(2,1)S(1)}) fusion(bf16[8,32,16,128]{3,2,1,0:T(8,128)(2,1)} %feat.1, bf16[2,128]{1,0:T(2,128)(2,1)S(1)} %get-tuple-element.47, bf16[2,128]{1,0:T(2,128)(2,1)S(1)} %get-tuple-element.48), kind=kLoop, calls=%fused_computation.7 | loop fusion | flops 131072 | bytes 525312 | tf_op jit(solution)/shard_map/transpose | solution.py:434
  11.5 0.1 pad.18.clone
  11.6 0.1 maximum_bitcast_fusion.1
  11.7 0.0 collective-permute-done.1
  11.7 0.0 copy-start
  11.7 0.0 copy-start.1
  11.7 0.0 collective-permute-done
  11.8 3.3 %collective-permute-start.2 = (bf16[21,32,128]{2,1,0:T(8,128)(2,1)S(1)}, bf16[21,32,128]{2,1,0:T(8,128)(2,1)S(1)}, u32[]{:S(2)}, u32[]{:S(2)}) collective-permute-start(bf16[21,32,128]{2,1,0:T(8,128)(2,1)S(1)} %pad_maximum_fusion), channel_id=1, source_target_pairs={{0,1},{1,2},{2,3},{3,4},{4,5},{5,6},{6,7},{8,9},{9,10},{10,11},{11... | collective-permute-start | bytes 516104 | tf_op jit(solution)/shard_map/ppermute | solution.py:395
  15.1 1.3 %collective-permute-start.3 = (bf16[21,32,128]{2,1,0:T(8,128)(2,1)S(1)}, bf16[21,32,128]{2,1,0:T(8,128)(2,1)S(1)}, u32[]{:S(2)}, u32[]{:S(2)}) collective-permute-start(bf16[21,32,128]{2,1,0:T(8,128)(2,1)S(1)} %pad_maximum_fusion.1), channel_id=1, source_target_pairs={{1,0},{2,1},{3,2},{4,3},{5,4},{6,5},{7,6},{9,8},{10,9},{11,10},{12... | collective-permute-start | bytes 516104 | tf_op jit(solution)/shard_map/ppermute | solution.py:395
  16.4 0.1 broadcast_in_dim.27
  16.5 0.1 convert_element_type.48.lanes
  16.5 0.0 copy-done.11
  16.6 0.2 reshape.89
  16.8 0.7 rev.3
  17.5 0.1 copy.41
  17.6 0.2 reshape.90.weight
  17.8 0.2 copy.42
  18.0 0.2 reshape.91._.weight
  18.2 0.1 copy.44.x_high
  18.3 0.1 copy.43.x_low
  18.3 0.8 collective-permute-done.2.y_low
  19.1 4.1 %collective-permute-done.3.y_high = bf16[21,32,128]{2,1,0:T(8,128)(2,1)S(1)} collective-permute-done((bf16[21,32,128]{2,1,0:T(8,128)(2,1)S(1)}, bf16[21,32,128]{2,1,0:T(8,128)(2,1)S(1)}, u32[]{:S(2)}, u32[]{:S(2)}) %collective-permute-start.3) | collective-permute-done | bytes 172064 | tf_op jit(solution)/shard_map/ppermute | solution.py:395
  23.2 0.0 copy-done
  23.2 0.0 copy-done.1
  23.2 10.6 %shard_map.121 = (bf16[10,20,96,128]{3,2,1,0:T(8,128)(2,1)S(1)}, bf16[8,32,2304]{2,1,0:T(8,128)(2,1)S(1)}, bf16[8,48,256]{2,1,0:T(8,128)(2,1)S(1)}, f32[2,32,128]{2,1,0:T(8,128)S(1)}) custom-call(bf16[8,32,16,128]{3,2,1,0:T(8,128)(2,1)S(1)} %copy-done, bf16[32,16,128]{2,1,0:T(8,128)(2,1)S(1)} %copy.43.x_low, bf16[32,16,128]{2,1,0:T(8,128)(2,1)S(1)} %copy.44.x_high, ...), custom_call_target="tpu_custom_call" | custom-call | flops 12000000000 | bytes 36000000 | tf_op jit(solution)/shard_map/pallas_call | solution.py:380
  33.8 0.0 copy-start.8
  33.8 0.0 copy-start.9
  33.8 12.6 %all_to_all.34.parts = bf16[8,48,256]{2,1,0:T(8,128)(2,1)S(1)} all-to-all(bf16[8,48,256]{2,1,0:T(8,128)(2,1)S(1)} %get-tuple-element.17), channel_id=1, replica_groups=mesh['drift'=4,'beam'=8] {'beam'}, dimensions={0} | all-to-all | bytes 393216 | tf_op jit(solution)/shard_map/all_to_all | solution.py:399
  46.5 0.0 copy-start.6
  46.5 0.0 copy-start.7
  46.5 0.7 shard_map.122
  47.2 4.0 %all-to-all-start.1 = ((bf16[8,32,256]{2,1,0:T(8,128)(2,1)}), bf16[8,32,256]{2,1,0:T(8,128)(2,1)S(1)}, u32[]{:S(2)}, u32[]{:S(2)}) async-start(bf16[8,32,256]{2,1,0:T(8,128)(2,1)} %get-tuple-element.18), calls=%async_computation.1 | async-start | bytes 262144 | tf_op jit(solution)/shard_map/all_to_all | solution.py:399
  51.2 0.7 slice_bitcast_fusion.6.mine
  52.0 5.5 %all-to-all-done.1.table = bf16[8,32,256]{2,1,0:T(8,128)(2,1)S(1)} async-done(((bf16[8,32,256]{2,1,0:T(8,128)(2,1)}), bf16[8,32,256]{2,1,0:T(8,128)(2,1)S(1)}, u32[]{:S(2)}, u32[]{:S(2)}) %all-to-all-start.1) | async-done | bytes 131104 | tf_op jit(solution)/shard_map/all_to_all | solution.py:399
  57.4 0.0 copy-done.3
  57.5 0.0 slice-start
  57.5 2.9 %shard_map.123 = (bf16[256,256]{1,0:T(8,128)(2,1)}, bf16[8,32,256]{2,1,0:T(8,128)(2,1)S(1)}, f32[32,256]{1,0:T(8,128)S(1)}) custom-call(bf16[8,32,256]{2,1,0:T(8,128)(2,1)S(1)} %all-to-all-done.1.table, bf16[32,256]{1,0:T(8,128)(2,1)S(1)} %slice_bitcast_fusion.6.mine, bf16[32,256]{1,0:T(8,128)(2,1)S(1)} %copy-done.5, bf16[256,256]{1,0:T(8,128)(2,1)S(1)} %copy-done.2, ...), custom_call_target="tpu_custom_call" | custom-call | flops 2000000000 | bytes 6000000 | tf_op jit(solution)/shard_map/pallas_call | solution.py:380
  60.3 8.6 %all_to_all.35.parts = bf16[8,32,256]{2,1,0:T(8,128)(2,1)S(1)} all-to-all(bf16[8,32,256]{2,1,0:T(8,128)(2,1)S(1)} %get-tuple-element.20), channel_id=1, replica_groups=mesh['drift'=4,'beam'=8] {'beam'}, dimensions={0} | all-to-all | bytes 262144 | tf_op jit(solution)/shard_map/all_to_all | solution.py:399
  69.0 8.7 %all_to_all.36.table = bf16[8,32,256]{2,1,0:T(8,128)(2,1)S(1)} all-to-all(bf16[8,32,256]{2,1,0:T(8,128)(2,1)S(1)} %shard_map.124), channel_id=1, replica_groups=mesh['drift'=4,'beam'=8] {'beam'}, dimensions={0} | all-to-all | bytes 262144 | tf_op jit(solution)/shard_map/all_to_all | solution.py:399
  77.7 0.0 slice-done
  77.7 8.0 %shard_map.125 = (bf16[8,32,2048]{2,1,0:T(8,128)(2,1)S(1)}, bf16[8,18,32,128]{3,2,1,0:T(8,128)(2,1)S(1)}, bf16[18,32,128]{2,1,0:T(8,128)(2,1)S(1)}, bf16[18,32,128]{2,1,0:T(8,128)(2,1)S(1)}, f32[256,128]{1,0:T(8,128)}) custom-call(bf16[8,32,256]{2,1,0:T(8,128)(2,1)S(1)} %all_to_all.36.table, s32[8,16,128]{2,1,0:T(8,128)S(1)} %copy-done.1, ...), custom_call_target="tpu_custom_call" | custom-call | flops 14000000000 | bytes 42000000 | tf_op jit(solution)/shard_map/pallas_call | solution.py:380
  85.7 7.0 %all-to-all-start.4 = ((f32[32,8,128]{2,1,0:T(8,128)}), f32[32,8,128]{2,1,0:T(8,128)S(1)}, u32[]{:S(2)}, u32[]{:S(2)}) async-start(f32[32,8,128]{2,1,0:T(8,128)} %bitcast.26), calls=%async_computation.4 | async-start | bytes 262144 | tf_op jit(solution)/shard_map/all_to_all | solution.py:399
  92.7 3.5 %collective-permute-start.4 = (bf16[18,32,128]{2,1,0:T(8,128)(2,1)S(1)}, bf16[18,32,128]{2,1,0:T(8,128)(2,1)S(1)}, u32[]{:S(2)}, u32[]{:S(2)}) collective-permute-start(bf16[18,32,128]{2,1,0:T(8,128)(2,1)S(1)} %get-tuple-element.27), channel_id=1, source_target_pairs={{0,8},{8,16},{16,24},{1,9},{9,17},{17,25},{2,10},{10,18},{18,26},{... | collective-permute-start | bytes 442376 | tf_op jit(solution)/shard_map/ppermute | solution.py:395
  96.2 1.9 %collective-permute-start.5 = (bf16[18,32,128]{2,1,0:T(8,128)(2,1)S(1)}, bf16[18,32,128]{2,1,0:T(8,128)(2,1)S(1)}, u32[]{:S(2)}, u32[]{:S(2)}) collective-permute-start(bf16[18,32,128]{2,1,0:T(8,128)(2,1)S(1)} %get-tuple-element.28), channel_id=1, source_target_pairs={{8,0},{16,8},{24,16},{9,1},{17,9},{25,17},{10,2},{18,10},{26,18},{... | collective-permute-start | bytes 442376 | tf_op jit(solution)/shard_map/ppermute | solution.py:395
  98.2 2.3 %all-to-all-done.4 = f32[32,8,128]{2,1,0:T(8,128)S(1)} async-done(((f32[32,8,128]{2,1,0:T(8,128)}), f32[32,8,128]{2,1,0:T(8,128)S(1)}, u32[]{:S(2)}, u32[]{:S(2)}) %all-to-all-start.4) | async-done | bytes 131104 | tf_op jit(solution)/shard_map/all_to_all | solution.py:399
  100.4 0.7 broadcast_in_dim.28
  101.1 3.8 %all-to-all-start.5 = ((f32[32,8,128]{2,1,0:T(8,128)}), f32[32,8,128]{2,1,0:T(8,128)S(1)}, u32[]{:S(2)}, u32[]{:S(2)}) async-start(f32[32,8,128]{2,1,0:T(8,128)} %broadcast_in_dim.28), calls=%async_computation.5 | async-start | bytes 262144 | tf_op jit(solution)/shard_map/all_to_all | solution.py:399
  104.9 0.0 collective-permute-done.4.x_low
  104.9 0.0 collective-permute-done.5.x_high
  105.0 6.0 %shard_map.126 = f32[8,32,16,128]{3,2,1,0:T(8,128)} custom-call(bf16[8,18,32,128]{3,2,1,0:T(8,128)(2,1)S(1)} %get-tuple-element.26.back_conv, bf16[18,32,128]{2,1,0:T(8,128)(2,1)S(1)} %collective-permute-done.4.x_low, bf16[18,32,128]{2,1,0:T(8,128)(2,1)S(1)} %collective-permute-done.5.x_high, bf16[8,32,2048]{2,1,0:T(8,128)(2,1)S(1)} %get-tuple-element.29.back_hidden, ...), custom_call_target="tpu_custom_call" | custom-call | flops 10000000000 | bytes 30000000 | tf_op jit(solution)/shard_map/pallas_call | solution.py:380
  111.0 1.5 %all-to-all-done.5 = f32[32,8,128]{2,1,0:T(8,128)S(1)} async-done(((f32[32,8,128]{2,1,0:T(8,128)}), f32[32,8,128]{2,1,0:T(8,128)S(1)}, u32[]{:S(2)}, u32[]{:S(2)}) %all-to-all-start.5) | async-done | bytes 131104 | tf_op jit(solution)/shard_map/all_to_all | solution.py:399
  112.5 0.1 reshape.94
  112.7 0.2 reshape.96
  112.9 0.1 copy.47
  113.0 0.9 reshape.97
  (35 shorter events, 0.3 us)
Async XLA Ops:
  0.6 15.9 %copy-start.11 = (bf16[32,864]{1,0:T(8,128)(2,1)S(1)}, bf16[32,864]{1,0:T(8,128)(2,1)}, u32[]{:S(2)}) copy-start(bf16[32,864]{1,0:T(8,128)(2,1)} %param.13) | copy-start | bytes 165892
  2.6 9.1 %collective-permute-start.1 = (bf16[32,16,128]{2,0,1:T(8,128)(2,1)S(1)}, bf16[32,16,128]{2,0,1:T(8,128)(2,1)S(1)}, u32[]{:S(2)}, u32[]{:S(2)}) collective-permute-start(bf16[32,16,128]{2,0,1:T(8,128)(2,1)S(1)} %get-tuple-element.51), channel_id=1, source_target_pairs={{8,0},{16,8},{24,16},{9,1},{17,9},{25,17},{10,2},{18,10},{26,18},{... | collective-permute-start | bytes 393224 | tf_op jit(solution)/shard_map/ppermute | solution.py:395
  4.6 7.1 %collective-permute-start = (bf16[32,16,128]{2,0,1:T(8,128)(2,1)S(1)}, bf16[32,16,128]{2,0,1:T(8,128)(2,1)S(1)}, u32[]{:S(2)}, u32[]{:S(2)}) collective-permute-start(bf16[32,16,128]{2,0,1:T(8,128)(2,1)S(1)} %get-tuple-element.52), channel_id=1, source_target_pairs={{0,8},{8,16},{16,24},{1,9},{9,17},{17,25},{2,10},{10,18},{18,26},{... | collective-permute-start | bytes 393224 | tf_op jit(solution)/shard_map/ppermute | solution.py:395
  11.7 11.6 %copy-start = (bf16[8,32,16,128]{3,2,1,0:T(8,128)(2,1)S(1)}, bf16[8,32,16,128]{3,2,1,0:T(8,128)(2,1)}, u32[]{:S(2)}) copy-start(bf16[8,32,16,128]{3,2,1,0:T(8,128)(2,1)} %feat.1) | copy-start | bytes 3145732
  11.7 11.6 %copy-start.1 = (s32[8,16,128]{2,1,0:T(8,128)S(1)}, s32[8,16,128]{2,1,0:T(8,128)}, u32[]{:S(2)}) copy-start(s32[8,16,128]{2,1,0:T(8,128)} %fragment.3) | copy-start | bytes 196612
  11.8 7.4 %collective-permute-start.2 = (bf16[21,32,128]{2,1,0:T(8,128)(2,1)S(1)}, bf16[21,32,128]{2,1,0:T(8,128)(2,1)S(1)}, u32[]{:S(2)}, u32[]{:S(2)}) collective-permute-start(bf16[21,32,128]{2,1,0:T(8,128)(2,1)S(1)} %pad_maximum_fusion), channel_id=1, source_target_pairs={{0,1},{1,2},{2,3},{3,4},{4,5},{5,6},{6,7},{8,9},{9,10},{10,11},{11... | collective-permute-start | bytes 516104 | tf_op jit(solution)/shard_map/ppermute | solution.py:395
  15.1 8.1 %collective-permute-start.3 = (bf16[21,32,128]{2,1,0:T(8,128)(2,1)S(1)}, bf16[21,32,128]{2,1,0:T(8,128)(2,1)S(1)}, u32[]{:S(2)}, u32[]{:S(2)}) collective-permute-start(bf16[21,32,128]{2,1,0:T(8,128)(2,1)S(1)} %pad_maximum_fusion.1), channel_id=1, source_target_pairs={{1,0},{2,1},{3,2},{4,3},{5,4},{6,5},{7,6},{9,8},{10,9},{11,10},{12... | collective-permute-start | bytes 516104 | tf_op jit(solution)/shard_map/ppermute | solution.py:395
  33.8 13.4 %copy-start.8 = (bf16[10,20,96,128]{3,2,1,0:T(8,128)(2,1)}, bf16[10,20,96,128]{3,2,1,0:T(8,128)(2,1)S(1)}, u32[]{:S(2)}) copy-start(bf16[10,20,96,128]{3,2,1,0:T(8,128)(2,1)S(1)} %get-tuple-element.25.taps) | copy-start | bytes 14745604
  33.8 13.4 %copy-start.9 = (bf16[8,32,2304]{2,1,0:T(8,128)(2,1)}, bf16[8,32,2304]{2,1,0:T(8,128)(2,1)S(1)}, u32[]{:S(2)}) copy-start(bf16[8,32,2304]{2,1,0:T(8,128)(2,1)S(1)} %get-tuple-element.24.slopes) | copy-start | bytes 3538948
  46.5 11.0 %copy-start.2 = (bf16[256,256]{1,0:T(8,128)(2,1)S(1)}, bf16[256,256]{1,0:T(8,128)(2,1)}, u32[]{:S(2)}) copy-start(bf16[256,256]{1,0:T(8,128)(2,1)} %message.1) | copy-start | bytes 393220
  46.5 11.0 %copy-start.3 = (bf16[256,256]{1,0:T(8,128)(2,1)S(1)}, bf16[256,256]{1,0:T(8,128)(2,1)}, u32[]{:S(2)}) copy-start(bf16[256,256]{1,0:T(8,128)(2,1)} %update.1) | copy-start | bytes 393220
  46.5 11.0 %copy-start.4 = (bf16[256,256]{1,0:T(8,128)(2,1)S(1)}, bf16[256,256]{1,0:T(8,128)(2,1)}, u32[]{:S(2)}) copy-start(bf16[256,256]{1,0:T(8,128)(2,1)} %cotangent.1) | copy-start | bytes 393220
  46.5 11.0 %copy-start.5 = (bf16[32,256]{1,0:T(8,128)(2,1)S(1)}, bf16[32,256]{1,0:T(8,128)(2,1)}, u32[]{:S(2)}) copy-start(bf16[32,256]{1,0:T(8,128)(2,1)} %embed.1) | copy-start | bytes 49156
  46.5 11.0 %copy-start.6 = (s32[1024]{0:T(1024)S(1)}, s32[1024]{0:T(1024)}, u32[]{:S(2)}) copy-start(s32[1024]{0:T(1024)} %param.17) | copy-start | bytes 12292
  46.5 11.0 %copy-start.7 = (s32[1024]{0:T(1024)S(1)}, s32[1024]{0:T(1024)}, u32[]{:S(2)}) copy-start(s32[1024]{0:T(1024)} %param.18) | copy-start | bytes 12292
  47.2 10.2 %all-to-all-start.1 = ((bf16[8,32,256]{2,1,0:T(8,128)(2,1)}), bf16[8,32,256]{2,1,0:T(8,128)(2,1)S(1)}, u32[]{:S(2)}, u32[]{:S(2)}) async-start(bf16[8,32,256]{2,1,0:T(8,128)(2,1)} %get-tuple-element.18), calls=%async_computation.1 | async-start | bytes 262144 | tf_op jit(solution)/shard_map/all_to_all | solution.py:399
  57.5 20.2 %slice-start = ((s8[4915200]{0:T(1024)(128)(4,1)}), s8[4194304]{0:T(1024)(128)(4,1)S(1)}, s32[]{:S(2)}) async-start(s8[4915200]{0:T(1024)(128)(4,1)} %bitcast.60), calls=%async_computation.6 | async-start | bytes 8388608
  68.9 8.8 %slice-start.1 = ((s8[4915200]{0:T(1024)(128)(4,1)}), s8[720896]{0:T(1024)(128)(4,1)S(1)}, s32[]{:S(2)}) async-start(s8[4915200]{0:T(1024)(128)(4,1)} %bitcast.60), calls=%async_computation.7 | async-start | bytes 1441792
  68.9 8.8 %copy-start.10 = (bf16[8,32,2304]{2,1,0:T(8,128)(2,1)S(1)}, bf16[8,32,2304]{2,1,0:T(8,128)(2,1)}, u32[]{:S(2)}) copy-start(bf16[8,32,2304]{2,1,0:T(8,128)(2,1)} %copy-done.9) | copy-start | bytes 3538948
  85.7 14.7 %all-to-all-start.4 = ((f32[32,8,128]{2,1,0:T(8,128)}), f32[32,8,128]{2,1,0:T(8,128)S(1)}, u32[]{:S(2)}, u32[]{:S(2)}) async-start(f32[32,8,128]{2,1,0:T(8,128)} %bitcast.26), calls=%async_computation.4 | async-start | bytes 262144 | tf_op jit(solution)/shard_map/all_to_all | solution.py:399
  92.7 12.3 %collective-permute-start.4 = (bf16[18,32,128]{2,1,0:T(8,128)(2,1)S(1)}, bf16[18,32,128]{2,1,0:T(8,128)(2,1)S(1)}, u32[]{:S(2)}, u32[]{:S(2)}) collective-permute-start(bf16[18,32,128]{2,1,0:T(8,128)(2,1)S(1)} %get-tuple-element.27), channel_id=1, source_target_pairs={{0,8},{8,16},{16,24},{1,9},{9,17},{17,25},{2,10},{10,18},{18,26},{... | collective-permute-start | bytes 442376 | tf_op jit(solution)/shard_map/ppermute | solution.py:395
  96.2 8.7 %collective-permute-start.5 = (bf16[18,32,128]{2,1,0:T(8,128)(2,1)S(1)}, bf16[18,32,128]{2,1,0:T(8,128)(2,1)S(1)}, u32[]{:S(2)}, u32[]{:S(2)}) collective-permute-start(bf16[18,32,128]{2,1,0:T(8,128)(2,1)S(1)} %get-tuple-element.28), channel_id=1, source_target_pairs={{8,0},{16,8},{24,16},{9,1},{17,9},{25,17},{10,2},{18,10},{26,18},{... | collective-permute-start | bytes 442376 | tf_op jit(solution)/shard_map/ppermute | solution.py:395
  101.1 11.4 %all-to-all-start.5 = ((f32[32,8,128]{2,1,0:T(8,128)}), f32[32,8,128]{2,1,0:T(8,128)S(1)}, u32[]{:S(2)}, u32[]{:S(2)}) async-start(f32[32,8,128]{2,1,0:T(8,128)} %broadcast_in_dim.28), calls=%async_computation.5 | async-start | bytes 262144 | tf_op jit(solution)/shard_map/all_to_all | solution.py:399

commit v6 on v5

--- a/solution.py
+++ b/solution.py
@@ -14,7 +14,7 @@
 LANES = 128
 SUBLANES = 8
 DIGIT = 128.0
-LIMIT = 32 * 1024 * 1024
+LIMIT = 24 * 1024 * 1024
 bf16 = jnp.bfloat16
 f32 = jnp.float32
 
@@ -102,15 +102,22 @@
     lax.fori_loop(0, rows, step, 0)
 
 
+def tap(taps, row, y):
+    for part in taps:
+        if y < part.shape[1]:
+            return part[row, y]
+        y -= part.shape[1]
+
+
 def columns(taps, row, first, count):
     wide = []
     for y in range(first, first + count):
-        wide.append(jnp.concatenate([taps[row + a, y] for a in range(REACH)], 0))
+        wide.append(jnp.concatenate([tap(taps, row + a, y) for a in range(REACH)], 0))
     return jnp.concatenate(wide, 1)
 
 
 def convolve_row(taps, weight, row, height):
-    depth = taps.shape[-1]
+    depth = taps[0].shape[-1]
     channels = weight.shape[0] // REACH
     wide = height * depth
     found = jnp.concatenate(
@@ -123,38 +130,45 @@
     return total
 
 
-def forward_kernel(
-    feat, x_low, x_high, y_low, y_high, lanes, fragment, weight, _, taps, slopes, partial,
-    sides, total, rims, rims_here
-):
+def inner_kernel(feat, x_low, x_high, lanes, core):
     rows, channels, height, depth = feat.shape
-    owners, _, frag_dev = partial.shape
 
     def turned(block):
         return jnp.swapaxes(block.astype(f32), 0, 1)
 
-    get_low = pltpu.make_async_copy(y_low, rims.at[0], rims_here.at[0])
-    get_high = pltpu.make_async_copy(y_high, rims.at[1], rims_here.at[1])
-    get_low.start()
-    get_high.start()
-    store_taps(taps, 0, RIM, turned(x_low[...]).astype(bf16))
-    store_taps(taps, rows + 1, RIM, turned(x_high[...]).astype(bf16))
+    store_taps(core, 0, 0, turned(x_low[...]).astype(bf16))
+    store_taps(core, rows + 1, 0, turned(x_high[...]).astype(bf16))
 
     def fill(x, _):
         tiles = turned(feat[x])
         live = live_line(lanes, x, height)
         gates = [live[:, y * depth : (y + 1) * depth] for y in range(height)]
         gates = jnp.concatenate([jnp.broadcast_to(g, (1, channels, depth)) for g in gates], 0)
-        store_taps(taps, x + 1, RIM, (tiles * gates).astype(bf16))
+        store_taps(core, x + 1, 0, (tiles * gates).astype(bf16))
         return 0
 
     lax.fori_loop(0, rows, fill, 0)
+
+
+def forward_kernel(
+    core, y_low, y_high, lanes, fragment, weight, low, high, slopes, partial,
+    sides, total, rims, rims_here
+):
+    owners, _, frag_dev = partial.shape
+    height = core.shape[1]
+    rows, channels, wide = slopes.shape
+    depth = wide // (height + 2)
+    taps = (low, core, high)
+    get_low = pltpu.make_async_copy(y_low, rims.at[0], rims_here.at[0])
+    get_high = pltpu.make_async_copy(y_high, rims.at[1], rims_here.at[1])
+    get_low.start()
+    get_high.start()
     get_low.wait()
     get_high.wait()
 
     def edges(x, _):
-        store_taps(taps, x, 0, rims[0, pl.ds(RIM * x, RIM)])
-        store_taps(taps, x, height + RIM, rims[1, pl.ds(RIM * x, RIM)])
+        store_taps(low, x, 0, rims[0, pl.ds(RIM * x, RIM)])
+        store_taps(high, x, 0, rims[1, pl.ds(RIM * x, RIM)])
         return 0
 
     lax.fori_loop(0, rows + 2, edges, 0)
@@ -165,7 +179,7 @@
     def one_row(x, _):
         wide = convolve_row(taps, weight[...], x, height + 2)
         active = jnp.concatenate(
-            [taps[x + 1, y + RIM, channels : 2 * channels, :] for y in range(height)], 1
+            [core[x + 1, y, channels : 2 * channels, :] for y in range(height)], 1
         )
         live = live_line(lanes, x, height)
         owner, local = owner_and_local(line_of(fragment[x]), frag_dev)
@@ -214,7 +228,7 @@
 
 
 def fragment_kernel(
-    table, mine, embed, message, update, cotangent, edge_from, target, out, partial, direct
+    table, mine, embed, message, update, cotangent, edge_from, target, _, out, partial, direct
 ):
     owners, channels, frag_dev = table.shape
     flat = table[...].reshape(owners * channels, frag_dev)
@@ -256,12 +270,13 @@
 
 
 def hidden_kernel(
-    table, fragment, lanes, sides, slopes, taps,
+    table, fragment, lanes, sides, slopes, low, core, high,
     back_hidden, back_conv, face_low, face_high, packed, grad
 ):
     owners, channels, frag_dev = table.shape
     rows, wide_height, _, depth = back_conv.shape
     height = wide_height - 2
+    taps = (low, core, high)
     flat = table[...].reshape(owners * channels, frag_dev)
     empty = jnp.zeros((channels, depth), bf16)
     grad[...] = jnp.zeros_like(grad)
@@ -358,7 +373,7 @@
 
     def one_row(x, _):
         live = live_line(lanes, x, height)
-        found = convolve_row(taps, weight[...], x, height)
+        found = convolve_row((taps,), weight[...], x, height)
         result = live * (back_hidden[x].astype(f32) + found)
         tiles = [result[:, y * depth : (y + 1) * depth][None] for y in range(height)]
         grad[x] = jnp.swapaxes(jnp.concatenate(tiles, 0), 0, 1)
@@ -447,21 +462,26 @@
     conv_shape = (rows, height + 2, channels, depth)
     dma = lambda count: pltpu.SemaphoreType.DMA((count,))
     tapped = (rows + 2, height + 2, REACH * channels, depth)
-    padded = (rows + 2, height + 2 * RIM, REACH * channels, depth)
-    taps, slopes, partial, sides = call(
+    inner_shape = (rows + 2, height, REACH * channels, depth)
+    rim_shape = (rows + 2, RIM, REACH * channels, depth)
+    (core,) = call(
+        inner_kernel, [(inner_shape, bf16)], features, x_low, x_high, lanes, micros=3
+    )
+    low, high, slopes, partial, sides = call(
         forward_kernel,
         [
-            (padded, bf16),
+            (rim_shape, bf16),
+            (rim_shape, bf16),
             (wide_shape, bf16),
             ((owners, channels + SPARE, frag_dev), bf16),
             ((2, channels, depth), f32),
         ],
-        features, x_low, x_high, y_low, y_high, lanes, voxel_fragment, stacked, flipped, micros=12,
+        core, y_low, y_high, lanes, voxel_fragment, stacked, micros=9,
         scratch=[
             pltpu.VMEM((owners * channels + heads, frag_dev), f32),
             pltpu.VMEM((2,) + y_low.shape, bf16), dma(2),
         ],
-        far_in=(3, 4, 8),
+        far_in=(1, 2),
     )
     spread_shape = (owners, channels, frag_dev)
     pooled, divisor = call(
@@ -475,7 +495,7 @@
         [((frag_dev, hid), bf16), (spread_shape, bf16), ((channels, frag_dev), f32)],
         table, pooled[0], embed_weight, message_weight, update_weight, out_cotangent,
         edge_source.reshape(1, edge_count),
-        edge_target.reshape(1, edge_count),
+        edge_target.reshape(1, edge_count), flipped, far_in=(8,),
     )
     (mean,) = call(
         mean_kernel, [(spread_shape, bf16)], exchange(back_parts, "beam"), direct, divisor
@@ -490,7 +510,7 @@
             (line_shape, bf16), (conv_shape, bf16), (conv_shape[1:], bf16), (conv_shape[1:], bf16),
             ((devices * share, LANES), f32),
         ],
-        exchange(mean, "beam"), voxel_fragment, lanes, sides, slopes, taps, micros=14,
+        exchange(mean, "beam"), voxel_fragment, lanes, sides, slopes, low, core, high, micros=9,
         scratch=[pltpu.VMEM(stacked_shape[::-1], f32)],
     )
     gx_low, gx_high = pass_on(face_low, face_high, "drift")

time: 115 us -> 115 us (level)
  waiting for transfers between devices: 14.2 us -> 11.9 us
  local copies, waits for them, and re-layouts: 6 us -> 8.18 us
    all_to_all x3, waiting for transfers between devices: 9.27 us -> 6.95 us  [exchange(): return lax.all_to_all(parts, axes, 0, 0, tiled=True)]
    unnamed x28 -> x34, local copies, waits for them, and re-layouts: 0.07 us -> 2.26 us
    pallas_call x6 -> x7, Pallas kernels: 28.2 us -> 28.3 us  [call(): pl.pallas_call(kernel, in_specs=[there if i in far_in else here for i in...]
  transfers between devices with their start and end apart: 9 -> 9, of which waited for: 5 -> 5; matrix products, arithmetic and copies ran while one was open for 5% -> 5% of each run, Pallas kernels for 5% -> 7%
where the time goes in v6:
time: 115 us; the launch traced here: 114 us
  starting transfers between devices  31.3 us (27%)
  blocking collectives  30.1 us (26%)
  Pallas kernels  28.3 us (25%)
  waiting for transfers between devices  11.9 us (10%)
  local copies, waits for them, and re-layouts  8.18 us (7%)
  other arithmetic  3.31 us (3%)
    all_to_all x3, blocking collectives, exchange(): return lax.all_to_all(parts, axes, 0, 0, tiled=True)  30.1 us
    pallas_call x7, Pallas kernels, call(): pl.pallas_call(kernel, in_specs=[there if i in far_in else here for i in...  28.3 us
    ppermute x6, starting transfers between devices, pass_on(): return (lax.ppermute(high, axis, up), lax.ppermute(low, axis, down))  16.5 us
    all_to_all x3, starting transfers between devices, exchange(): return lax.all_to_all(parts, axes, 0, 0, tiled=True)  14.8 us
    all_to_all x3, waiting for transfers between devices, exchange(): return lax.all_to_all(parts, axes, 0, 0, tiled=True)  6.95 us
    ppermute x6, waiting for transfers between devices, pass_on(): return (lax.ppermute(high, axis, up), lax.ppermute(low, axis, down))  4.97 us
  transfers between devices with their start and end apart: 9, of which 5 were waited for; matrix products, arithmetic and copies ran while one was open for 5% of the time, Pallas kernels for 7%

profile of v6, /device:TPU:1, one launch (start us, length us, event | category | flops | bytes accessed | tf_op | source)
XLA Modules:
  0.0 114.1 jit_solution(14459643107721598602)
XLA Ops:
  0.6 0.7 convert_bitcast_fusion
  1.3 0.1 broadcast_in_dim.23
  1.4 0.1 convert_element_type.41
  1.5 1.0 fusion.3
  2.5 0.1 fusion
  2.6 0.0 copy-start
  2.6 2.1 %collective-permute-start.1 = (bf16[32,16,128]{2,0,1:T(8,128)(2,1)S(1)}, bf16[32,16,128]{2,0,1:T(8,128)(2,1)S(1)}, u32[]{:S(2)}, u32[]{:S(2)}) collective-permute-start(bf16[32,16,128]{2,0,1:T(8,128)(2,1)S(1)} %get-tuple-element.53), channel_id=1, source_target_pairs={{8,0},{16,8},{24,16},{9,1},{17,9},{25,17},{10,2},{18,10},{26,18},{... | collective-permute-start | bytes 393224 | tf_op jit(solution)/shard_map/ppermute | solution.py:410
  4.7 4.5 %collective-permute-start = (bf16[32,16,128]{2,0,1:T(8,128)(2,1)S(1)}, bf16[32,16,128]{2,0,1:T(8,128)(2,1)S(1)}, u32[]{:S(2)}, u32[]{:S(2)}) collective-permute-start(bf16[32,16,128]{2,0,1:T(8,128)(2,1)S(1)} %get-tuple-element.54), channel_id=1, source_target_pairs={{0,8},{8,16},{16,24},{1,9},{9,17},{17,25},{2,10},{10,18},{18,26},{... | collective-permute-start | bytes 393224 | tf_op jit(solution)/shard_map/ppermute | solution.py:410
  9.2 0.1 broadcast_in_dim.25
  9.3 0.1 convert_element_type.44.lanes
  9.4 0.9 shift-right-arithmetic_convert_fusion
  10.2 1.5 %multiply_bitcast_fusion = (bf16[8,2,32,128]{3,1,2,0:T(2,128)(2,1)S(1)}, bf16[8,2,32,128]{3,1,2,0:T(2,128)(2,1)S(1)}) fusion(bf16[8,32,16,128]{3,2,1,0:T(8,128)(2,1)} %feat.1, bf16[2,128]{1,0:T(2,128)(2,1)S(1)} %get-tuple-element.49, bf16[2,128]{1,0:T(2,128)(2,1)S(1)} %get-tuple-element.50), kind=kLoop, calls=%fused_computation.7 | loop fusion | flops 131072 | bytes 525312 | tf_op jit(solution)/shard_map/transpose | solution.py:449
  11.8 0.0 copy-done.16
  11.8 0.2 reshape.89
  12.0 0.1 copy.43
  12.1 0.2 reshape.90.weight
  12.3 0.1 pad.18.clone
  12.4 0.1 maximum_bitcast_fusion.1
  12.5 0.0 collective-permute-done.1
  12.5 0.0 collective-permute-done
  12.5 3.2 %collective-permute-start.2 = (bf16[21,32,128]{2,1,0:T(8,128)(2,1)S(1)}, bf16[21,32,128]{2,1,0:T(8,128)(2,1)S(1)}, u32[]{:S(2)}, u32[]{:S(2)}) collective-permute-start(bf16[21,32,128]{2,1,0:T(8,128)(2,1)S(1)} %pad_maximum_fusion), channel_id=1, source_target_pairs={{0,1},{1,2},{2,3},{3,4},{4,5},{5,6},{6,7},{8,9},{9,10},{10,11},{11... | collective-permute-start | bytes 516104 | tf_op jit(solution)/shard_map/ppermute | solution.py:410
  15.8 1.3 %collective-permute-start.3 = (bf16[21,32,128]{2,1,0:T(8,128)(2,1)S(1)}, bf16[21,32,128]{2,1,0:T(8,128)(2,1)S(1)}, u32[]{:S(2)}, u32[]{:S(2)}) collective-permute-start(bf16[21,32,128]{2,1,0:T(8,128)(2,1)S(1)} %pad_maximum_fusion.1), channel_id=1, source_target_pairs={{1,0},{2,1},{3,2},{4,3},{5,4},{6,5},{7,6},{9,8},{10,9},{11,10},{12... | collective-permute-start | bytes 516104 | tf_op jit(solution)/shard_map/ppermute | solution.py:410
  17.1 0.1 copy.38.x_high
  17.1 0.1 copy.37.x_low
  17.2 0.0 copy-start.1
  17.2 1.7 %shard_map.121.core = bf16[10,16,96,128]{3,2,1,0:T(8,128)(2,1)S(1)} custom-call(bf16[8,32,16,128]{3,2,1,0:T(8,128)(2,1)S(1)} %copy-done, bf16[32,16,128]{2,1,0:T(8,128)(2,1)S(1)} %copy.37.x_low, bf16[32,16,128]{2,1,0:T(8,128)(2,1)S(1)} %copy.38.x_high, f32[1,2,128]{2,1,0:T(2,128)S(1)} %convert_element_type.44.lanes), custom_call_target="tpu_custom_call" | custom-call | flops 3000000000 | bytes 9000000 | tf_op jit(solution)/shard_map/pallas_call | solution.py:395
  18.9 0.9 collective-permute-done.2.y_low
  19.8 4.1 %collective-permute-done.3.y_high = bf16[21,32,128]{2,1,0:T(8,128)(2,1)S(1)} collective-permute-done((bf16[21,32,128]{2,1,0:T(8,128)(2,1)S(1)}, bf16[21,32,128]{2,1,0:T(8,128)(2,1)S(1)}, u32[]{:S(2)}, u32[]{:S(2)}) %collective-permute-start.3) | collective-permute-done | bytes 172064 | tf_op jit(solution)/shard_map/ppermute | solution.py:410
  23.9 8.9 %shard_map.122 = (bf16[10,2,96,128]{3,2,1,0:T(8,128)(2,1)S(1)}, bf16[10,2,96,128]{3,2,1,0:T(8,128)(2,1)S(1)}, bf16[8,32,2304]{2,1,0:T(8,128)(2,1)S(1)}, bf16[8,48,256]{2,1,0:T(8,128)(2,1)S(1)}, f32[2,32,128]{2,1,0:T(8,128)S(1)}) custom-call(bf16[10,16,96,128]{3,2,1,0:T(8,128)(2,1)S(1)} %shard_map.121.core, ...), custom_call_target="tpu_custom_call" | custom-call | flops 8999999488 | bytes 27000000 | tf_op jit(solution)/shard_map/pallas_call | solution.py:395
  32.8 0.0 copy-done.8
  32.8 0.0 copy-start.12
  32.8 12.6 %all_to_all.34.parts = bf16[8,48,256]{2,1,0:T(8,128)(2,1)S(1)} all-to-all(bf16[8,48,256]{2,1,0:T(8,128)(2,1)S(1)} %get-tuple-element.18), channel_id=1, replica_groups=mesh['drift'=4,'beam'=8] {'beam'}, dimensions={0} | all-to-all | bytes 393216 | tf_op jit(solution)/shard_map/all_to_all | solution.py:414
  45.5 0.0 copy-start.6
  45.5 0.0 copy-start.7
  45.5 0.7 shard_map.123
  46.2 0.0 copy-done.14
  46.2 4.0 %all-to-all-start.1 = ((bf16[8,32,256]{2,1,0:T(8,128)(2,1)}), bf16[8,32,256]{2,1,0:T(8,128)(2,1)S(1)}, u32[]{:S(2)}, u32[]{:S(2)}) async-start(bf16[8,32,256]{2,1,0:T(8,128)(2,1)} %get-tuple-element.19), calls=%async_computation.1 | async-start | bytes 262144 | tf_op jit(solution)/shard_map/all_to_all | solution.py:414
  50.2 0.7 rev.3
  50.9 0.2 copy.44
  51.2 0.2 reshape.93._.weight
  51.3 0.7 slice_bitcast_fusion.6.mine
  52.1 4.4 %all-to-all-done.1.table = bf16[8,32,256]{2,1,0:T(8,128)(2,1)S(1)} async-done(((bf16[8,32,256]{2,1,0:T(8,128)(2,1)}), bf16[8,32,256]{2,1,0:T(8,128)(2,1)S(1)}, u32[]{:S(2)}, u32[]{:S(2)}) %all-to-all-start.1) | async-done | bytes 131104 | tf_op jit(solution)/shard_map/all_to_all | solution.py:414
  56.4 0.0 copy-done.3
  56.5 2.9 %shard_map.124 = (bf16[256,256]{1,0:T(8,128)(2,1)}, bf16[8,32,256]{2,1,0:T(8,128)(2,1)S(1)}, f32[32,256]{1,0:T(8,128)S(1)}) custom-call(bf16[8,32,256]{2,1,0:T(8,128)(2,1)S(1)} %all-to-all-done.1.table, bf16[32,256]{1,0:T(8,128)(2,1)S(1)} %slice_bitcast_fusion.6.mine, bf16[32,256]{1,0:T(8,128)(2,1)S(1)} %copy-done.5, bf16[256,256]{1,0:T(8,128)(2,1)S(1)} %copy-done.2, ...), custom_call_target="tpu_custom_call" | custom-call | flops 2000000000 | bytes 6000000 | tf_op jit(solution)/shard_map/pallas_call | solution.py:395
  59.3 8.6 %all_to_all.35.parts = bf16[8,32,256]{2,1,0:T(8,128)(2,1)S(1)} all-to-all(bf16[8,32,256]{2,1,0:T(8,128)(2,1)S(1)} %get-tuple-element.21), channel_id=1, replica_groups=mesh['drift'=4,'beam'=8] {'beam'}, dimensions={0} | all-to-all | bytes 262144 | tf_op jit(solution)/shard_map/all_to_all | solution.py:414
  68.0 8.8 %all_to_all.36.table = bf16[8,32,256]{2,1,0:T(8,128)(2,1)S(1)} all-to-all(bf16[8,32,256]{2,1,0:T(8,128)(2,1)S(1)} %shard_map.125), channel_id=1, replica_groups=mesh['drift'=4,'beam'=8] {'beam'}, dimensions={0} | all-to-all | bytes 262144 | tf_op jit(solution)/shard_map/all_to_all | solution.py:414
  76.8 8.0 %shard_map.126 = (bf16[8,32,2048]{2,1,0:T(8,128)(2,1)S(1)}, bf16[8,18,32,128]{3,2,1,0:T(8,128)(2,1)S(1)}, bf16[18,32,128]{2,1,0:T(8,128)(2,1)S(1)}, bf16[18,32,128]{2,1,0:T(8,128)(2,1)S(1)}, f32[256,128]{1,0:T(8,128)}) custom-call(bf16[8,32,256]{2,1,0:T(8,128)(2,1)S(1)} %all_to_all.36.table, s32[8,16,128]{2,1,0:T(8,128)S(1)} %copy-done.1, ...), custom_call_target="tpu_custom_call" | custom-call | flops 8999999488 | bytes 27000000 | tf_op jit(solution)/shard_map/pallas_call | solution.py:395
  84.9 1.0 copy-done.10
  85.8 7.0 %all-to-all-start.4 = ((f32[32,8,128]{2,1,0:T(8,128)}), f32[32,8,128]{2,1,0:T(8,128)S(1)}, u32[]{:S(2)}, u32[]{:S(2)}) async-start(f32[32,8,128]{2,1,0:T(8,128)} %bitcast.26), calls=%async_computation.4 | async-start | bytes 262144 | tf_op jit(solution)/shard_map/all_to_all | solution.py:414
  92.8 3.5 %collective-permute-start.4 = (bf16[18,32,128]{2,1,0:T(8,128)(2,1)S(1)}, bf16[18,32,128]{2,1,0:T(8,128)(2,1)S(1)}, u32[]{:S(2)}, u32[]{:S(2)}) collective-permute-start(bf16[18,32,128]{2,1,0:T(8,128)(2,1)S(1)} %get-tuple-element.29), channel_id=1, source_target_pairs={{0,8},{8,16},{16,24},{1,9},{9,17},{17,25},{2,10},{10,18},{18,26},{... | collective-permute-start | bytes 442376 | tf_op jit(solution)/shard_map/ppermute | solution.py:410
  96.4 1.9 %collective-permute-start.5 = (bf16[18,32,128]{2,1,0:T(8,128)(2,1)S(1)}, bf16[18,32,128]{2,1,0:T(8,128)(2,1)S(1)}, u32[]{:S(2)}, u32[]{:S(2)}) collective-permute-start(bf16[18,32,128]{2,1,0:T(8,128)(2,1)S(1)} %get-tuple-element.30), channel_id=1, source_target_pairs={{8,0},{16,8},{24,16},{9,1},{17,9},{25,17},{10,2},{18,10},{26,18},{... | collective-permute-start | bytes 442376 | tf_op jit(solution)/shard_map/ppermute | solution.py:410
  98.3 2.3 %all-to-all-done.4 = f32[32,8,128]{2,1,0:T(8,128)S(1)} async-done(((f32[32,8,128]{2,1,0:T(8,128)}), f32[32,8,128]{2,1,0:T(8,128)S(1)}, u32[]{:S(2)}, u32[]{:S(2)}) %all-to-all-start.4) | async-done | bytes 131104 | tf_op jit(solution)/shard_map/all_to_all | solution.py:414
  100.6 0.7 broadcast_in_dim.28
  101.2 3.8 %all-to-all-start.5 = ((f32[32,8,128]{2,1,0:T(8,128)}), f32[32,8,128]{2,1,0:T(8,128)S(1)}, u32[]{:S(2)}, u32[]{:S(2)}) async-start(f32[32,8,128]{2,1,0:T(8,128)} %broadcast_in_dim.28), calls=%async_computation.5 | async-start | bytes 262144 | tf_op jit(solution)/shard_map/all_to_all | solution.py:414
  105.1 0.0 collective-permute-done.4.x_low
  105.1 0.0 collective-permute-done.5.x_high
  105.1 0.0 copy-start.11
  105.1 1.2 %copy-done.11 = bf16[8,32,2048]{2,1,0:T(8,128)(2,1)S(1)} copy-done((bf16[8,32,2048]{2,1,0:T(8,128)(2,1)S(1)}, bf16[8,32,2048]{2,1,0:T(8,128)(2,1)}, u32[]{:S(2)}) %copy-start.11) | copy-done | bytes 1048600
  106.3 6.0 %shard_map.127 = f32[8,32,16,128]{3,2,1,0:T(8,128)} custom-call(bf16[8,18,32,128]{3,2,1,0:T(8,128)(2,1)S(1)} %get-tuple-element.28.back_conv, bf16[18,32,128]{2,1,0:T(8,128)(2,1)S(1)} %collective-permute-done.4.x_low, bf16[18,32,128]{2,1,0:T(8,128)(2,1)S(1)} %collective-permute-done.5.x_high, bf16[8,32,2048]{2,1,0:T(8,128)(2,1)S(1)} %copy-done.11, ...), custom_call_target="tpu_custom_call" | custom-call | flops 10000000000 | bytes 30000000 | tf_op jit(solution)/shard_map/pallas_call | solution.py:395
  112.3 0.3 all-to-all-done.5
  112.7 0.1 reshape.94
  112.8 0.2 reshape.96
  113.1 0.1 copy.47
  113.2 0.9 reshape.97
  (41 shorter events, 0.3 us)
Async XLA Ops:
  0.6 11.2 %copy-start.16 = (bf16[32,864]{1,0:T(8,128)(2,1)S(1)}, bf16[32,864]{1,0:T(8,128)(2,1)}, u32[]{:S(2)}) copy-start(bf16[32,864]{1,0:T(8,128)(2,1)} %param.13) | copy-start | bytes 165892
  2.6 14.6 %copy-start = (bf16[8,32,16,128]{3,2,1,0:T(8,128)(2,1)S(1)}, bf16[8,32,16,128]{3,2,1,0:T(8,128)(2,1)}, u32[]{:S(2)}) copy-start(bf16[8,32,16,128]{3,2,1,0:T(8,128)(2,1)} %feat.1) | copy-start | bytes 3145732
  2.6 9.9 %collective-permute-start.1 = (bf16[32,16,128]{2,0,1:T(8,128)(2,1)S(1)}, bf16[32,16,128]{2,0,1:T(8,128)(2,1)S(1)}, u32[]{:S(2)}, u32[]{:S(2)}) collective-permute-start(bf16[32,16,128]{2,0,1:T(8,128)(2,1)S(1)} %get-tuple-element.53), channel_id=1, source_target_pairs={{8,0},{16,8},{24,16},{9,1},{17,9},{25,17},{10,2},{18,10},{26,18},{... | collective-permute-start | bytes 393224 | tf_op jit(solution)/shard_map/ppermute | solution.py:410
  4.7 7.8 %collective-permute-start = (bf16[32,16,128]{2,0,1:T(8,128)(2,1)S(1)}, bf16[32,16,128]{2,0,1:T(8,128)(2,1)S(1)}, u32[]{:S(2)}, u32[]{:S(2)}) collective-permute-start(bf16[32,16,128]{2,0,1:T(8,128)(2,1)S(1)} %get-tuple-element.54), channel_id=1, source_target_pairs={{0,8},{8,16},{16,24},{1,9},{9,17},{17,25},{2,10},{10,18},{18,26},{... | collective-permute-start | bytes 393224 | tf_op jit(solution)/shard_map/ppermute | solution.py:410
  12.5 7.3 %collective-permute-start.2 = (bf16[21,32,128]{2,1,0:T(8,128)(2,1)S(1)}, bf16[21,32,128]{2,1,0:T(8,128)(2,1)S(1)}, u32[]{:S(2)}, u32[]{:S(2)}) collective-permute-start(bf16[21,32,128]{2,1,0:T(8,128)(2,1)S(1)} %pad_maximum_fusion), channel_id=1, source_target_pairs={{0,1},{1,2},{2,3},{3,4},{4,5},{5,6},{6,7},{8,9},{9,10},{10,11},{11... | collective-permute-start | bytes 516104 | tf_op jit(solution)/shard_map/ppermute | solution.py:410
  15.8 8.1 %collective-permute-start.3 = (bf16[21,32,128]{2,1,0:T(8,128)(2,1)S(1)}, bf16[21,32,128]{2,1,0:T(8,128)(2,1)S(1)}, u32[]{:S(2)}, u32[]{:S(2)}) collective-permute-start(bf16[21,32,128]{2,1,0:T(8,128)(2,1)S(1)} %pad_maximum_fusion.1), channel_id=1, source_target_pairs={{1,0},{2,1},{3,2},{4,3},{5,4},{6,5},{7,6},{9,8},{10,9},{11,10},{12... | collective-permute-start | bytes 516104 | tf_op jit(solution)/shard_map/ppermute | solution.py:410
  17.2 6.7 %copy-start.1 = (s32[8,16,128]{2,1,0:T(8,128)S(1)}, s32[8,16,128]{2,1,0:T(8,128)}, u32[]{:S(2)}) copy-start(s32[8,16,128]{2,1,0:T(8,128)} %fragment.3) | copy-start | bytes 196612
  18.9 13.9 %copy-start.8 = (bf16[10,16,96,128]{3,2,1,0:T(8,128)(2,1)}, bf16[10,16,96,128]{3,2,1,0:T(8,128)(2,1)S(1)}, u32[]{:S(2)}) copy-start(bf16[10,16,96,128]{3,2,1,0:T(8,128)(2,1)S(1)} %shard_map.121.core) | copy-start | bytes 11796484
  32.8 13.4 %copy-start.12 = (bf16[10,2,96,128]{3,2,1,0:T(8,128)(2,1)}, bf16[10,2,96,128]{3,2,1,0:T(8,128)(2,1)S(1)}, u32[]{:S(2)}) copy-start(bf16[10,2,96,128]{3,2,1,0:T(8,128)(2,1)S(1)} %get-tuple-element.26.low) | copy-start | bytes 1474564
  32.8 13.4 %copy-start.14 = (bf16[10,2,96,128]{3,2,1,0:T(8,128)(2,1)}, bf16[10,2,96,128]{3,2,1,0:T(8,128)(2,1)S(1)}, u32[]{:S(2)}) copy-start(bf16[10,2,96,128]{3,2,1,0:T(8,128)(2,1)S(1)} %get-tuple-element.27.high) | copy-start | bytes 1474564
  45.5 11.0 %copy-start.2 = (bf16[256,256]{1,0:T(8,128)(2,1)S(1)}, bf16[256,256]{1,0:T(8,128)(2,1)}, u32[]{:S(2)}) copy-start(bf16[256,256]{1,0:T(8,128)(2,1)} %message.1) | copy-start | bytes 393220
  45.5 11.0 %copy-start.3 = (bf16[256,256]{1,0:T(8,128)(2,1)S(1)}, bf16[256,256]{1,0:T(8,128)(2,1)}, u32[]{:S(2)}) copy-start(bf16[256,256]{1,0:T(8,128)(2,1)} %update.1) | copy-start | bytes 393220
  45.5 11.0 %copy-start.4 = (bf16[256,256]{1,0:T(8,128)(2,1)S(1)}, bf16[256,256]{1,0:T(8,128)(2,1)}, u32[]{:S(2)}) copy-start(bf16[256,256]{1,0:T(8,128)(2,1)} %cotangent.1) | copy-start | bytes 393220
  45.5 11.0 %copy-start.5 = (bf16[32,256]{1,0:T(8,128)(2,1)S(1)}, bf16[32,256]{1,0:T(8,128)(2,1)}, u32[]{:S(2)}) copy-start(bf16[32,256]{1,0:T(8,128)(2,1)} %embed.1) | copy-start | bytes 49156
  45.5 11.0 %copy-start.6 = (s32[1024]{0:T(1024)S(1)}, s32[1024]{0:T(1024)}, u32[]{:S(2)}) copy-start(s32[1024]{0:T(1024)} %param.17) | copy-start | bytes 12292
  45.5 11.0 %copy-start.7 = (s32[1024]{0:T(1024)S(1)}, s32[1024]{0:T(1024)}, u32[]{:S(2)}) copy-start(s32[1024]{0:T(1024)} %param.18) | copy-start | bytes 12292
  46.2 10.2 %all-to-all-start.1 = ((bf16[8,32,256]{2,1,0:T(8,128)(2,1)}), bf16[8,32,256]{2,1,0:T(8,128)(2,1)S(1)}, u32[]{:S(2)}, u32[]{:S(2)}) async-start(bf16[8,32,256]{2,1,0:T(8,128)(2,1)} %get-tuple-element.19), calls=%async_computation.1 | async-start | bytes 262144 | tf_op jit(solution)/shard_map/all_to_all | solution.py:414
  67.9 8.9 %copy-start.9 = (bf16[10,16,96,128]{3,2,1,0:T(8,128)(2,1)S(1)}, bf16[10,16,96,128]{3,2,1,0:T(8,128)(2,1)}, u32[]{:S(2)}) copy-start(bf16[10,16,96,128]{3,2,1,0:T(8,128)(2,1)} %copy-done.8) | copy-start | bytes 11796484
  67.9 8.9 %copy-start.13 = (bf16[10,2,96,128]{3,2,1,0:T(8,128)(2,1)S(1)}, bf16[10,2,96,128]{3,2,1,0:T(8,128)(2,1)}, u32[]{:S(2)}) copy-start(bf16[10,2,96,128]{3,2,1,0:T(8,128)(2,1)} %copy-done.12) | copy-start | bytes 1474564
  67.9 8.9 %copy-start.15 = (bf16[10,2,96,128]{3,2,1,0:T(8,128)(2,1)S(1)}, bf16[10,2,96,128]{3,2,1,0:T(8,128)(2,1)}, u32[]{:S(2)}) copy-start(bf16[10,2,96,128]{3,2,1,0:T(8,128)(2,1)} %copy-done.14) | copy-start | bytes 1474564
  84.8 1.0 copy-start.10
  85.8 14.7 %all-to-all-start.4 = ((f32[32,8,128]{2,1,0:T(8,128)}), f32[32,8,128]{2,1,0:T(8,128)S(1)}, u32[]{:S(2)}, u32[]{:S(2)}) async-start(f32[32,8,128]{2,1,0:T(8,128)} %bitcast.26), calls=%async_computation.4 | async-start | bytes 262144 | tf_op jit(solution)/shard_map/all_to_all | solution.py:414
  92.8 12.3 %collective-permute-start.4 = (bf16[18,32,128]{2,1,0:T(8,128)(2,1)S(1)}, bf16[18,32,128]{2,1,0:T(8,128)(2,1)S(1)}, u32[]{:S(2)}, u32[]{:S(2)}) collective-permute-start(bf16[18,32,128]{2,1,0:T(8,128)(2,1)S(1)} %get-tuple-element.29), channel_id=1, source_target_pairs={{0,8},{8,16},{16,24},{1,9},{9,17},{17,25},{2,10},{10,18},{18,26},{... | collective-permute-start | bytes 442376 | tf_op jit(solution)/shard_map/ppermute | solution.py:410
  96.4 8.7 %collective-permute-start.5 = (bf16[18,32,128]{2,1,0:T(8,128)(2,1)S(1)}, bf16[18,32,128]{2,1,0:T(8,128)(2,1)S(1)}, u32[]{:S(2)}, u32[]{:S(2)}) collective-permute-start(bf16[18,32,128]{2,1,0:T(8,128)(2,1)S(1)} %get-tuple-element.30), channel_id=1, source_target_pairs={{8,0},{16,8},{24,16},{9,1},{17,9},{25,17},{10,2},{18,10},{26,18},{... | collective-permute-start | bytes 442376 | tf_op jit(solution)/shard_map/ppermute | solution.py:410
  101.2 11.4 %all-to-all-start.5 = ((f32[32,8,128]{2,1,0:T(8,128)}), f32[32,8,128]{2,1,0:T(8,128)S(1)}, u32[]{:S(2)}, u32[]{:S(2)}) async-start(f32[32,8,128]{2,1,0:T(8,128)} %broadcast_in_dim.28), calls=%async_computation.5 | async-start | bytes 262144 | tf_op jit(solution)/shard_map/all_to_all | solution.py:414
  105.1 1.2 %copy-start.11 = (bf16[8,32,2048]{2,1,0:T(8,128)(2,1)S(1)}, bf16[8,32,2048]{2,1,0:T(8,128)(2,1)}, u32[]{:S(2)}) copy-start(bf16[8,32,2048]{2,1,0:T(8,128)(2,1)} %copy-done.10) | copy-start | bytes 3145732

commit v7 on v6

--- a/solution.py
+++ b/solution.py
@@ -271,12 +271,13 @@
 
 def hidden_kernel(
     table, fragment, lanes, sides, slopes, low, core, high,
-    back_hidden, back_conv, face_low, face_high, packed, grad
+    hidden_out, back_conv, face_low, face_high, packed, grad, back_hidden, hidden_sent
 ):
     owners, channels, frag_dev = table.shape
     rows, wide_height, _, depth = back_conv.shape
     height = wide_height - 2
     taps = (low, core, high)
+    send = row_copy(back_hidden, hidden_out, hidden_sent)
     flat = table[...].reshape(owners * channels, frag_dev)
     empty = jnp.zeros((channels, depth), bf16)
     grad[...] = jnp.zeros_like(grad)
@@ -293,6 +294,7 @@
         hidden = jnp.concatenate(pieces, 1)
         inner = hidden[:, depth : depth + height * depth]
         back_hidden[x] = (live_line(lanes, x, height) * inner).astype(bf16)
+        send(x).start()
         conv = (hidden * slopes[x].astype(f32)).astype(bf16)
         for y in range(wide_height):
             back_conv[x, y] = conv[:, y * depth : (y + 1) * depth]
@@ -315,9 +317,10 @@
     packed[...] = jnp.zeros_like(packed)
     turned = grad[...].T
     for place, part in packed_parts(turned.shape):
-        high = part[0].stop - part[0].start
+        tall = part[0].stop - part[0].start
         width = part[1].stop - part[1].start
-        packed[place[0] : place[0] + high, place[1] : place[1] + width] = turned[part]
+        packed[place[0] : place[0] + tall, place[1] : place[1] + width] = turned[part]
+    wait_rows(send, rows)
 
 
 def packed_parts(shape):
@@ -350,8 +353,8 @@
 
 
 def backward_kernel(
-    back_conv, x_low, x_high, back_hidden, lanes, weight, grad_out,
-    grad, taps, faces, sent, faces_here
+    back_conv, x_low, x_high, hidden_in, lanes, weight, grad_out,
+    grad, taps, faces, back_hidden, sent, faces_here, hidden_here
 ):
     rows, wide_height, channels, depth = back_conv.shape
     height = wide_height - 2
@@ -360,6 +363,13 @@
     get_high = pltpu.make_async_copy(x_high, faces.at[1], faces_here.at[1])
     get_low.start()
     get_high.start()
+    fetch = row_copy(hidden_in, back_hidden, hidden_here)
+
+    def ask(x, _):
+        fetch(x).start()
+        return 0
+
+    lax.fori_loop(0, rows, ask, 0)
 
     def fill(x, _):
         store_taps(taps, x + 1, 0, back_conv[x])
@@ -374,6 +384,7 @@
     def one_row(x, _):
         live = live_line(lanes, x, height)
         found = convolve_row((taps,), weight[...], x, height)
+        fetch(x).wait()
         result = live * (back_hidden[x].astype(f32) + found)
         tiles = [result[:, y * depth : (y + 1) * depth][None] for y in range(height)]
         grad[x] = jnp.swapaxes(jnp.concatenate(tiles, 0), 0, 1)
@@ -390,12 +401,16 @@
     )
 
 
-def call(kernel, shapes, *operands, scratch=(), micros=2, far_in=(), far_out=()):
+def call(kernel, shapes, *operands, scratch=(), micros=2, far_in=(), far_out=(), fixed_in=()):
+    fixed = pl.BlockSpec(memory_space=pltpu.HBM)
     here, there = pl.BlockSpec(memory_space=pltpu.VMEM), pl.BlockSpec(memory_space=pl.ANY)
     return pl.pallas_call(
         kernel,
-        in_specs=[there if i in far_in else here for i in range(len(operands))],
-        out_specs=[there if i in far_out else here for i in range(len(shapes))],
+        in_specs=[
+            fixed if i in fixed_in else there if i in far_in else here
+            for i in range(len(operands))
+        ],
+        out_specs=[fixed if i in far_out else here for i in range(len(shapes))],
         out_shape=[jax.ShapeDtypeStruct(shape, kind) for shape, kind in shapes],
         scratch_shapes=list(scratch),
         cost_estimate=cost(micros),
@@ -511,7 +526,10 @@
             ((devices * share, LANES), f32),
         ],
         exchange(mean, "beam"), voxel_fragment, lanes, sides, slopes, low, core, high, micros=9,
-        scratch=[pltpu.VMEM(stacked_shape[::-1], f32)],
+        scratch=[
+            pltpu.VMEM(stacked_shape[::-1], f32), pltpu.VMEM(line_shape, bf16), dma(rows),
+        ],
+        far_out=(0,),
     )
     gx_low, gx_high = pass_on(face_low, face_high, "drift")
     (grad_features,) = call(
@@ -520,9 +538,10 @@
         back_conv, gx_low, gx_high, back_hidden, lanes, flipped, micros=10,
         scratch=[
             pltpu.VMEM(features.shape, f32), pltpu.VMEM(tapped, bf16),
-            pltpu.VMEM((2,) + conv_shape[1:], bf16), dma(rows), dma(2),
+            pltpu.VMEM((2,) + conv_shape[1:], bf16), pltpu.VMEM(line_shape, bf16),
+            dma(rows), dma(2), dma(rows),
         ],
-        far_in=(1, 2), far_out=(0,),
+        far_in=(1, 2), fixed_in=(3,), far_out=(0,),
     )
     parts = exchange(packed, everyone).reshape(devices, share, LANES)
     full = exchange(jnp.broadcast_to(parts.sum(0)[None], parts.shape), everyone)

time: 115 us -> 120 us (1.043)
  Pallas kernels: 28.3 us -> 33.5 us
    pallas_call x7, Pallas kernels: 28.3 us -> 33.5 us  [call(): pl.pallas_call(kernel, in_specs=[fixed if i in fixed_in else there if i i...]
  transfers between devices with their start and end apart: 9 -> 9, of which waited for: 5 -> 4; matrix products, arithmetic and copies ran while one was open for 5% -> 5% of each run, Pallas kernels for 7% -> 8%
where the time goes in v7:
time: 120 us; the launch traced here: 119 us
  Pallas kernels  33.5 us (28%)
  starting transfers between devices  31.3 us (26%)
  blocking collectives  30.1 us (25%)
  waiting for transfers between devices  11.6 us (10%)
  local copies, waits for them, and re-layouts  8.18 us (7%)
  other arithmetic  3.31 us (3%)
    pallas_call x7, Pallas kernels, call(): pl.pallas_call(kernel, in_specs=[fixed if i in fixed_in else there if i i...  33.5 us
    all_to_all x3, blocking collectives, exchange(): return lax.all_to_all(parts, axes, 0, 0, tiled=True)  30.1 us
    ppermute x6, starting transfers between devices, pass_on(): return (lax.ppermute(high, axis, up), lax.ppermute(low, axis, down))  16.5 us
    all_to_all x3, starting transfers between devices, exchange(): return lax.all_to_all(parts, axes, 0, 0, tiled=True)  14.8 us
    all_to_all x3, waiting for transfers between devices, exchange(): return lax.all_to_all(parts, axes, 0, 0, tiled=True)  6.61 us
    ppermute x6, waiting for transfers between devices, pass_on(): return (lax.ppermute(high, axis, up), lax.ppermute(low, axis, down))  4.97 us
  transfers between devices with their start and end apart: 9, of which 4 were waited for; matrix products, arithmetic and copies ran while one was open for 5% of the time, Pallas kernels for 8%

profile of v7, /device:TPU:1, one launch (start us, length us, event | category | flops | bytes accessed | tf_op | source)
XLA Modules:
  0.0 119.0 jit_solution(17564224773964450816)
XLA Ops:
  0.6 0.7 convert_bitcast_fusion
  1.3 0.1 broadcast_in_dim.23
  1.4 0.1 convert_element_type.41
  1.5 1.0 fusion.3
  2.5 0.1 fusion
  2.6 0.0 copy-start
  2.6 2.1 %collective-permute-start.1 = (bf16[32,16,128]{2,0,1:T(8,128)(2,1)S(1)}, bf16[32,16,128]{2,0,1:T(8,128)(2,1)S(1)}, u32[]{:S(2)}, u32[]{:S(2)}) collective-permute-start(bf16[32,16,128]{2,0,1:T(8,128)(2,1)S(1)} %get-tuple-element.53), channel_id=1, source_target_pairs={{8,0},{16,8},{24,16},{9,1},{17,9},{25,17},{10,2},{18,10},{26,18},{... | collective-permute-start | bytes 393224 | tf_op jit(solution)/shard_map/ppermute | solution.py:425
  4.7 4.5 %collective-permute-start = (bf16[32,16,128]{2,0,1:T(8,128)(2,1)S(1)}, bf16[32,16,128]{2,0,1:T(8,128)(2,1)S(1)}, u32[]{:S(2)}, u32[]{:S(2)}) collective-permute-start(bf16[32,16,128]{2,0,1:T(8,128)(2,1)S(1)} %get-tuple-element.54), channel_id=1, source_target_pairs={{0,8},{8,16},{16,24},{1,9},{9,17},{17,25},{2,10},{10,18},{18,26},{... | collective-permute-start | bytes 393224 | tf_op jit(solution)/shard_map/ppermute | solution.py:425
  9.2 0.1 broadcast_in_dim.25
  9.3 0.1 convert_element_type.44.lanes
  9.4 0.9 shift-right-arithmetic_convert_fusion
  10.2 1.5 %multiply_bitcast_fusion = (bf16[8,2,32,128]{3,1,2,0:T(2,128)(2,1)S(1)}, bf16[8,2,32,128]{3,1,2,0:T(2,128)(2,1)S(1)}) fusion(bf16[8,32,16,128]{3,2,1,0:T(8,128)(2,1)} %feat.1, bf16[2,128]{1,0:T(2,128)(2,1)S(1)} %get-tuple-element.49, bf16[2,128]{1,0:T(2,128)(2,1)S(1)} %get-tuple-element.50), kind=kLoop, calls=%fused_computation.7 | loop fusion | flops 131072 | bytes 525312 | tf_op jit(solution)/shard_map/transpose | solution.py:464
  11.8 0.2 reshape.89
  12.0 0.1 copy.43
  12.1 0.2 reshape.90.weight
  12.3 0.1 pad.18.clone
  12.4 0.1 maximum_bitcast_fusion.1
  12.5 0.0 collective-permute-done.1
  12.5 0.0 collective-permute-done
  12.5 3.2 %collective-permute-start.2 = (bf16[21,32,128]{2,1,0:T(8,128)(2,1)S(1)}, bf16[21,32,128]{2,1,0:T(8,128)(2,1)S(1)}, u32[]{:S(2)}, u32[]{:S(2)}) collective-permute-start(bf16[21,32,128]{2,1,0:T(8,128)(2,1)S(1)} %pad_maximum_fusion), channel_id=1, source_target_pairs={{0,1},{1,2},{2,3},{3,4},{4,5},{5,6},{6,7},{8,9},{9,10},{10,11},{11... | collective-permute-start | bytes 516104 | tf_op jit(solution)/shard_map/ppermute | solution.py:425
  15.8 1.3 %collective-permute-start.3 = (bf16[21,32,128]{2,1,0:T(8,128)(2,1)S(1)}, bf16[21,32,128]{2,1,0:T(8,128)(2,1)S(1)}, u32[]{:S(2)}, u32[]{:S(2)}) collective-permute-start(bf16[21,32,128]{2,1,0:T(8,128)(2,1)S(1)} %pad_maximum_fusion.1), channel_id=1, source_target_pairs={{1,0},{2,1},{3,2},{4,3},{5,4},{6,5},{7,6},{9,8},{10,9},{11,10},{12... | collective-permute-start | bytes 516104 | tf_op jit(solution)/shard_map/ppermute | solution.py:425
  17.1 0.1 copy.38.x_high
  17.1 0.1 copy.37.x_low
  17.2 0.0 copy-start.1
  17.2 1.7 %shard_map.121.core = bf16[10,16,96,128]{3,2,1,0:T(8,128)(2,1)S(1)} custom-call(bf16[8,32,16,128]{3,2,1,0:T(8,128)(2,1)S(1)} %copy-done, bf16[32,16,128]{2,1,0:T(8,128)(2,1)S(1)} %copy.37.x_low, bf16[32,16,128]{2,1,0:T(8,128)(2,1)S(1)} %copy.38.x_high, f32[1,2,128]{2,1,0:T(2,128)S(1)} %convert_element_type.44.lanes), custom_call_target="tpu_custom_call" | custom-call | flops 3000000000 | bytes 9000000 | tf_op jit(solution)/shard_map/pallas_call | solution.py:407
  18.9 0.9 collective-permute-done.2.y_low
  19.8 4.1 %collective-permute-done.3.y_high = bf16[21,32,128]{2,1,0:T(8,128)(2,1)S(1)} collective-permute-done((bf16[21,32,128]{2,1,0:T(8,128)(2,1)S(1)}, bf16[21,32,128]{2,1,0:T(8,128)(2,1)S(1)}, u32[]{:S(2)}, u32[]{:S(2)}) %collective-permute-start.3) | collective-permute-done | bytes 172064 | tf_op jit(solution)/shard_map/ppermute | solution.py:425
  23.9 0.0 copy-done.1
  23.9 8.9 %shard_map.122 = (bf16[10,2,96,128]{3,2,1,0:T(8,128)(2,1)S(1)}, bf16[10,2,96,128]{3,2,1,0:T(8,128)(2,1)S(1)}, bf16[8,32,2304]{2,1,0:T(8,128)(2,1)S(1)}, bf16[8,48,256]{2,1,0:T(8,128)(2,1)S(1)}, f32[2,32,128]{2,1,0:T(8,128)S(1)}) custom-call(bf16[10,16,96,128]{3,2,1,0:T(8,128)(2,1)S(1)} %shard_map.121.core, ...), custom_call_target="tpu_custom_call" | custom-call | flops 8999999488 | bytes 27000000 | tf_op jit(solution)/shard_map/pallas_call | solution.py:407
  32.8 0.0 copy-start.12
  32.8 12.6 %all_to_all.34.parts = bf16[8,48,256]{2,1,0:T(8,128)(2,1)S(1)} all-to-all(bf16[8,48,256]{2,1,0:T(8,128)(2,1)S(1)} %get-tuple-element.18), channel_id=1, replica_groups=mesh['drift'=4,'beam'=8] {'beam'}, dimensions={0} | all-to-all | bytes 393216 | tf_op jit(solution)/shard_map/all_to_all | solution.py:429
  45.5 0.0 copy-start.6
  45.5 0.0 copy-start.7
  45.5 0.7 shard_map.123
  46.2 0.0 copy-done.12
  46.2 4.0 %all-to-all-start.1 = ((bf16[8,32,256]{2,1,0:T(8,128)(2,1)}), bf16[8,32,256]{2,1,0:T(8,128)(2,1)S(1)}, u32[]{:S(2)}, u32[]{:S(2)}) async-start(bf16[8,32,256]{2,1,0:T(8,128)(2,1)} %get-tuple-element.19), calls=%async_computation.1 | async-start | bytes 262144 | tf_op jit(solution)/shard_map/all_to_all | solution.py:429
  50.2 0.7 rev.3
  50.9 0.2 copy.44
  51.2 0.2 reshape.93._.weight
  51.3 0.7 slice_bitcast_fusion.6.mine
  52.1 4.4 %all-to-all-done.1.table = bf16[8,32,256]{2,1,0:T(8,128)(2,1)S(1)} async-done(((bf16[8,32,256]{2,1,0:T(8,128)(2,1)}), bf16[8,32,256]{2,1,0:T(8,128)(2,1)S(1)}, u32[]{:S(2)}, u32[]{:S(2)}) %all-to-all-start.1) | async-done | bytes 131104 | tf_op jit(solution)/shard_map/all_to_all | solution.py:429
  56.4 0.0 copy-done.4
  56.5 2.9 %shard_map.124 = (bf16[256,256]{1,0:T(8,128)(2,1)}, bf16[8,32,256]{2,1,0:T(8,128)(2,1)S(1)}, f32[32,256]{1,0:T(8,128)S(1)}) custom-call(bf16[8,32,256]{2,1,0:T(8,128)(2,1)S(1)} %all-to-all-done.1.table, bf16[32,256]{1,0:T(8,128)(2,1)S(1)} %slice_bitcast_fusion.6.mine, bf16[32,256]{1,0:T(8,128)(2,1)S(1)} %copy-done.5, bf16[256,256]{1,0:T(8,128)(2,1)S(1)} %copy-done.2, ...), custom_call_target="tpu_custom_call" | custom-call | flops 2000000000 | bytes 6000000 | tf_op jit(solution)/shard_map/pallas_call | solution.py:407
  59.3 8.6 %all_to_all.35.parts = bf16[8,32,256]{2,1,0:T(8,128)(2,1)S(1)} all-to-all(bf16[8,32,256]{2,1,0:T(8,128)(2,1)S(1)} %get-tuple-element.21), channel_id=1, replica_groups=mesh['drift'=4,'beam'=8] {'beam'}, dimensions={0} | all-to-all | bytes 262144 | tf_op jit(solution)/shard_map/all_to_all | solution.py:429
  68.0 8.8 %all_to_all.36.table = bf16[8,32,256]{2,1,0:T(8,128)(2,1)S(1)} all-to-all(bf16[8,32,256]{2,1,0:T(8,128)(2,1)S(1)} %shard_map.125), channel_id=1, replica_groups=mesh['drift'=4,'beam'=8] {'beam'}, dimensions={0} | all-to-all | bytes 262144 | tf_op jit(solution)/shard_map/all_to_all | solution.py:429
  76.8 11.3 %shard_map.126 = (bf16[8,32,2048]{2,1,0:T(8,128)(2,1)S(1)}, bf16[8,18,32,128]{3,2,1,0:T(8,128)(2,1)S(1)}, bf16[18,32,128]{2,1,0:T(8,128)(2,1)S(1)}, bf16[18,32,128]{2,1,0:T(8,128)(2,1)S(1)}, f32[256,128]{1,0:T(8,128)}) custom-call(bf16[8,32,256]{2,1,0:T(8,128)(2,1)S(1)} %all_to_all.36.table, s32[8,16,128]{2,1,0:T(8,128)S(1)} %copy-done.1, ...), custom_call_target="tpu_custom_call" | custom-call | flops 8999999488 | bytes 27000000 | tf_op jit(solution)/shard_map/pallas_call | solution.py:407
  88.1 0.0 copy-start.10
  88.1 1.0 copy-done.10
  89.1 7.0 %all-to-all-start.4 = ((f32[32,8,128]{2,1,0:T(8,128)}), f32[32,8,128]{2,1,0:T(8,128)S(1)}, u32[]{:S(2)}, u32[]{:S(2)}) async-start(f32[32,8,128]{2,1,0:T(8,128)} %bitcast.26), calls=%async_computation.4 | async-start | bytes 262144 | tf_op jit(solution)/shard_map/all_to_all | solution.py:429
  96.1 3.5 %collective-permute-start.4 = (bf16[18,32,128]{2,1,0:T(8,128)(2,1)S(1)}, bf16[18,32,128]{2,1,0:T(8,128)(2,1)S(1)}, u32[]{:S(2)}, u32[]{:S(2)}) collective-permute-start(bf16[18,32,128]{2,1,0:T(8,128)(2,1)S(1)} %get-tuple-element.29), channel_id=1, source_target_pairs={{0,8},{8,16},{16,24},{1,9},{9,17},{17,25},{2,10},{10,18},{18,26},{... | collective-permute-start | bytes 442376 | tf_op jit(solution)/shard_map/ppermute | solution.py:425
  99.7 1.9 %collective-permute-start.5 = (bf16[18,32,128]{2,1,0:T(8,128)(2,1)S(1)}, bf16[18,32,128]{2,1,0:T(8,128)(2,1)S(1)}, u32[]{:S(2)}, u32[]{:S(2)}) collective-permute-start(bf16[18,32,128]{2,1,0:T(8,128)(2,1)S(1)} %get-tuple-element.30), channel_id=1, source_target_pairs={{8,0},{16,8},{24,16},{9,1},{17,9},{25,17},{10,2},{18,10},{26,18},{... | collective-permute-start | bytes 442376 | tf_op jit(solution)/shard_map/ppermute | solution.py:425
  101.6 2.3 %all-to-all-done.4 = f32[32,8,128]{2,1,0:T(8,128)S(1)} async-done(((f32[32,8,128]{2,1,0:T(8,128)}), f32[32,8,128]{2,1,0:T(8,128)S(1)}, u32[]{:S(2)}, u32[]{:S(2)}) %all-to-all-start.4) | async-done | bytes 131104 | tf_op jit(solution)/shard_map/all_to_all | solution.py:429
  103.9 0.7 broadcast_in_dim.28
  104.5 3.8 %all-to-all-start.5 = ((f32[32,8,128]{2,1,0:T(8,128)}), f32[32,8,128]{2,1,0:T(8,128)S(1)}, u32[]{:S(2)}, u32[]{:S(2)}) async-start(f32[32,8,128]{2,1,0:T(8,128)} %broadcast_in_dim.28), calls=%async_computation.5 | async-start | bytes 262144 | tf_op jit(solution)/shard_map/all_to_all | solution.py:429
  108.4 0.0 collective-permute-done.4.x_low
  108.4 0.0 collective-permute-done.5.x_high
  108.4 0.0 copy-start.11
  108.4 1.2 %copy-done.11 = bf16[8,32,2048]{2,1,0:T(8,128)(2,1)S(1)} copy-done((bf16[8,32,2048]{2,1,0:T(8,128)(2,1)S(1)}, bf16[8,32,2048]{2,1,0:T(8,128)(2,1)}, u32[]{:S(2)}) %copy-start.11) | copy-done | bytes 1048600
  109.6 7.9 %shard_map.127 = f32[8,32,16,128]{3,2,1,0:T(8,128)} custom-call(bf16[8,18,32,128]{3,2,1,0:T(8,128)(2,1)S(1)} %get-tuple-element.28.back_conv, bf16[18,32,128]{2,1,0:T(8,128)(2,1)S(1)} %collective-permute-done.4.x_low, bf16[18,32,128]{2,1,0:T(8,128)(2,1)S(1)} %collective-permute-done.5.x_high, bf16[8,32,2048]{2,1,0:T(8,128)(2,1)S(1)} %copy-done.11, ...), custom_call_target="tpu_custom_call" | custom-call | flops 10000000000 | bytes 30000000 | tf_op jit(solution)/shard_map/pallas_call | solution.py:407
  117.5 0.0 all-to-all-done.5
  117.6 0.1 reshape.94
  117.7 0.2 reshape.96
  118.0 0.1 copy.47
  118.1 0.9 reshape.97
  (41 shorter events, 0.3 us)
Async XLA Ops:
  0.6 11.2 %copy-start.16 = (bf16[32,864]{1,0:T(8,128)(2,1)S(1)}, bf16[32,864]{1,0:T(8,128)(2,1)}, u32[]{:S(2)}) copy-start(bf16[32,864]{1,0:T(8,128)(2,1)} %param.13) | copy-start | bytes 165892
  2.6 14.6 %copy-start = (bf16[8,32,16,128]{3,2,1,0:T(8,128)(2,1)S(1)}, bf16[8,32,16,128]{3,2,1,0:T(8,128)(2,1)}, u32[]{:S(2)}) copy-start(bf16[8,32,16,128]{3,2,1,0:T(8,128)(2,1)} %feat.1) | copy-start | bytes 3145732
  2.6 9.9 %collective-permute-start.1 = (bf16[32,16,128]{2,0,1:T(8,128)(2,1)S(1)}, bf16[32,16,128]{2,0,1:T(8,128)(2,1)S(1)}, u32[]{:S(2)}, u32[]{:S(2)}) collective-permute-start(bf16[32,16,128]{2,0,1:T(8,128)(2,1)S(1)} %get-tuple-element.53), channel_id=1, source_target_pairs={{8,0},{16,8},{24,16},{9,1},{17,9},{25,17},{10,2},{18,10},{26,18},{... | collective-permute-start | bytes 393224 | tf_op jit(solution)/shard_map/ppermute | solution.py:425
  4.7 7.8 %collective-permute-start = (bf16[32,16,128]{2,0,1:T(8,128)(2,1)S(1)}, bf16[32,16,128]{2,0,1:T(8,128)(2,1)S(1)}, u32[]{:S(2)}, u32[]{:S(2)}) collective-permute-start(bf16[32,16,128]{2,0,1:T(8,128)(2,1)S(1)} %get-tuple-element.54), channel_id=1, source_target_pairs={{0,8},{8,16},{16,24},{1,9},{9,17},{17,25},{2,10},{10,18},{18,26},{... | collective-permute-start | bytes 393224 | tf_op jit(solution)/shard_map/ppermute | solution.py:425
  12.5 7.3 %collective-permute-start.2 = (bf16[21,32,128]{2,1,0:T(8,128)(2,1)S(1)}, bf16[21,32,128]{2,1,0:T(8,128)(2,1)S(1)}, u32[]{:S(2)}, u32[]{:S(2)}) collective-permute-start(bf16[21,32,128]{2,1,0:T(8,128)(2,1)S(1)} %pad_maximum_fusion), channel_id=1, source_target_pairs={{0,1},{1,2},{2,3},{3,4},{4,5},{5,6},{6,7},{8,9},{9,10},{10,11},{11... | collective-permute-start | bytes 516104 | tf_op jit(solution)/shard_map/ppermute | solution.py:425
  15.8 8.1 %collective-permute-start.3 = (bf16[21,32,128]{2,1,0:T(8,128)(2,1)S(1)}, bf16[21,32,128]{2,1,0:T(8,128)(2,1)S(1)}, u32[]{:S(2)}, u32[]{:S(2)}) collective-permute-start(bf16[21,32,128]{2,1,0:T(8,128)(2,1)S(1)} %pad_maximum_fusion.1), channel_id=1, source_target_pairs={{1,0},{2,1},{3,2},{4,3},{5,4},{6,5},{7,6},{9,8},{10,9},{11,10},{12... | collective-permute-start | bytes 516104 | tf_op jit(solution)/shard_map/ppermute | solution.py:425
  17.2 6.7 %copy-start.1 = (s32[8,16,128]{2,1,0:T(8,128)S(1)}, s32[8,16,128]{2,1,0:T(8,128)}, u32[]{:S(2)}) copy-start(s32[8,16,128]{2,1,0:T(8,128)} %fragment.3) | copy-start | bytes 196612
  18.9 13.9 %copy-start.8 = (bf16[10,16,96,128]{3,2,1,0:T(8,128)(2,1)}, bf16[10,16,96,128]{3,2,1,0:T(8,128)(2,1)S(1)}, u32[]{:S(2)}) copy-start(bf16[10,16,96,128]{3,2,1,0:T(8,128)(2,1)S(1)} %shard_map.121.core) | copy-start | bytes 11796484
  32.8 13.4 %copy-start.12 = (bf16[10,2,96,128]{3,2,1,0:T(8,128)(2,1)}, bf16[10,2,96,128]{3,2,1,0:T(8,128)(2,1)S(1)}, u32[]{:S(2)}) copy-start(bf16[10,2,96,128]{3,2,1,0:T(8,128)(2,1)S(1)} %get-tuple-element.26.low) | copy-start | bytes 1474564
  32.8 13.4 %copy-start.14 = (bf16[10,2,96,128]{3,2,1,0:T(8,128)(2,1)}, bf16[10,2,96,128]{3,2,1,0:T(8,128)(2,1)S(1)}, u32[]{:S(2)}) copy-start(bf16[10,2,96,128]{3,2,1,0:T(8,128)(2,1)S(1)} %get-tuple-element.27.high) | copy-start | bytes 1474564
  45.5 11.0 %copy-start.2 = (bf16[256,256]{1,0:T(8,128)(2,1)S(1)}, bf16[256,256]{1,0:T(8,128)(2,1)}, u32[]{:S(2)}) copy-start(bf16[256,256]{1,0:T(8,128)(2,1)} %message.1) | copy-start | bytes 393220
  45.5 11.0 %copy-start.3 = (bf16[256,256]{1,0:T(8,128)(2,1)S(1)}, bf16[256,256]{1,0:T(8,128)(2,1)}, u32[]{:S(2)}) copy-start(bf16[256,256]{1,0:T(8,128)(2,1)} %update.1) | copy-start | bytes 393220
  45.5 11.0 %copy-start.4 = (bf16[256,256]{1,0:T(8,128)(2,1)S(1)}, bf16[256,256]{1,0:T(8,128)(2,1)}, u32[]{:S(2)}) copy-start(bf16[256,256]{1,0:T(8,128)(2,1)} %cotangent.1) | copy-start | bytes 393220
  45.5 11.0 %copy-start.5 = (bf16[32,256]{1,0:T(8,128)(2,1)S(1)}, bf16[32,256]{1,0:T(8,128)(2,1)}, u32[]{:S(2)}) copy-start(bf16[32,256]{1,0:T(8,128)(2,1)} %embed.1) | copy-start | bytes 49156
  45.5 11.0 %copy-start.6 = (s32[1024]{0:T(1024)S(1)}, s32[1024]{0:T(1024)}, u32[]{:S(2)}) copy-start(s32[1024]{0:T(1024)} %param.17) | copy-start | bytes 12292
  45.5 11.0 %copy-start.7 = (s32[1024]{0:T(1024)S(1)}, s32[1024]{0:T(1024)}, u32[]{:S(2)}) copy-start(s32[1024]{0:T(1024)} %param.18) | copy-start | bytes 12292
  46.2 10.2 %all-to-all-start.1 = ((bf16[8,32,256]{2,1,0:T(8,128)(2,1)}), bf16[8,32,256]{2,1,0:T(8,128)(2,1)S(1)}, u32[]{:S(2)}, u32[]{:S(2)}) async-start(bf16[8,32,256]{2,1,0:T(8,128)(2,1)} %get-tuple-element.19), calls=%async_computation.1 | async-start | bytes 262144 | tf_op jit(solution)/shard_map/all_to_all | solution.py:429
  67.9 8.9 %copy-start.9 = (bf16[10,16,96,128]{3,2,1,0:T(8,128)(2,1)S(1)}, bf16[10,16,96,128]{3,2,1,0:T(8,128)(2,1)}, u32[]{:S(2)}) copy-start(bf16[10,16,96,128]{3,2,1,0:T(8,128)(2,1)} %copy-done.8) | copy-start | bytes 11796484
  67.9 8.9 %copy-start.13 = (bf16[10,2,96,128]{3,2,1,0:T(8,128)(2,1)S(1)}, bf16[10,2,96,128]{3,2,1,0:T(8,128)(2,1)}, u32[]{:S(2)}) copy-start(bf16[10,2,96,128]{3,2,1,0:T(8,128)(2,1)} %copy-done.12) | copy-start | bytes 1474564
  67.9 8.9 %copy-start.15 = (bf16[10,2,96,128]{3,2,1,0:T(8,128)(2,1)S(1)}, bf16[10,2,96,128]{3,2,1,0:T(8,128)(2,1)}, u32[]{:S(2)}) copy-start(bf16[10,2,96,128]{3,2,1,0:T(8,128)(2,1)} %copy-done.14) | copy-start | bytes 1474564
  88.1 1.0 copy-start.10
  89.1 14.7 %all-to-all-start.4 = ((f32[32,8,128]{2,1,0:T(8,128)}), f32[32,8,128]{2,1,0:T(8,128)S(1)}, u32[]{:S(2)}, u32[]{:S(2)}) async-start(f32[32,8,128]{2,1,0:T(8,128)} %bitcast.26), calls=%async_computation.4 | async-start | bytes 262144 | tf_op jit(solution)/shard_map/all_to_all | solution.py:429
  96.1 12.3 %collective-permute-start.4 = (bf16[18,32,128]{2,1,0:T(8,128)(2,1)S(1)}, bf16[18,32,128]{2,1,0:T(8,128)(2,1)S(1)}, u32[]{:S(2)}, u32[]{:S(2)}) collective-permute-start(bf16[18,32,128]{2,1,0:T(8,128)(2,1)S(1)} %get-tuple-element.29), channel_id=1, source_target_pairs={{0,8},{8,16},{16,24},{1,9},{9,17},{17,25},{2,10},{10,18},{18,26},{... | collective-permute-start | bytes 442376 | tf_op jit(solution)/shard_map/ppermute | solution.py:425
  99.7 8.7 %collective-permute-start.5 = (bf16[18,32,128]{2,1,0:T(8,128)(2,1)S(1)}, bf16[18,32,128]{2,1,0:T(8,128)(2,1)S(1)}, u32[]{:S(2)}, u32[]{:S(2)}) collective-permute-start(bf16[18,32,128]{2,1,0:T(8,128)(2,1)S(1)} %get-tuple-element.30), channel_id=1, source_target_pairs={{8,0},{16,8},{24,16},{9,1},{17,9},{25,17},{10,2},{18,10},{26,18},{... | collective-permute-start | bytes 442376 | tf_op jit(solution)/shard_map/ppermute | solution.py:425
  104.5 13.0 %all-to-all-start.5 = ((f32[32,8,128]{2,1,0:T(8,128)}), f32[32,8,128]{2,1,0:T(8,128)S(1)}, u32[]{:S(2)}, u32[]{:S(2)}) async-start(f32[32,8,128]{2,1,0:T(8,128)} %broadcast_in_dim.28), calls=%async_computation.5 | async-start | bytes 262144 | tf_op jit(solution)/shard_map/all_to_all | solution.py:429
  108.4 1.2 %copy-start.11 = (bf16[8,32,2048]{2,1,0:T(8,128)(2,1)S(1)}, bf16[8,32,2048]{2,1,0:T(8,128)(2,1)}, u32[]{:S(2)}) copy-start(bf16[8,32,2048]{2,1,0:T(8,128)(2,1)} %copy-done.10) | copy-start | bytes 3145732
